TPU v7x, 32 devices: a whole 2x2x4 slice. The times are simulated.
32 devices in a mesh: row: 4 (over y, x), col: 8 (over z, core).
Axes of the slice: x: 2, y: 2, z: 4, core: 2. Of those that a mesh axis runs over, the one named last changes fastest.
Arguments:
- eigenvectors: float32 [1536, 61440], P('col', 'row'), may hold values from -6 to 6
- householder: float32 [2, 128, 61440], P(None, 'col', 'row'), may hold values from -0.5 to 0.5
- factors: float32 [2, 128, 128], replicated, may hold values from -0.0234375 to 0.0234375
Outputs:
- transformed: float32 [1536, 61440], P('col', 'row')
All inputs are finite; a program needn't handle non-finite values.
Results may differ from a plain program's by a relative error of at most 0.0001.
Values sent between devices are 32-bit elements; how exact they have to be, the bound alone decides.
No kernel may reach another device: no remote copies, remote signals or barrier semaphores. Data moves between devices by JAX's collectives and lax.ppermute only.
A program may use at most 128 MiB of HBM per device.

v0:
```python
import jax
import jax.numpy as jnp
from jax import lax
from jax.sharding import PartitionSpec as P


def matmul(left, right):
    return jnp.dot(left, right, precision=lax.Precision.HIGHEST, preferred_element_type=jnp.float32)


def project(vectors, slab):
    return lax.dot_general(
        vectors,
        slab,
        (((1,), (1,)), ((), ())),
        precision=lax.Precision.HIGHEST,
        preferred_element_type=jnp.float32,
    )


def update(coeffs, vectors):
    return lax.dot_general(
        coeffs,
        vectors,
        (((0,), (0,)), ((), ())),
        precision=lax.Precision.HIGHEST,
        preferred_element_type=jnp.float32,
    )


def gather_block(piece):
    return lax.all_gather(piece, "col", axis=0, tiled=True)


def reduce_apply(partial_value, solver):
    summed = lax.psum(partial_value, "row")
    return solver(summed)


def per_device(eigenvectors, householder, factors):
    slab = eigenvectors
    count = householder.shape[0]
    upper = jnp.triu(factors)
    for block in range(count):
        vectors = gather_block(householder[block])
        partial_value = project(vectors, slab)
        factor = upper[block]
        coeffs = reduce_apply(partial_value, lambda summed: matmul(factor, summed))
        slab = slab - update(coeffs, vectors)
    return slab


def solution(mesh):
    in_specs = (P("col", "row"), P(None, "col", "row"), P())
    out_specs = P("col", "row")
    return jax.shard_map(
        per_device, mesh=mesh, in_specs=in_specs, out_specs=out_specs, check_vma=False
    )
```

profile of v0, /device:TPU:0, one launch (start us, length us, event | category | flops | bytes accessed | tf_op | source)
XLA Modules:
  0.0 305.3 jit_solution(16689842980097219363)
XLA Ops:
  6.5 0.0 all-gather.5.cloned.1.call-start
  6.5 2.9 fusion.11
  9.4 0.0 all-gather.5.cloned.1.call-update
  9.5 0.0 copy-start
  9.5 0.0 all-reduce.3.cloned.1.call-start
  9.5 80.5 %all-gather.5.cloned.1.call-done = f32[1,128,15360]{2,1,0:T(8,128)} async-done(((f32[1,16,15360]{2,1,0:T(8,128)}), f32[1,128,15360]{2,1,0:T(8,128)}) %all-gather.5.cloned.1.call-update) | async-done | bytes 7864336 | tf_op jit(solution)/shard_map/all_gather | solution.py:32
  90.0 16.1 %fusion.4 = f32[128,192]{1,0:T(8,128)} fusion(f32[192,15360]{1,0:T(8,128)} %param.3, f32[1,128,15360]{2,1,0:T(8,128)} %all-gather.5.cloned.1.call-done), kind=kOutput, calls=%fused_computation.6 | convolution fusion | flops 4529848320 | bytes 19759104 | tf_op jit(solution)/shard_map/dot_general | solution.py:12
  106.2 0.0 all-reduce.3.cloned.1.call-update
  106.2 0.0 all-gather.7.cloned.1.call-start
  106.2 0.7 all-gather.7.cloned.1.call-update
  106.9 0.2 all-reduce.5.cloned.1.call-start
  107.2 0.1 iota_compare_fusion
  107.3 0.0 copy-done
  107.3 39.6 %all-reduce.3.cloned.1.call-done = f32[128,192]{1,0:T(8,128)} async-done(((f32[128,192]{1,0:T(8,128)}), f32[128,192]{1,0:T(8,128)}) %all-reduce.3.cloned.1.call-update) | async-done | bytes 98320 | tf_op jit(solution)/shard_map/psum | solution.py:36
  146.9 1.2 fusion.10
  148.1 16.3 %convolution_subtract_fusion.1 = f32[192,15360]{1,0:T(8,128)} fusion(f32[192,15360]{1,0:T(8,128)} %param.3, f32[128,192]{1,0:T(8,128)S(1)} %fusion.10, f32[1,128,15360]{2,1,0:T(8,128)} %all-gather.5.cloned.1.call-done), kind=kOutput, calls=%fused_computation.1 | convolution fusion | flops 4532797440 | bytes 31555584 | tf_op jit(solution)/shard_map/dot_general | solution.py:22
  164.4 62.1 %all-gather.7.cloned.1.call-done = f32[1,128,15360]{2,1,0:T(8,128)} async-done(((f32[1,16,15360]{2,1,0:T(8,128)}), f32[1,128,15360]{2,1,0:T(8,128)}) %all-gather.7.cloned.1.call-update) | async-done | bytes 7864336 | tf_op jit(solution)/shard_map/all_gather | solution.py:32
  226.4 14.0 %fusion.6 = f32[128,192]{0,1:T(8,128)} fusion(f32[192,15360]{1,0:T(8,128)} %convolution_subtract_fusion.1, f32[1,128,15360]{2,1,0:T(8,128)} %all-gather.7.cloned.1.call-done), kind=kOutput, calls=%fused_computation.8 | convolution fusion | flops 4529848320 | bytes 19759104 | tf_op jit(solution)/shard_map/dot_general | solution.py:12
  240.4 0.0 all-reduce.5.cloned.1.call-update
  240.4 40.6 %all-reduce.5.cloned.1.call-done = f32[128,192]{0,1:T(8,128)} async-done(((f32[128,192]{0,1:T(8,128)}), f32[128,192]{0,1:T(8,128)}) %all-reduce.5.cloned.1.call-update) | async-done | bytes 98320 | tf_op jit(solution)/shard_map/psum | solution.py:36
  281.0 1.2 fusion.9
  282.2 16.5 %convolution_subtract_fusion = f32[192,15360]{1,0:T(8,128)} fusion(f32[192,15360]{1,0:T(8,128)} %convolution_subtract_fusion.1, f32[128,192]{1,0:T(8,128)S(1)} %fusion.9, f32[1,128,15360]{2,1,0:T(8,128)} %all-gather.7.cloned.1.call-done), kind=kOutput, calls=%fused_computation | convolution fusion | flops 4532797440 | bytes 31555584 | tf_op jit(solution)/shard_map/dot_general | solution.py:22
  (2 shorter events, 0.0 us)
Async XLA Ops:
  6.5 83.5 %all-gather.5.cloned.1.call-start = ((), (), s32[]{:S(2)}) async-start(), calls=%async_computation.2 | async-start | bytes 8847360 | tf_op jit(solution)/shard_map/all_gather | solution.py:32
  9.5 97.8 %copy-start = (f32[2,128,128]{2,1,0:T(8,128)S(1)}, f32[2,128,128]{2,1,0:T(8,128)}, u32[]{:S(2)}) copy-start(f32[2,128,128]{2,1,0:T(8,128)} %param.5) | copy-start | bytes 393220
  9.5 137.4 %all-reduce.3.cloned.1.call-start = ((), (), s32[]{:S(2)}) async-start(), calls=%async_computation | async-start | bytes 262144 | tf_op jit(solution)/shard_map/psum | solution.py:36
  106.2 120.2 %all-gather.7.cloned.1.call-start = ((), (), s32[]{:S(2)}) async-start(), calls=%async_computation.3 | async-start | bytes 8847360 | tf_op jit(solution)/shard_map/all_gather | solution.py:32
  106.9 174.1 %all-reduce.5.cloned.1.call-start = ((), (), s32[]{:S(2)}) async-start(), calls=%async_computation.1 | async-start | bytes 196608 | tf_op jit(solution)/shard_map/psum | solution.py:36
Sparse Core Ops, SparseCore 0:
  9.6 80.4 all-gather.4
  106.3 40.5 all-reduce.2
  148.7 77.7 all-gather.6
  240.5 40.4 all-reduce.4
where the time goes:
time: 305 us
  waiting for transfers between devices  224 us (73%)
  matrix products  65.3 us (21%)
  between operations  13.2 us (4%)
    all_gather x2, waiting for transfers between devices, gather_block(): return lax.all_gather(piece, 'col', axis=0, tiled=True)  143 us
    psum x2, waiting for transfers between devices, reduce_apply(): summed = lax.psum(partial_value, 'row')  80.2 us
    dot_general x2, matrix products, update(): lax.dot_general(coeffs, vectors, (((0,), (0,)), ((), ())), precision=lax....  32.8 us
    dot_general x2, matrix products, project(): lax.dot_general(vectors, slab, (((1,), (1,)), ((), ())), precision=lax.Pr...  30.1 us
  transfers between devices with their start and end apart: 4, of which 4 were waited for; matrix products, arithmetic and copies ran while one was open for 6% of the time, Pallas kernels for 0%

commit v1 on v0

v1 whole, which is shorter than its diff:
```python
import functools

import jax
import jax.numpy as jnp
from jax import lax
from jax.experimental import pallas as pl
from jax.experimental.pallas import tpu as pltpu
from jax.sharding import PartitionSpec as P

F32 = jnp.float32
BF16 = jnp.bfloat16
NT = (((1,), (1,)), ((), ()))
NN = (((1,), (0,)), ((), ()))
TILE = 1280
PARTS = 4
VMEM = 48 * 1024 * 1024


def split(x):
    high = x.astype(BF16)
    return high, (x - high.astype(F32)).astype(BF16)


def dot3(left, right, dims):
    (lh, ll), (rh, rl) = left, right
    dot = functools.partial(lax.dot_general, dimension_numbers=dims, preferred_element_type=F32)
    return dot(lh, rh) + (dot(ll, rh) + dot(lh, rl))


def exact(left, right, dims=NN):
    return lax.dot_general(left, right, dims, precision=lax.Precision.HIGHEST, preferred_element_type=F32)


def rows_of(refs, pick):
    return jnp.concatenate([refs[i][...] if b is None else refs[i][b] for i, b in pick], axis=0)


def project_kernel(pick, slab_ref, *refs):
    *pieces, out_ref = refs

    @pl.when(pl.program_id(0) == 0)
    def _():
        out_ref[...] = jnp.zeros_like(out_ref)

    out_ref[...] += dot3(split(rows_of(pieces, pick)), split(slab_ref[...]), NT)


def piece_spec(piece, tile, index):
    if piece.ndim == 2:
        return pl.BlockSpec((piece.shape[0], tile), lambda g: (0, index(g)))
    return pl.BlockSpec((2, piece.shape[1], tile), lambda g: (0, 0, index(g)))


def project(slab, pieces, pick, first=0):
    width = pieces[0].shape[-1]
    height = 16 * len(pick)
    count = width // TILE
    return pl.pallas_call(
        functools.partial(project_kernel, pick),
        out_shape=jax.ShapeDtypeStruct((height, slab.shape[0]), F32),
        grid=(count,),
        in_specs=[pl.BlockSpec((slab.shape[0], TILE), lambda g: (0, first + g))]
        + [piece_spec(p, TILE, lambda g: g) for p in pieces],
        out_specs=pl.BlockSpec((height, slab.shape[0]), lambda g: (0, 0)),
        compiler_params=pltpu.CompilerParams(vmem_limit_bytes=VMEM),
        cost_estimate=pl.CostEstimate(
            flops=6 * height * slab.shape[0] * width, bytes_accessed=4 * (height + slab.shape[0]) * width, transcendentals=0
        ),
        name="project",
    )(slab, *pieces)


def cross_kernel(low, high, *refs):
    *pieces, out_ref = refs

    @pl.when(pl.program_id(0) == 0)
    def _():
        out_ref[...] = jnp.zeros_like(out_ref)

    out_ref[...] += dot3(split(rows_of(pieces, high)), split(rows_of(pieces, low)), NT)


def cross(pieces, low, high):
    width = pieces[0].shape[-1]
    n = 16 * len(low)
    return pl.pallas_call(
        functools.partial(cross_kernel, low, high),
        out_shape=jax.ShapeDtypeStruct((n, n), F32),
        grid=(width // TILE,),
        in_specs=[piece_spec(p, TILE, lambda g: g) for p in pieces],
        out_specs=pl.BlockSpec((n, n), lambda g: (0, 0)),
        compiler_params=pltpu.CompilerParams(vmem_limit_bytes=VMEM),
        cost_estimate=pl.CostEstimate(flops=6 * n * n * width, bytes_accessed=8 * n * width, transcendentals=0),
        name="cross",
    )(*pieces)


def update_kernel(early, pick, per, slab_ref, upper_ref, cross_ref, known_ref, a_ref, b_ref, c_ref, d_ref, *refs):
    *pieces, out_ref, high_ref, low_ref = refs
    step = pl.program_id(0)

    @pl.when(step == 0)
    def _():
        last = (a_ref[...] + b_ref[...]) + (c_ref[...] + d_ref[...])
        half = last.shape[0] // 2
        one = jnp.concatenate([known_ref[0], last[:half]], axis=0)
        two = jnp.concatenate([known_ref[1], last[half:]], axis=0)
        first = exact(upper_ref[0], one)
        second = exact(upper_ref[1], two - exact(cross_ref[...], first))
        high, low = split(jnp.concatenate([first, second], axis=0).T)
        high_ref[...] = high
        low_ref[...] = low

    for part in range(len(pick)):

        @pl.when(step // per == part)
        def _():
            vectors = split(rows_of(pieces, pick[part]))
            out_ref[...] = slab_ref[...] - dot3((high_ref[...], low_ref[...]), vectors, NN)


def update(slab, upper, gram, known, lasts, pieces, parts, pick, pick_part):
    nev, width = slab.shape
    per = parts[0][0].shape[-1] // TILE
    operands = list(pieces)
    specs = [piece_spec(p, TILE, lambda g: g) for p in pieces]
    for i, part in enumerate(parts):
        operands += part
        specs += [piece_spec(p, TILE, lambda g, i=i: jnp.clip(g - i * per, 0, per - 1)) for p in part]
    whole = lambda x: pl.BlockSpec(x.shape, lambda g: (0,) * x.ndim)
    small = [upper, gram, known, *lasts]
    picks = [
        tuple(
            pick[b] + tuple((len(pieces) + i * len(parts[0]) + at, bb) for at, bb in pick_part[b]) for b in (0, 1)
        )
        for i in range(len(parts))
    ]
    n = sum(16 * len(r) for r in picks[0])
    return pl.pallas_call(
        functools.partial(update_kernel, None, [a + b for a, b in picks], per),
        out_shape=jax.ShapeDtypeStruct(slab.shape, F32),
        grid=(width // TILE,),
        in_specs=[pl.BlockSpec((nev, TILE), lambda g: (0, g))] + [whole(x) for x in small] + specs,
        out_specs=pl.BlockSpec((nev, TILE), lambda g: (0, g)),
        scratch_shapes=[pltpu.VMEM((nev, n), BF16), pltpu.VMEM((nev, n), BF16)],
        compiler_params=pltpu.CompilerParams(vmem_limit_bytes=VMEM),
        cost_estimate=pl.CostEstimate(
            flops=6 * n * nev * width, bytes_accessed=4 * (2 * nev + n) * width, transcendentals=0
        ),
        name="update",
    )(slab, *small, *operands)


def others(x):
    return [lax.ppermute(x, "row", [(i, i ^ k) for i in range(4)]) for k in (1, 2, 3)]


def sum_row(x):
    a, b, c = others(x)
    return (x + a) + (b + c)


def cores(pairs):
    return [(2 * a + c, 2 * b + c) for a, b in pairs for c in (0, 1)]


PAIR = cores([(0, 1), (1, 0), (2, 3), (3, 2)])
MIDDLE = cores([(1, 2), (2, 1)])
OUTWARD = cores([(1, 0), (2, 3)])
SIBLING = [(i, i ^ 1) for i in range(8)]


def along(x, pairs):
    return lax.ppermute(x, "col", pairs)


def line_of_four(slab, householder, factors):
    col = lax.axis_index("col")
    count, mine, width = householder.shape
    own = [householder[0], householder[1]]
    beside = [along(x, PAIR) for x in own]
    inner = [along(x, MIDDLE) for x in own]
    outer = [along(x, OUTWARD) for x in inner]
    across = [along(x, MIDDLE) for x in beside]
    third = [a + b for a, b in zip(outer, across)]
    step = width // PARTS
    cut = lambda pair, q: jnp.stack([x[:, q * step : (q + 1) * step] for x in pair])
    parts = []
    for q in range(PARTS):
        part = along(cut(across, q), OUTWARD) + cut(inner, q)
        parts.append([part, along(part, SIBLING)])

    other = along(householder, SIBLING)
    beside2 = [along(x, SIBLING) for x in beside]
    third2 = [along(x, SIBLING) for x in third]
    inner2 = [along(x, SIBLING) for x in inner]

    nev = slab.shape[0]
    four = ((0, 0), (1, 0), (0, 1), (1, 1))
    split4 = ((0, None), (2, None), (1, None), (3, None))
    p0 = project(slab, [householder, other], four).reshape(2, 2 * mine, nev)
    p1 = project(slab, beside + beside2, split4).reshape(2, 2 * mine, nev)
    p2 = project(slab, third + third2, split4).reshape(2, 2 * mine, nev)
    known = sum_row(jnp.concatenate([p0, p1, p2], axis=1))
    last = sum(project(slab, part, four, q * (step // TILE)) for q, part in enumerate(parts))
    lasts = [last, *others(last)]

    pieces = [householder, other, *beside, *beside2, *third, *third2]
    pick = [((0, b), (1, b), (2 + b, None), (4 + b, None), (6 + b, None), (8 + b, None)) for b in (0, 1)]
    full = [pick[b] + ((10 + b, None), (12 + b, None)) for b in (0, 1)]
    gram = sum_row(cross(pieces + inner + inner2, full[0], full[1]))
    given = along(gram, OUTWARD).reshape(2, 2, 2, mine, 2, 2, 2, mine)
    given = given[:, ::-1, :, :, :, ::-1].reshape(gram.shape)
    middle = jnp.logical_and(col >= 2, col < 6)
    gram = jnp.where(middle, gram, given)

    order = jnp.bitwise_xor(col, jnp.arange(8))
    upper = jnp.triu(factors).reshape(2, 8, mine, 8, mine)
    upper = jnp.take(jnp.take(upper, order, axis=1), order, axis=3).reshape(factors.shape)

    pick_part = [((0, b), (1, b)) for b in (0, 1)]
    return update(slab, upper, gram, known, lasts, pieces, parts, pick, pick_part)


def matmul(left, right):
    return jnp.dot(left, right, precision=lax.Precision.HIGHEST, preferred_element_type=F32)


def any_mesh(slab, householder, factors):
    upper = jnp.triu(factors)
    for block in range(householder.shape[0]):
        vectors = lax.all_gather(householder[block], "col", axis=0, tiled=True)
        projection = lax.psum(exact(vectors, slab, NT), "row")
        coeffs = matmul(upper[block], projection)
        slab = slab - exact(coeffs, vectors, (((0,), (0,)), ((), ())))
    return slab


def solution(mesh):
    small = mesh.shape["col"] == 8 and mesh.shape["row"] == 4
    return jax.shard_map(
        line_of_four if small else any_mesh,
        mesh=mesh,
        in_specs=(P("col", "row"), P(None, "col", "row"), P()),
        out_specs=P("col", "row"),
        check_vma=False,
    )
```

time: 305 us -> 260 us (0.85)
  waiting for transfers between devices: 224 us -> 102 us
  Pallas kernels: 0 us -> 81 us
  matrix products: 65.3 us -> 0 us
  starting transfers between devices: 0.3 us -> 32.8 us
  local copies, waits for them, and re-layouts: 2.9 us -> 34 us
  between operations: 13.2 us -> 0.71 us
  other arithmetic: 0.1 us -> 7.12 us
    all_gather x2 -> x0, waiting for transfers between devices: 143 us -> none  [gather_block(): return lax.all_gather(piece, 'col', axis=0, tiled=True)]
    ppermute x0 -> x33, waiting for transfers between devices: none -> 102 us  [the longest x24 101 us: along(): return lax.ppermute(x, 'col', pairs)]
    pallas_call x0 -> x9, Pallas kernels: none -> 81 us  [the longest x7 51.1 us: project(): pl.pallas_call(functools.partial(project_kernel, pick), out_shape=jax.Sha...]
    psum x2 -> x0, waiting for transfers between devices: 80.2 us -> none  [reduce_apply(): summed = lax.psum(partial_value, 'row')]
    dot_general x6 -> x0, matrix products: 65.3 us -> none  [the longest x2 32.8 us: update(): lax.dot_general(coeffs, vectors, (((0,), (0,)), ((), ())), precision=lax....]
    ppermute x0 -> x33, starting transfers between devices: none -> 32.8 us  [the longest x24 22.2 us: along(): return lax.ppermute(x, 'col', pairs)]
    gather x0 -> x4, local copies, waits for them, and re-layouts: none -> 10.6 us  [the longest x3 7.8 us: line_of_four(): jnp.take(jnp.take(upper, order, axis=1), order, axis=3)]
    unnamed x2 -> x64, local copies, waits for them, and re-layouts: 0.01 us -> 7.28 us
  transfers between devices with their start and end apart: 4 -> 33, of which waited for: 4 -> 11; matrix products, arithmetic and copies ran while one was open for 6% -> 12% of each run, Pallas kernels for 0% -> 24%
where the time goes in v1:
time: 260 us; the launch traced here: 258 us
  waiting for transfers between devices  102 us (39%)
  Pallas kernels  81 us (31%)
  local copies, waits for them, and re-layouts  34 us (13%)
  starting transfers between devices  32.8 us (13%)
  other arithmetic  7.12 us (3%)
    ppermute x24, waiting for transfers between devices, along(): return lax.ppermute(x, 'col', pairs)  101 us
    pallas_call x7, Pallas kernels, project(): pl.pallas_call(functools.partial(project_kernel, pick), out_shape=jax.Sha...  51.1 us
    ppermute x24, starting transfers between devices, along(): return lax.ppermute(x, 'col', pairs)  22.2 us
    pallas_call x1, Pallas kernels, update(): pl.pallas_call(functools.partial(update_kernel, None, [a + b for a, b in...  19.1 us
    pallas_call x1, Pallas kernels, cross(): pl.pallas_call(functools.partial(cross_kernel, low, high), out_shape=jax....  10.8 us
    ppermute x9, starting transfers between devices, others(): lax.ppermute(x, 'row', [(i, i ^ k) for i in range(4)])  10.6 us
    gather x3, local copies, waits for them, and re-layouts, line_of_four(): jnp.take(jnp.take(upper, order, axis=1), order, axis=3)  7.8 us
    unnamed x64, local copies, waits for them, and re-layouts  7.28 us
  transfers between devices with their start and end apart: 33, of which 11 were waited for; matrix products, arithmetic and copies ran while one was open for 12% of the time, Pallas kernels for 24%

profile of v1, /device:TPU:0, one launch (start us, length us, event | category | flops | bytes accessed | tf_op | source)
XLA Modules:
  0.0 258.0 jit_solution(9117757315966150151)
XLA Ops:
  0.0 2.7 %slice_bitcast_fusion = (f32[16,15360]{1,0:T(8,128)S(1)}, f32[16,15360]{1,0:T(8,128)}) fusion(f32[2,16,15360]{2,1,0:T(8,128)} %refs_0_.5), kind=kLoop, calls=%fused_computation.3 | loop fusion | bytes 3932160 | tf_op jit(solution)/shard_map/squeeze | solution.py:180
  2.7 1.6 collective-permute-start.8
  4.3 5.0 %collective-permute-start.2 = (f32[16,15360]{1,0:T(8,128)S(1)}, f32[16,15360]{1,0:T(8,128)}, u32[]{:S(2)}, u32[]{:S(2)}) collective-permute-start(f32[16,15360]{1,0:T(8,128)S(1)} %get-tuple-element.5), channel_id=1, source_target_pairs={{0,2},{1,3},{2,0},{3,1},{4,6},{5,7},{6,4},{7,5},{8,10},{9,11},{10,... | collective-permute-start | bytes 2949128 | tf_op jit(solution)/shard_map/ppermute | solution.py:174
  9.3 1.6 collective-permute-start.5
  10.9 1.5 collective-permute-start.1
  12.6 1.3 reshape.42
  13.9 2.8 %gather_fusion = f32[8,2,16,8,16]{4,3,2,1,0:T(8,128)} fusion(f32[2,8,16,8,16]{4,3,2,1,0:T(8,128)} %reshape.42, s32[1024]{0:T(1024)S(1)} %pad_clamp_fusion), kind=kCustom, calls=%fused_computation | custom fusion | bytes 262176 | tf_op jit(solution)/shard_map/jit(_take)/gather | solution.py:219
  16.7 2.4 select_bitcast_fusion
  19.3 2.4 copy.5
  21.7 2.8 %gather_fusion.1 = f32[8,2,8,16,16]{4,3,2,1,0:T(8,128)} fusion(f32[2,8,16,8,16]{4,2,3,1,0:T(8,128)} %copy.5, s32[1024]{0:T(1024)S(1)} %pad_clamp_fusion), kind=kCustom, calls=%fused_computation.1 | custom fusion | bytes 262176 | tf_op jit(solution)/shard_map/jit(_take)/gather | solution.py:219
  24.5 2.8 %copy.6 = f32[2,8,16,8,16]{4,3,2,1,0:T(8,128)} copy(f32[2,8,16,8,16]{4,2,1,0,3:T(8,128)} %bitcast.52) | data formatting | bytes 262144 | tf_op jit(solution)/shard_map/jit(_take)/gather | solution.py:219
  27.3 2.2 gather.12
  29.5 2.6 collective-permute-done.2.refs_3_.refs_1_
  32.0 0.7 collective-permute-start.10
  32.8 1.4 slice_bitcast_fusion.10
  34.1 1.3 collective-permute-start.9
  35.5 17.6 %collective-permute-done.1.refs_2_.refs_0_ = f32[16,15360]{1,0:T(8,128)} collective-permute-done((f32[16,15360]{1,0:T(8,128)}, f32[16,15360]{1,0:T(8,128)}, u32[]{:S(2)}, u32[]{:S(2)}) %collective-permute-start.1) | collective-permute-done | bytes 983072 | tf_op jit(solution)/shard_map/ppermute | solution.py:174
  53.1 0.7 collective-permute-start.7
  53.8 1.4 slice_bitcast_fusion.11
  55.2 1.3 collective-permute-start.6
  56.7 1.3 collective-permute-start.22
  58.1 14.8 %collective-permute-done.9 = f32[16,15360]{1,0:T(8,128)S(1)} collective-permute-done((f32[16,15360]{1,0:T(8,128)}, f32[16,15360]{1,0:T(8,128)S(1)}, u32[]{:S(2)}, u32[]{:S(2)}) %collective-permute-start.9) | collective-permute-done | bytes 983072 | tf_op jit(solution)/shard_map/ppermute | solution.py:174
  73.0 22.6 %collective-permute-done.6 = f32[16,15360]{1,0:T(8,128)S(1)} collective-permute-done((f32[16,15360]{1,0:T(8,128)}, f32[16,15360]{1,0:T(8,128)S(1)}, u32[]{:S(2)}, u32[]{:S(2)}) %collective-permute-start.6) | collective-permute-done | bytes 983072 | tf_op jit(solution)/shard_map/ppermute | solution.py:174
  95.6 1.3 collective-permute-start.26
  97.1 10.8 %collective-permute-done.22 = f32[2,16,3840]{2,1,0:T(8,128)S(1)} collective-permute-done((f32[2,16,3840]{2,1,0:T(8,128)S(1)}, f32[2,16,3840]{2,1,0:T(8,128)S(1)}, u32[]{:S(2)}, u32[]{:S(2)}) %collective-permute-start.22) | collective-permute-done | bytes 491552 | tf_op jit(solution)/shard_map/ppermute | solution.py:174
  107.8 1.3 collective-permute-start.28
  109.2 9.2 %collective-permute-done.26 = f32[2,16,3840]{2,1,0:T(8,128)S(1)} collective-permute-done((f32[2,16,3840]{2,1,0:T(8,128)S(1)}, f32[2,16,3840]{2,1,0:T(8,128)S(1)}, u32[]{:S(2)}, u32[]{:S(2)}) %collective-permute-start.26) | collective-permute-done | bytes 491552 | tf_op jit(solution)/shard_map/ppermute | solution.py:174
  118.4 1.3 collective-permute-start.24
  119.9 9.1 %collective-permute-done.28 = f32[2,16,3840]{2,1,0:T(8,128)S(1)} collective-permute-done((f32[2,16,3840]{2,1,0:T(8,128)S(1)}, f32[2,16,3840]{2,1,0:T(8,128)S(1)}, u32[]{:S(2)}, u32[]{:S(2)}) %collective-permute-start.28) | collective-permute-done | bytes 491552 | tf_op jit(solution)/shard_map/ppermute | solution.py:174
  129.0 0.6 collective-permute-start.14
  129.7 8.1 %collective-permute-done.24 = f32[2,16,3840]{2,1,0:T(8,128)S(1)} collective-permute-done((f32[2,16,3840]{2,1,0:T(8,128)S(1)}, f32[2,16,3840]{2,1,0:T(8,128)S(1)}, u32[]{:S(2)}, u32[]{:S(2)}) %collective-permute-start.24) | collective-permute-done | bytes 491552 | tf_op jit(solution)/shard_map/ppermute | solution.py:174
  138.4 4.0 %collective-permute-done.29.refs_1_.refs_17_ = f32[2,16,3840]{2,1,0:T(8,128)S(1)} collective-permute-done((f32[2,16,3840]{2,1,0:T(8,128)S(1)}, f32[2,16,3840]{2,1,0:T(8,128)S(1)}, u32[]{:S(2)}, u32[]{:S(2)}) %collective-permute-start.29) | collective-permute-done | bytes 491552 | tf_op jit(solution)/shard_map/ppermute | solution.py:174
  142.6 0.7 broadcast_select_fusion.upper_ref
  143.3 12.1 %project.7 = f32[64,192]{1,0:T(8,128)S(1)} custom-call(f32[192,15360]{1,0:T(8,128)} %slab_ref.15, f32[2,16,15360]{2,1,0:T(8,128)S(1)} %copy-done, f32[2,16,15360]{2,1,0:T(8,128)} %collective-permute-done.refs_1_), custom_call_target="tpu_custom_call" | custom-call | flops 1132462080 | bytes 15728640 | tf_op jit(solution)/shard_map/project/pallas_call | solution.py:58
  155.3 12.2 %project.8 = f32[64,192]{1,0:T(8,128)S(1)} custom-call(f32[192,15360]{1,0:T(8,128)} %slab_ref.15, f32[16,15360]{1,0:T(8,128)} %collective-permute-done.1.refs_2_.refs_0_, f32[16,15360]{1,0:T(8,128)} %collective-permute-done.2.refs_3_.refs_1_, f32[16,15360]{1,0:T(8,128)S(1)} %collective-permute-done.3.refs_4_.refs_2_, ...), custom_call_target="tpu_custom_call" | custom-call | flops 1132462080 | bytes 15728640 | tf_op jit(solution)/shard_map/project/pallas_call | solution.py:58
  167.6 3.7 %project.10 = f32[64,192]{1,0:T(8,128)S(1)} custom-call(f32[192,15360]{1,0:T(8,128)} %slab_ref.15, f32[2,16,3840]{2,1,0:T(8,128)S(1)} %maximum_add_fusion.refs_0_.refs_10_, f32[2,16,3840]{2,1,0:T(8,128)S(1)} %collective-permute-done.23.refs_1_.refs_11_), custom_call_target="tpu_custom_call" | custom-call | flops 283115520 | bytes 3932160 | tf_op jit(solution)/shard_map/project/pallas_call | solution.py:58
  171.3 3.7 %project.12 = f32[64,192]{1,0:T(8,128)S(1)} custom-call(f32[192,15360]{1,0:T(8,128)} %slab_ref.15, f32[2,16,3840]{2,1,0:T(8,128)S(1)} %maximum_add_fusion.2.refs_0_.refs_14_, f32[2,16,3840]{2,1,0:T(8,128)S(1)} %collective-permute-done.27.refs_1_.refs_15_), custom_call_target="tpu_custom_call" | custom-call | flops 283115520 | bytes 3932160 | tf_op jit(solution)/shard_map/project/pallas_call | solution.py:58
  175.0 3.7 %project.13 = f32[64,192]{1,0:T(8,128)S(1)} custom-call(f32[192,15360]{1,0:T(8,128)} %slab_ref.15, f32[2,16,3840]{2,1,0:T(8,128)S(1)} %maximum_add_fusion.3.refs_0_.refs_16_, f32[2,16,3840]{2,1,0:T(8,128)S(1)} %collective-permute-done.29.refs_1_.refs_17_), custom_call_target="tpu_custom_call" | custom-call | flops 283115520 | bytes 3932160 | tf_op jit(solution)/shard_map/project/pallas_call | solution.py:58
  178.7 3.8 %project.11 = f32[64,192]{1,0:T(8,128)S(1)} custom-call(f32[192,15360]{1,0:T(8,128)} %slab_ref.15, f32[2,16,3840]{2,1,0:T(8,128)S(1)} %maximum_add_fusion.1.refs_0_.refs_12_, f32[2,16,3840]{2,1,0:T(8,128)S(1)} %collective-permute-done.25.refs_1_.refs_13_), custom_call_target="tpu_custom_call" | custom-call | flops 283115520 | bytes 3932160 | tf_op jit(solution)/shard_map/project/pallas_call | solution.py:58
  182.6 0.6 add_add_fusion.1.a_ref
  183.2 2.4 collective-permute-start.32
  187.5 1.0 copy-done.7
  188.5 10.8 %cross.1 = f32[128,128]{1,0:T(8,128)S(1)} custom-call(f32[2,16,15360]{2,1,0:T(8,128)} %refs_0_.5, f32[2,16,15360]{2,1,0:T(8,128)} %collective-permute-done.refs_1_, f32[16,15360]{1,0:T(8,128)} %collective-permute-done.1.refs_2_.refs_0_, f32[16,15360]{1,0:T(8,128)} %collective-permute-done.2.refs_3_.refs_1_, ...), custom_call_target="tpu_custom_call" | custom-call | flops 1509949440 | bytes 15728640 | tf_op jit(solution)/shard_map/cross/pallas_call | solution.py:86
  199.2 1.6 collective-permute-start.17
  201.3 1.5 collective-permute-start.15
  202.8 1.2 copy-done.6
  204.0 1.2 copy-done.8
  205.2 12.0 %project.9 = f32[64,192]{1,0:T(8,128)S(1)} custom-call(f32[192,15360]{1,0:T(8,128)} %slab_ref.15, f32[16,15360]{1,0:T(8,128)S(1)} %add.75.refs_6_.refs_0_, f32[16,15360]{1,0:T(8,128)S(1)} %add.76.refs_7_.refs_1_, f32[16,15360]{1,0:T(8,128)S(1)} %copy-done.8, f32[16,15360]{1,0:T(8,128)S(1)} %copy-done.6), custom_call_target="tpu_custom_call" | custom-call | flops 1132462080 | bytes 15728640 | tf_op jit(solution)/shard_map/project/pallas_call | solution.py:58
  217.3 1.7 collective-permute-start.18
  219.0 0.7 pad_maximum_fusion.4
  219.7 1.5 collective-permute-start.20
  221.7 2.0 collective-permute-done.18
  223.7 0.6 copy-done.31
  224.3 0.5 collective-permute-start.19
  224.9 2.3 reshape.43
  227.2 2.0 rev.3
  229.2 2.3 reshape.44
  231.5 0.9 broadcast_select_fusion.2.cross_ref
  232.4 1.6 collective-permute-start.30
  234.0 1.2 add_add_fusion.known_ref
  235.2 1.8 collective-permute-done.30.b_ref
  237.0 1.0 copy-done.22
  238.0 0.9 copy-done.25
  238.9 19.1 %update.1 = f32[192,15360]{1,0:T(8,128)} custom-call(f32[192,15360]{1,0:T(8,128)} %slab_ref.15, f32[2,128,128]{2,1,0:T(8,128)S(1)} %copy-done.25, f32[128,128]{1,0:T(8,128)S(1)} %broadcast_select_fusion.2.cross_ref, f32[2,96,192]{2,1,0:T(8,128)S(1)} %add_add_fusion.known_ref, f32[64,192]{1,0:T(8,128)} %add_add_fusion.1.a_ref, ...), custom_call_target="tpu_custom_call" | custom-call | flops 4529848320 | bytes 39321600 | tf_op jit(solution)/shard_map/update/pallas_call | solution.py:139
  (114 shorter events, 4.9 us)
Async XLA Ops:
  0.0 12.5 %copy-start = (f32[2,16,15360]{2,1,0:T(8,128)S(1)}, f32[2,16,15360]{2,1,0:T(8,128)}, u32[]{:S(2)}) copy-start(f32[2,16,15360]{2,1,0:T(8,128)} %refs_0_.5) | copy-start | bytes 5898244
  0.0 12.6 %copy-start.30 = (f32[2,128,128]{2,1,0:T(8,128)S(1)}, f32[2,128,128]{2,1,0:T(8,128)}, u32[]{:S(2)}) copy-start(f32[2,128,128]{2,1,0:T(8,128)} %param.5) | copy-start | bytes 393220
  2.7 30.0 %collective-permute-start.8 = (f32[16,15360]{1,0:T(8,128)S(1)}, f32[16,15360]{1,0:T(8,128)}, u32[]{:S(2)}, u32[]{:S(2)}) collective-permute-start(f32[16,15360]{1,0:T(8,128)S(1)} %get-tuple-element.5), channel_id=1, source_target_pairs={{2,4},{3,5},{4,2},{5,3},{10,12},{11,13},{12,10},{13,11},{18,20},{1... | collective-permute-start | bytes 2949128 | tf_op jit(solution)/shard_map/ppermute | solution.py:174
  4.3 27.7 %collective-permute-start.2 = (f32[16,15360]{1,0:T(8,128)S(1)}, f32[16,15360]{1,0:T(8,128)}, u32[]{:S(2)}, u32[]{:S(2)}) collective-permute-start(f32[16,15360]{1,0:T(8,128)S(1)} %get-tuple-element.5), channel_id=1, source_target_pairs={{0,2},{1,3},{2,0},{3,1},{4,6},{5,7},{6,4},{7,5},{8,10},{9,11},{10,... | collective-permute-start | bytes 2949128 | tf_op jit(solution)/shard_map/ppermute | solution.py:174
  9.3 26.1 %collective-permute-start.5 = (f32[16,15360]{1,0:T(8,128)}, f32[16,15360]{1,0:T(8,128)}, u32[]{:S(2)}, u32[]{:S(2)}) collective-permute-start(f32[16,15360]{1,0:T(8,128)} %get-tuple-element.6), channel_id=1, source_target_pairs={{2,4},{3,5},{4,2},{5,3},{10,12},{11,13},{12,10},{13,11},{18,20},{1... | collective-permute-start | bytes 2949128 | tf_op jit(solution)/shard_map/ppermute | solution.py:174
  10.9 42.2 %collective-permute-start.1 = (f32[16,15360]{1,0:T(8,128)}, f32[16,15360]{1,0:T(8,128)}, u32[]{:S(2)}, u32[]{:S(2)}) collective-permute-start(f32[16,15360]{1,0:T(8,128)} %get-tuple-element.6), channel_id=1, source_target_pairs={{0,2},{1,3},{2,0},{3,1},{4,6},{5,7},{6,4},{7,5},{8,10},{9,11},{10,... | collective-permute-start | bytes 2949128 | tf_op jit(solution)/shard_map/ppermute | solution.py:174
  12.5 117.1 %collective-permute-start = (f32[2,16,15360]{2,1,0:T(8,128)S(1)}, f32[2,16,15360]{2,1,0:T(8,128)}, u32[]{:S(2)}, u32[]{:S(2)}) collective-permute-start(f32[2,16,15360]{2,1,0:T(8,128)S(1)} %copy-done), channel_id=1, source_target_pairs={{0,1},{1,0},{2,3},{3,2},{4,5},{5,4},{6,7},{7,6},{8,9},{9,8},{10,11... | collective-permute-start | bytes 5898248 | tf_op jit(solution)/shard_map/ppermute | solution.py:174
  32.0 23.2 %collective-permute-start.10 = (f32[16,15360]{1,0:T(8,128)}, f32[16,15360]{1,0:T(8,128)S(1)}, u32[]{:S(2)}, u32[]{:S(2)}) collective-permute-start(f32[16,15360]{1,0:T(8,128)} %collective-permute-done.2.refs_3_.refs_1_), channel_id=1, source_target_pairs={{2,4},{3,5},{4,2},{5,3},{10,12},{11,13},{12,10},{13,11},{18,20},{1... | collective-permute-start | bytes 2949128 | tf_op jit(solution)/shard_map/ppermute | solution.py:174
  34.1 38.8 %collective-permute-start.9 = (f32[16,15360]{1,0:T(8,128)}, f32[16,15360]{1,0:T(8,128)S(1)}, u32[]{:S(2)}, u32[]{:S(2)}) collective-permute-start(f32[16,15360]{1,0:T(8,128)} %collective-permute-done.8.refs_11_), channel_id=1, source_target_pairs={{2,0},{3,1},{4,6},{5,7},{10,8},{11,9},{12,14},{13,15},{18,16},{19,... | collective-permute-start | bytes 2949128 | tf_op jit(solution)/shard_map/ppermute | solution.py:174
  35.5 84.3 %collective-permute-start.4 = (f32[16,15360]{1,0:T(8,128)}, f32[16,15360]{1,0:T(8,128)S(1)}, u32[]{:S(2)}, u32[]{:S(2)}) collective-permute-start(f32[16,15360]{1,0:T(8,128)} %collective-permute-done.2.refs_3_.refs_1_), channel_id=1, source_target_pairs={{0,1},{1,0},{2,3},{3,2},{4,5},{5,4},{6,7},{7,6},{8,9},{9,8},{10,11... | collective-permute-start | bytes 2949128 | tf_op jit(solution)/shard_map/ppermute | solution.py:174
  53.1 3.5 %collective-permute-start.7 = (f32[16,15360]{1,0:T(8,128)}, f32[16,15360]{1,0:T(8,128)S(1)}, u32[]{:S(2)}, u32[]{:S(2)}) collective-permute-start(f32[16,15360]{1,0:T(8,128)} %collective-permute-done.1.refs_2_.refs_0_), channel_id=1, source_target_pairs={{2,4},{3,5},{4,2},{5,3},{10,12},{11,13},{12,10},{13,11},{18,20},{1... | collective-permute-start | bytes 2949128 | tf_op jit(solution)/shard_map/ppermute | solution.py:174
  55.2 40.4 %collective-permute-start.6 = (f32[16,15360]{1,0:T(8,128)}, f32[16,15360]{1,0:T(8,128)S(1)}, u32[]{:S(2)}, u32[]{:S(2)}) collective-permute-start(f32[16,15360]{1,0:T(8,128)} %collective-permute-done.5.refs_10_), channel_id=1, source_target_pairs={{2,0},{3,1},{4,6},{5,7},{10,8},{11,9},{12,14},{13,15},{18,16},{19,... | collective-permute-start | bytes 2949128 | tf_op jit(solution)/shard_map/ppermute | solution.py:174
  56.7 51.1 %collective-permute-start.22 = (f32[2,16,3840]{2,1,0:T(8,128)S(1)}, f32[2,16,3840]{2,1,0:T(8,128)S(1)}, u32[]{:S(2)}, u32[]{:S(2)}) collective-permute-start(f32[2,16,3840]{2,1,0:T(8,128)S(1)} %pad_maximum_fusion), channel_id=1, source_target_pairs={{2,0},{3,1},{4,6},{5,7},{10,8},{11,9},{12,14},{13,15},{18,16},{19,... | collective-permute-start | bytes 1474568 | tf_op jit(solution)/shard_map/ppermute | solution.py:174
  72.9 56.1 %collective-permute-start.3 = (f32[16,15360]{1,0:T(8,128)}, f32[16,15360]{1,0:T(8,128)S(1)}, u32[]{:S(2)}, u32[]{:S(2)}) collective-permute-start(f32[16,15360]{1,0:T(8,128)} %collective-permute-done.1.refs_2_.refs_0_), channel_id=1, source_target_pairs={{0,1},{1,0},{2,3},{3,2},{4,5},{5,4},{6,7},{7,6},{8,9},{9,8},{10,11... | collective-permute-start | bytes 2949128 | tf_op jit(solution)/shard_map/ppermute | solution.py:174
  73.0 129.8 %copy-start.1 = (f32[16,15360]{1,0:T(8,128)}, f32[16,15360]{1,0:T(8,128)S(1)}, u32[]{:S(2)}) copy-start(f32[16,15360]{1,0:T(8,128)S(1)} %add.76.refs_7_.refs_1_) | copy-start | bytes 2949124
  95.6 22.7 %collective-permute-start.26 = (f32[2,16,3840]{2,1,0:T(8,128)S(1)}, f32[2,16,3840]{2,1,0:T(8,128)S(1)}, u32[]{:S(2)}, u32[]{:S(2)}) collective-permute-start(f32[2,16,3840]{2,1,0:T(8,128)S(1)} %pad_maximum_fusion.2), channel_id=1, source_target_pairs={{2,0},{3,1},{4,6},{5,7},{10,8},{11,9},{12,14},{13,15},{18,16},{19,... | collective-permute-start | bytes 1474568 | tf_op jit(solution)/shard_map/ppermute | solution.py:174
  97.0 105.7 %copy-start.2 = (f32[16,15360]{1,0:T(8,128)}, f32[16,15360]{1,0:T(8,128)S(1)}, u32[]{:S(2)}) copy-start(f32[16,15360]{1,0:T(8,128)S(1)} %add.75.refs_6_.refs_0_) | copy-start | bytes 2949124
  107.8 21.1 %collective-permute-start.28 = (f32[2,16,3840]{2,1,0:T(8,128)S(1)}, f32[2,16,3840]{2,1,0:T(8,128)S(1)}, u32[]{:S(2)}, u32[]{:S(2)}) collective-permute-start(f32[2,16,3840]{2,1,0:T(8,128)S(1)} %pad_maximum_fusion.3), channel_id=1, source_target_pairs={{2,0},{3,1},{4,6},{5,7},{10,8},{11,9},{12,14},{13,15},{18,16},{19,... | collective-permute-start | bytes 1474568 | tf_op jit(solution)/shard_map/ppermute | solution.py:174
  118.4 19.4 %collective-permute-start.24 = (f32[2,16,3840]{2,1,0:T(8,128)S(1)}, f32[2,16,3840]{2,1,0:T(8,128)S(1)}, u32[]{:S(2)}, u32[]{:S(2)}) collective-permute-start(f32[2,16,3840]{2,1,0:T(8,128)S(1)} %pad_maximum_fusion.1), channel_id=1, source_target_pairs={{2,0},{3,1},{4,6},{5,7},{10,8},{11,9},{12,14},{13,15},{18,16},{19,... | collective-permute-start | bytes 1474568 | tf_op jit(solution)/shard_map/ppermute | solution.py:174
  119.7 22.9 %copy-start.28 = (f32[2,128,128]{2,1,0:T(8,128)S(1)}, f32[2,128,128]{2,1,0:T(8,128)}, u32[]{:S(2)}) copy-start(f32[2,128,128]{2,1,0:T(8,128)} %gather.12) | copy-start | bytes 393220
  119.7 51.5 %copy-start.9 = (f32[2,16,3840]{2,1,0:T(8,128)}, f32[2,16,3840]{2,1,0:T(8,128)S(1)}, u32[]{:S(2)}) copy-start(f32[2,16,3840]{2,1,0:T(8,128)S(1)} %maximum_add_fusion.2.refs_0_.refs_14_) | copy-start | bytes 1474564
  119.8 66.4 %copy-start.3 = (f32[16,15360]{1,0:T(8,128)}, f32[16,15360]{1,0:T(8,128)S(1)}, u32[]{:S(2)}) copy-start(f32[16,15360]{1,0:T(8,128)S(1)} %collective-permute-done.4.refs_5_.refs_3_) | copy-start | bytes 2949124
  119.8 18.0 %collective-permute-start.23 = (f32[2,16,3840]{2,1,0:T(8,128)S(1)}, f32[2,16,3840]{2,1,0:T(8,128)S(1)}, u32[]{:S(2)}, u32[]{:S(2)}) collective-permute-start(f32[2,16,3840]{2,1,0:T(8,128)S(1)} %maximum_add_fusion.refs_0_.refs_10_), channel_id=1, source_target_pairs={{0,1},{1,0},{2,3},{3,2},{4,5},{5,4},{6,7},{7,6},{8,9},{9,8},{10,11... | collective-permute-start | bytes 1474568 | tf_op jit(solution)/shard_map/ppermute | solution.py:174
  128.9 9.4 %collective-permute-start.27 = (f32[2,16,3840]{2,1,0:T(8,128)S(1)}, f32[2,16,3840]{2,1,0:T(8,128)S(1)}, u32[]{:S(2)}, u32[]{:S(2)}) collective-permute-start(f32[2,16,3840]{2,1,0:T(8,128)S(1)} %maximum_add_fusion.2.refs_0_.refs_14_), channel_id=1, source_target_pairs={{0,1},{1,0},{2,3},{3,2},{4,5},{5,4},{6,7},{7,6},{8,9},{9,8},{10,11... | collective-permute-start | bytes 1474568 | tf_op jit(solution)/shard_map/ppermute | solution.py:174
  129.0 46.0 %copy-start.11 = (f32[2,16,3840]{2,1,0:T(8,128)}, f32[2,16,3840]{2,1,0:T(8,128)S(1)}, u32[]{:S(2)}) copy-start(f32[2,16,3840]{2,1,0:T(8,128)S(1)} %maximum_add_fusion.3.refs_0_.refs_16_) | copy-start | bytes 1474564
  129.0 57.2 %copy-start.4 = (f32[16,15360]{1,0:T(8,128)}, f32[16,15360]{1,0:T(8,128)S(1)}, u32[]{:S(2)}) copy-start(f32[16,15360]{1,0:T(8,128)S(1)} %collective-permute-done.3.refs_4_.refs_2_) | copy-start | bytes 2949124
  129.0 56.7 %collective-permute-start.14 = (f32[16,15360]{1,0:T(8,128)}, f32[16,15360]{1,0:T(8,128)S(1)}, u32[]{:S(2)}, u32[]{:S(2)}) collective-permute-start(f32[16,15360]{1,0:T(8,128)} %collective-permute-done.8.refs_11_), channel_id=1, source_target_pairs={{0,1},{1,0},{2,3},{3,2},{4,5},{5,4},{6,7},{7,6},{8,9},{9,8},{10,11... | collective-permute-start | bytes 2949128 | tf_op jit(solution)/shard_map/ppermute | solution.py:174
  129.6 56.6 %collective-permute-start.13 = (f32[16,15360]{1,0:T(8,128)}, f32[16,15360]{1,0:T(8,128)S(1)}, u32[]{:S(2)}, u32[]{:S(2)}) collective-permute-start(f32[16,15360]{1,0:T(8,128)} %collective-permute-done.5.refs_10_), channel_id=1, source_target_pairs={{0,1},{1,0},{2,3},{3,2},{4,5},{5,4},{6,7},{7,6},{8,9},{9,8},{10,11... | collective-permute-start | bytes 2949128 | tf_op jit(solution)/shard_map/ppermute | solution.py:174
  137.7 48.4 %collective-permute-start.12 = (f32[16,15360]{1,0:T(8,128)S(1)}, f32[16,15360]{1,0:T(8,128)S(1)}, u32[]{:S(2)}, u32[]{:S(2)}) collective-permute-start(f32[16,15360]{1,0:T(8,128)S(1)} %add.76.refs_7_.refs_1_), channel_id=1, source_target_pairs={{0,1},{1,0},{2,3},{3,2},{4,5},{5,4},{6,7},{7,6},{8,9},{9,8},{10,11... | collective-permute-start | bytes 2949128 | tf_op jit(solution)/shard_map/ppermute | solution.py:174
  137.8 29.8 %copy-start.15 = (f32[2,16,3840]{2,1,0:T(8,128)}, f32[2,16,3840]{2,1,0:T(8,128)S(1)}, u32[]{:S(2)}) copy-start(f32[2,16,3840]{2,1,0:T(8,128)S(1)} %collective-permute-done.23.refs_1_.refs_11_) | copy-start | bytes 1474564
  137.8 48.4 %collective-permute-start.11 = (f32[16,15360]{1,0:T(8,128)S(1)}, f32[16,15360]{1,0:T(8,128)S(1)}, u32[]{:S(2)}, u32[]{:S(2)}) collective-permute-start(f32[16,15360]{1,0:T(8,128)S(1)} %add.75.refs_6_.refs_0_), channel_id=1, source_target_pairs={{0,1},{1,0},{2,3},{3,2},{4,5},{5,4},{6,7},{7,6},{8,9},{9,8},{10,11... | collective-permute-start | bytes 2949128 | tf_op jit(solution)/shard_map/ppermute | solution.py:174
  138.3 33.0 %copy-start.17 = (f32[2,16,3840]{2,1,0:T(8,128)}, f32[2,16,3840]{2,1,0:T(8,128)S(1)}, u32[]{:S(2)}) copy-start(f32[2,16,3840]{2,1,0:T(8,128)S(1)} %collective-permute-done.27.refs_1_.refs_15_) | copy-start | bytes 1474564
  138.3 4.2 %collective-permute-start.29 = (f32[2,16,3840]{2,1,0:T(8,128)S(1)}, f32[2,16,3840]{2,1,0:T(8,128)S(1)}, u32[]{:S(2)}, u32[]{:S(2)}) collective-permute-start(f32[2,16,3840]{2,1,0:T(8,128)S(1)} %maximum_add_fusion.3.refs_0_.refs_16_), channel_id=1, source_target_pairs={{0,1},{1,0},{2,3},{3,2},{4,5},{5,4},{6,7},{7,6},{8,9},{9,8},{10,11... | collective-permute-start | bytes 1474568 | tf_op jit(solution)/shard_map/ppermute | solution.py:174
  138.4 40.3 %copy-start.13 = (f32[2,16,3840]{2,1,0:T(8,128)}, f32[2,16,3840]{2,1,0:T(8,128)S(1)}, u32[]{:S(2)}) copy-start(f32[2,16,3840]{2,1,0:T(8,128)S(1)} %maximum_add_fusion.1.refs_0_.refs_12_) | copy-start | bytes 1474564
  142.4 32.6 %copy-start.19 = (f32[2,16,3840]{2,1,0:T(8,128)}, f32[2,16,3840]{2,1,0:T(8,128)S(1)}, u32[]{:S(2)}) copy-start(f32[2,16,3840]{2,1,0:T(8,128)S(1)} %collective-permute-done.29.refs_1_.refs_17_) | copy-start | bytes 1474564
  142.4 36.3 %collective-permute-start.25 = (f32[2,16,3840]{2,1,0:T(8,128)S(1)}, f32[2,16,3840]{2,1,0:T(8,128)S(1)}, u32[]{:S(2)}, u32[]{:S(2)}) collective-permute-start(f32[2,16,3840]{2,1,0:T(8,128)S(1)} %maximum_add_fusion.1.refs_0_.refs_12_), channel_id=1, source_target_pairs={{0,1},{1,0},{2,3},{3,2},{4,5},{5,4},{6,7},{7,6},{8,9},{9,8},{10,11... | collective-permute-start | bytes 1474568 | tf_op jit(solution)/shard_map/ppermute | solution.py:174
  167.6 51.4 %copy-start.23 = (f32[64,192]{1,0:T(8,128)}, f32[64,192]{1,0:T(8,128)S(1)}, u32[]{:S(2)}) copy-start(f32[64,192]{1,0:T(8,128)S(1)} %project.8) | copy-start | bytes 147460
  178.7 3.9 %copy-start.21 = (f32[2,16,3840]{2,1,0:T(8,128)}, f32[2,16,3840]{2,1,0:T(8,128)S(1)}, u32[]{:S(2)}) copy-start(f32[2,16,3840]{2,1,0:T(8,128)S(1)} %collective-permute-done.25.refs_1_.refs_13_) | copy-start | bytes 1474564
  183.2 51.9 %collective-permute-start.32 = (f32[64,192]{1,0:T(8,128)}, f32[64,192]{1,0:T(8,128)}, u32[]{:S(2)}, u32[]{:S(2)}) collective-permute-start(f32[64,192]{1,0:T(8,128)} %add_add_fusion.1.a_ref), channel_id=1, source_target_pairs={{0,24},{8,16},{16,8},{24,0},{1,25},{9,17},{17,9},{25,1},{2,26},{10... | collective-permute-start | bytes 147464 | tf_op jit(solution)/shard_map/ppermute | solution.py:155
  185.7 1.0 copy-start.26
  185.7 49.5 %collective-permute-start.31 = (f32[64,192]{1,0:T(8,128)}, f32[64,192]{1,0:T(8,128)}, u32[]{:S(2)}, u32[]{:S(2)}) collective-permute-start(f32[64,192]{1,0:T(8,128)} %add_add_fusion.1.a_ref), channel_id=1, source_target_pairs={{0,16},{8,24},{16,0},{24,8},{1,17},{9,25},{17,1},{25,9},{2,18},{10... | collective-permute-start | bytes 147464 | tf_op jit(solution)/shard_map/ppermute | solution.py:155
  186.2 0.9 copy-start.27
  186.2 1.3 copy-start.5
  187.5 1.0 copy-start.7
  199.2 17.9 %collective-permute-start.17 = (f32[128,128]{1,0:T(8,128)S(1)}, f32[128,128]{1,0:T(8,128)S(1)}, u32[]{:S(2)}, u32[]{:S(2)}) collective-permute-start(f32[128,128]{1,0:T(8,128)S(1)} %cross.1), channel_id=1, source_target_pairs={{0,24},{8,16},{16,8},{24,0},{1,25},{9,17},{17,9},{25,1},{2,26},{10... | collective-permute-start | bytes 196616 | tf_op jit(solution)/shard_map/ppermute | solution.py:155
  200.8 16.4 %collective-permute-start.16 = (f32[128,128]{1,0:T(8,128)S(1)}, f32[128,128]{1,0:T(8,128)S(1)}, u32[]{:S(2)}, u32[]{:S(2)}) collective-permute-start(f32[128,128]{1,0:T(8,128)S(1)} %cross.1), channel_id=1, source_target_pairs={{0,16},{8,24},{16,0},{24,8},{1,17},{9,25},{17,1},{25,9},{2,18},{10... | collective-permute-start | bytes 196616 | tf_op jit(solution)/shard_map/ppermute | solution.py:155
  201.3 15.9 %collective-permute-start.15 = (f32[128,128]{1,0:T(8,128)S(1)}, f32[128,128]{1,0:T(8,128)S(1)}, u32[]{:S(2)}, u32[]{:S(2)}) collective-permute-start(f32[128,128]{1,0:T(8,128)S(1)} %cross.1), channel_id=1, source_target_pairs={{0,8},{8,0},{16,24},{24,16},{1,9},{9,1},{17,25},{25,17},{2,10},{10... | collective-permute-start | bytes 196616 | tf_op jit(solution)/shard_map/ppermute | solution.py:155
  202.8 1.2 copy-start.6
  204.0 1.2 copy-start.8
  217.1 2.6 copy-start.24
  217.2 4.0 %copy-start.29 = (f32[128,128]{1,0:T(8,128)}, f32[128,128]{1,0:T(8,128)S(1)}, u32[]{:S(2)}) copy-start(f32[128,128]{1,0:T(8,128)S(1)} %add_add_fusion.2) | copy-start | bytes 196612
  217.2 19.7 %copy-start.10 = (f32[2,16,3840]{2,1,0:T(8,128)S(1)}, f32[2,16,3840]{2,1,0:T(8,128)}, u32[]{:S(2)}) copy-start(f32[2,16,3840]{2,1,0:T(8,128)} %copy-done.9) | copy-start | bytes 1474564
  217.2 19.7 %copy-start.12 = (f32[2,16,3840]{2,1,0:T(8,128)S(1)}, f32[2,16,3840]{2,1,0:T(8,128)}, u32[]{:S(2)}) copy-start(f32[2,16,3840]{2,1,0:T(8,128)} %copy-done.11) | copy-start | bytes 1474564
  217.2 19.7 %copy-start.14 = (f32[2,16,3840]{2,1,0:T(8,128)S(1)}, f32[2,16,3840]{2,1,0:T(8,128)}, u32[]{:S(2)}) copy-start(f32[2,16,3840]{2,1,0:T(8,128)} %copy-done.13) | copy-start | bytes 1474564
  217.2 19.7 %copy-start.16 = (f32[2,16,3840]{2,1,0:T(8,128)S(1)}, f32[2,16,3840]{2,1,0:T(8,128)}, u32[]{:S(2)}) copy-start(f32[2,16,3840]{2,1,0:T(8,128)} %copy-done.15) | copy-start | bytes 1474564
  217.3 19.7 %copy-start.18 = (f32[2,16,3840]{2,1,0:T(8,128)S(1)}, f32[2,16,3840]{2,1,0:T(8,128)}, u32[]{:S(2)}) copy-start(f32[2,16,3840]{2,1,0:T(8,128)} %copy-done.17) | copy-start | bytes 1474564
  217.3 19.7 %copy-start.20 = (f32[2,16,3840]{2,1,0:T(8,128)S(1)}, f32[2,16,3840]{2,1,0:T(8,128)}, u32[]{:S(2)}) copy-start(f32[2,16,3840]{2,1,0:T(8,128)} %copy-done.19) | copy-start | bytes 1474564
  217.3 6.4 %collective-permute-start.18 = (f32[128,128]{1,0:T(8,128)S(1)}, f32[128,128]{1,0:T(8,128)S(1)}, u32[]{:S(2)}, u32[]{:S(2)}) collective-permute-start(f32[128,128]{1,0:T(8,128)S(1)} %add_add_fusion.2), channel_id=1, source_target_pairs={{2,0},{3,1},{4,6},{5,7},{10,8},{11,9},{12,14},{13,15},{18,16},{19,... | collective-permute-start | bytes 196616 | tf_op jit(solution)/shard_map/ppermute | solution.py:174
  219.7 12.7 %collective-permute-start.20 = (f32[2,96,192]{2,1,0:T(8,128)}, f32[2,96,192]{2,1,0:T(8,128)}, u32[]{:S(2)}, u32[]{:S(2)}) collective-permute-start(f32[2,96,192]{2,1,0:T(8,128)} %pad_maximum_fusion.4), channel_id=1, source_target_pairs={{0,16},{8,24},{16,0},{24,8},{1,17},{9,25},{17,1},{25,9},{2,18},{10... | collective-permute-start | bytes 442376 | tf_op jit(solution)/shard_map/ppermute | solution.py:155
  221.2 12.7 %collective-permute-start.21 = (f32[2,96,192]{2,1,0:T(8,128)}, f32[2,96,192]{2,1,0:T(8,128)}, u32[]{:S(2)}, u32[]{:S(2)}) collective-permute-start(f32[2,96,192]{2,1,0:T(8,128)} %pad_maximum_fusion.4), channel_id=1, source_target_pairs={{0,24},{8,16},{16,8},{24,0},{1,25},{9,17},{17,9},{25,1},{2,26},{10... | collective-permute-start | bytes 442376 | tf_op jit(solution)/shard_map/ppermute | solution.py:155
  224.3 9.6 %collective-permute-start.19 = (f32[2,96,192]{2,1,0:T(8,128)}, f32[2,96,192]{2,1,0:T(8,128)}, u32[]{:S(2)}, u32[]{:S(2)}) collective-permute-start(f32[2,96,192]{2,1,0:T(8,128)} %pad_maximum_fusion.4), channel_id=1, source_target_pairs={{0,8},{8,0},{16,24},{24,16},{1,9},{9,1},{17,25},{25,17},{2,10},{10... | collective-permute-start | bytes 442376 | tf_op jit(solution)/shard_map/ppermute | solution.py:155
  232.4 4.5 %collective-permute-start.30 = (f32[64,192]{1,0:T(8,128)}, f32[64,192]{1,0:T(8,128)S(1)}, u32[]{:S(2)}, u32[]{:S(2)}) collective-permute-start(f32[64,192]{1,0:T(8,128)} %add_add_fusion.1.a_ref), channel_id=1, source_target_pairs={{0,8},{8,0},{16,24},{24,16},{1,9},{9,1},{17,25},{25,17},{2,10},{10... | collective-permute-start | bytes 147464 | tf_op jit(solution)/shard_map/ppermute | solution.py:155
  237.0 1.0 copy-start.22
  238.0 0.9 copy-start.25
  (1 other events, 0.6 us)

commit v2 on v0

v2 whole, which is shorter than its diff:
```python
import functools

import jax
import jax.numpy as jnp
from jax import lax
from jax.experimental import pallas as pl
from jax.experimental.pallas import tpu as pltpu
from jax.sharding import PartitionSpec as P

F32 = jnp.float32
BF16 = jnp.bfloat16
NT = (((1,), (1,)), ((), ()))
NN = (((1,), (0,)), ((), ()))
MIB = 1024 * 1024
TILE = 2560
WIDTHS = (5, 1)
COST = dict(join=10**6, project=10**9, cross=10**9, prepare=10**6, update=10**9)


def split(x):
    high = x.astype(BF16)
    return high, (x - high.astype(F32)).astype(BF16)


def dot3(left, right, dims):
    (lh, ll), (rh, rl) = left, right
    dot = functools.partial(lax.dot_general, dimension_numbers=dims, preferred_element_type=F32)
    return dot(lh, rh) + (dot(ll, rh) + dot(lh, rl))


def exact(left, right, dims=NN):
    return lax.dot_general(left, right, dims, precision=lax.Precision.HIGHEST, preferred_element_type=F32)


def block_rows(refs):
    return jnp.concatenate([r[b] for b in (0, 1) for r in refs], axis=0)


def total(refs):
    a, b, c, d = (r[...] for r in refs)
    return (a + b) + (c + d)


def whole(x):
    return pl.BlockSpec(x.shape, lambda g: (0,) * x.ndim)


def columns(x, at=0):
    lead = x.shape[:-1]
    return pl.BlockSpec(lead + (TILE,), lambda g: (0,) * len(lead) + (at // TILE + g,))


def call(kernel, steps, operands, specs, outs, out_specs, name, scratch=(), vmem=16):
    return pl.pallas_call(
        kernel,
        out_shape=outs,
        grid=(steps,),
        in_specs=specs,
        out_specs=out_specs,
        scratch_shapes=list(scratch),
        compiler_params=pltpu.CompilerParams(vmem_limit_bytes=vmem * MIB),
        cost_estimate=pl.CostEstimate(flops=COST[name], bytes_accessed=1, transcendentals=0),
        name=name,
    )(*operands)


def corner(x):
    lead = x.ndim - 2
    return pl.BlockSpec((1,) * lead + (8, 128), lambda g: (0,) * x.ndim)


def join_kernel(a_ref, b_ref, *refs):
    refs[-1][...] = a_ref[...] + b_ref[...]


def join(a, b, at, *after):
    out = jax.ShapeDtypeStruct(a.shape, F32)
    return call(
        join_kernel,
        a.shape[-1] // TILE,
        [a, b, *after],
        [columns(a), columns(b, at)] + [corner(y) for y in after],
        out,
        columns(out),
        "join",
    )


def project_kernel(steps, started, slab_ref, *refs):
    before, refs = (refs[0], refs[1:]) if started else (None, refs)
    *pieces, proj_ref, acc_ref = refs
    step = pl.program_id(0)

    @pl.when(step == 0)
    def _():
        acc_ref[...] = jnp.zeros_like(acc_ref)

    high, low = split(block_rows(pieces))
    slab_high, slab_low = split(slab_ref[...])
    n = high.shape[0]
    dot = functools.partial(lax.dot_general, dimension_numbers=NT, preferred_element_type=F32)
    both = dot(slab_high, jnp.concatenate([high, low], axis=0))
    acc_ref[...] += both[:, :n] + (both[:, n:] + dot(slab_low, high))

    @pl.when(step == steps - 1)
    def _():
        made = acc_ref[...].T
        proj_ref[...] = made + before[...] if started else made


def project(slab, pieces, at=0, before=None):
    nev = slab.shape[0]
    mine, width = pieces[0].shape[1:]
    steps = width // TILE
    rows = 2 * mine * len(pieces)
    out = jax.ShapeDtypeStruct((rows, nev), F32)
    small = [] if before is None else [before]
    return call(
        functools.partial(project_kernel, steps, bool(small)),
        steps,
        [slab, *small, *pieces],
        [columns(slab, at)] + [whole(x) for x in small] + [columns(p) for p in pieces],
        out,
        whole(out),
        "project",
        [pltpu.VMEM((nev, rows), F32)],
    )


def cross_kernel(*refs):
    *pieces, gram_ref = refs

    @pl.when(pl.program_id(0) == 0)
    def _():
        gram_ref[...] = jnp.zeros_like(gram_ref)

    high, low = split(block_rows(pieces))
    half = high.shape[0] // 2
    gram_ref[...] += dot3((high[half:], low[half:]), (high[:half], low[:half]), NT)


def cross(pieces):
    mine, width = pieces[0].shape[1:]
    n = mine * len(pieces)
    out = jax.ShapeDtypeStruct((n, n), F32)
    return call(cross_kernel, width // TILE, pieces, [columns(p) for p in pieces], out, whole(out), "cross")


def swap_matrix(n, mask):
    row = lax.broadcasted_iota(jnp.int32, (n, n), 0)
    column = lax.broadcasted_iota(jnp.int32, (n, n), 1)
    return jnp.where(column == jnp.bitwise_xor(row, mask), 1.0, 0.0).astype(F32)


def prepare_kernel(mine, col_ref, factors_ref, gram_ref, given_ref, *refs):
    sums, (known_ref, mats_ref) = refs[:8], refs[8:]
    n = factors_ref.shape[1]
    swap = swap_matrix(n, col_ref[0] * mine)
    row = lax.broadcasted_iota(jnp.int32, (n, n), 0)
    column = lax.broadcasted_iota(jnp.int32, (n, n), 1)
    for block in range(2):
        upper = jnp.where(row <= column, factors_ref[block], 0.0)
        mats_ref[block] = exact(swap, exact(upper, swap))
    turn = swap_matrix(n, 2 * mine)
    middle = jnp.logical_and(col_ref[0] >= 2, col_ref[0] < 6)
    mats_ref[2] = jnp.where(middle, gram_ref[...], exact(turn, exact(given_ref[...], turn)))
    first, second = total(sums[:4]), total(sums[4:])
    known_ref[...] = jnp.concatenate([x[b * x.shape[0] // 2 :][: x.shape[0] // 2] for b in (0, 1) for x in (first, second)], axis=0)


def prepare(col, factors, gram, given, sums, mine):
    small = [factors, gram, given, *sums[0], *sums[1]]
    outs = [
        jax.ShapeDtypeStruct((sum(s[0].shape[0] for s in sums), sums[0][0].shape[1]), F32),
        jax.ShapeDtypeStruct((3, *gram.shape), F32),
    ]
    return call(
        functools.partial(prepare_kernel, mine),
        1,
        [col[None], *small],
        [pl.BlockSpec(memory_space=pltpu.SMEM)] + [whole(x) for x in small],
        outs,
        [whole(x) for x in outs],
        "prepare",
    )


def update_kernel(starts, base, known_ref, mats_ref, *refs):
    lasts, (slab_ref, *pieces, out_ref, left_ref) = refs[:4], refs[4:]
    step = pl.program_id(0)

    @pl.when(step == 0)
    def _():
        last = total(lasts)
        kept, rest = known_ref.shape[0] // 2, last.shape[0] // 2
        half = lambda b: jnp.concatenate([known_ref[b * kept : (b + 1) * kept], last[b * rest : (b + 1) * rest]], axis=0)
        first = exact(mats_ref[0], half(0))
        second = exact(mats_ref[1], half(1) - exact(mats_ref[2], first))
        high, low = split(jnp.concatenate([first, second], axis=0).T)
        left_ref[...] = jnp.concatenate([high, low, high], axis=1)

    each = (len(pieces) - base) // (len(starts) - 1)
    for i in range(len(starts) - 1):

        @pl.when(jnp.logical_and(step >= starts[i], step < starts[i + 1]))
        def _():
            high, low = split(block_rows(pieces[:base] + pieces[base + each * i : base + each * (i + 1)]))
            right = jnp.concatenate([high, high, low], axis=0)
            out_ref[...] = slab_ref[...] - lax.dot_general(left_ref[...], right, NN, preferred_element_type=F32)


def update(known, mats, lasts, slab, pieces, parts):
    mine = pieces[0].shape[1]
    nev, width = slab.shape
    small = [known, mats, *lasts]
    starts, specs = [0], []
    for part in parts:
        first, count = starts[-1], part[0].shape[-1] // TILE
        starts.append(first + count)
        specs += [
            pl.BlockSpec((2, mine, TILE), lambda g, first=first, count=count: (0, 0, jnp.clip(g - first, 0, count - 1)))
            for x in part
        ]
    stay = [pltpu.with_memory_space_constraint(x, pltpu.HBM) for x in (slab, *pieces)]
    return call(
        functools.partial(update_kernel, starts, len(pieces)),
        width // TILE,
        [*small, *stay, *[x for part in parts for x in part]],
        [whole(x) for x in small] + [columns(x) for x in (slab, *pieces)] + specs,
        jax.ShapeDtypeStruct(slab.shape, F32),
        columns(slab),
        "update",
        [pltpu.VMEM((nev, 6 * mats.shape[1]), BF16)],
        vmem=32,
    )


def others(x):
    return [lax.ppermute(x, "row", [(i, i ^ k) for i in range(4)]) for k in (1, 2, 3)]


def cores(pairs):
    return [(2 * a + c, 2 * b + c) for a, b in pairs for c in (0, 1)]


PAIR = cores([(0, 1), (1, 0), (2, 3), (3, 2)])
MIDDLE = cores([(1, 2), (2, 1)])
OUTWARD = cores([(1, 0), (2, 3)])
SIBLING = [(i, i ^ 1) for i in range(8)]


def along(x, pairs):
    return lax.ppermute(x, "col", pairs)


def line_of_four(slab, householder, factors):
    col = lax.axis_index("col")
    mine, width = householder.shape[1:]
    swap = lambda x: along(x, SIBLING)
    other = swap(householder)

    beside, inner = along(householder, PAIR), along(householder, MIDDLE)
    across, outer = along(beside, MIDDLE), along(inner, OUTWARD)
    stretches = [(sum(WIDTHS[:i]) * TILE, w * TILE) for i, w in enumerate(WIDTHS)]
    final = [along(across if w == width else across[:, :, at : at + w], OUTWARD) for at, w in stretches]
    inner2 = swap(inner)

    near = [householder, other, beside, swap(beside)]
    p0 = project(slab, near)
    sums0 = [p0, *others(p0)]
    third = join(outer, across, 0, *sums0)
    third = [third, swap(third)]
    p1 = project(slab, third)
    gram = cross(near + third + [inner, inner2])
    sums1 = [p1, *others(p1)]
    a, b, c = others(gram)
    gram = (gram + a) + (b + c)
    known, mats = prepare(col, factors, gram, along(gram, OUTWARD), [sums0, sums1], mine)

    last, parts, behind = None, [], [known]
    for i, (at, w) in enumerate(stretches):
        fourth = join(final[i], inner, at, *behind)
        parts.append([fourth, swap(fourth)])
        last = project(slab, parts[-1], at, last)
        behind = [last]
    return update(known, mats, [last, *others(last)], slab, near + third, parts)


def any_mesh(slab, householder, factors):
    upper = jnp.triu(factors)
    for block in range(householder.shape[0]):
        vectors = lax.all_gather(householder[block], "col", axis=0, tiled=True)
        projection = lax.psum(exact(vectors, slab, NT), "row")
        coeffs = exact(upper[block], projection)
        slab = slab - exact(coeffs, vectors, (((0,), (0,)), ((), ())))
    return slab


def solution(mesh):
    small = mesh.shape["col"] == 8 and mesh.shape["row"] == 4
    return jax.shard_map(
        line_of_four if small else any_mesh,
        mesh=mesh,
        in_specs=(P("col", "row"), P(None, "col", "row"), P()),
        out_specs=P("col", "row"),
        check_vma=False,
    )
```

time: 305 us -> 184 us (0.60)
  waiting for transfers between devices: 224 us -> 100 us
  matrix products: 65.3 us -> 0 us
  Pallas kernels: 0 us -> 43.8 us
  starting transfers between devices: 0.3 us -> 25.2 us
  between operations: 13.2 us -> 0.36 us
  local copies, waits for them, and re-layouts: 2.9 us -> 14.2 us
    all_gather x2 -> x0, waiting for transfers between devices: 143 us -> none  [gather_block(): return lax.all_gather(piece, 'col', axis=0, tiled=True)]
    ppermute x0 -> x25, waiting for transfers between devices: none -> 100 us  [the longest x13 89.7 us: along(): return lax.ppermute(x, 'col', pairs)]
    psum x2 -> x0, waiting for transfers between devices: 80.2 us -> none  [reduce_apply(): summed = lax.psum(partial_value, 'row')]
    dot_general x6 -> x0, matrix products: 65.3 us -> none  [the longest x2 32.8 us: update(): lax.dot_general(coeffs, vectors, (((0,), (0,)), ((), ())), precision=lax....]
    pallas_call x0 -> x10, Pallas kernels: none -> 43.8 us  [call(): pl.pallas_call(kernel, out_shape=outs, grid=(steps,), in_specs=specs, out...]
    ppermute x0 -> x25, starting transfers between devices: none -> 25.2 us  [the longest x12 14.2 us: others(): lax.ppermute(x, 'row', [(i, i ^ k) for i in range(4)])]
    unnamed x2 -> x36, local copies, waits for them, and re-layouts: 0.01 us -> 11.9 us
  transfers between devices with their start and end apart: 4 -> 25, of which waited for: 4 -> 17; matrix products, arithmetic and copies ran while one was open for 6% -> 1% of each run, Pallas kernels for 0% -> 13%
where the time goes in v2:
time: 184 us
  waiting for transfers between devices  100 us (54%)
  Pallas kernels  43.8 us (24%)
  starting transfers between devices  25.2 us (14%)
  local copies, waits for them, and re-layouts  14.2 us (8%)
    ppermute x13, waiting for transfers between devices, along(): return lax.ppermute(x, 'col', pairs)  89.7 us
    pallas_call x10, Pallas kernels, call(): pl.pallas_call(kernel, out_shape=outs, grid=(steps,), in_specs=specs, out...  43.8 us
    ppermute x12, starting transfers between devices, others(): lax.ppermute(x, 'row', [(i, i ^ k) for i in range(4)])  14.2 us
    unnamed x36, local copies, waits for them, and re-layouts  11.9 us
    ppermute x13, starting transfers between devices, along(): return lax.ppermute(x, 'col', pairs)  10.9 us
    ppermute x12, waiting for transfers between devices, others(): lax.ppermute(x, 'row', [(i, i ^ k) for i in range(4)])  10.5 us
  transfers between devices with their start and end apart: 25, of which 17 were waited for; matrix products, arithmetic and copies ran while one was open for 1% of the time, Pallas kernels for 13%

profile of v2, /device:TPU:0, one launch (start us, length us, event | category | flops | bytes accessed | tf_op | source)
XLA Modules:
  0.0 183.7 jit_solution(14311177504876412383)
XLA Ops:
  0.0 3.0 %collective-permute-start.1 = (f32[2,16,15360]{2,1,0:T(8,128)}, f32[2,16,15360]{2,1,0:T(8,128)S(1)}, u32[]{:S(2)}, u32[]{:S(2)}) collective-permute-start(f32[2,16,15360]{2,1,0:T(8,128)} %refs_5_.1), channel_id=1, source_target_pairs={{0,2},{1,3},{2,0},{3,1},{4,6},{5,7},{6,4},{7,5},{8,10},{9,11},{10,... | collective-permute-start | bytes 5898248 | tf_op jit(solution)/shard_map/ppermute | solution.py:253
  3.0 0.8 collective-permute-start.3
  3.8 0.1 collective-permute-start
  3.9 42.2 %collective-permute-done.1.refs_2_.refs_7_ = f32[2,16,15360]{2,1,0:T(8,128)S(1)} collective-permute-done((f32[2,16,15360]{2,1,0:T(8,128)}, f32[2,16,15360]{2,1,0:T(8,128)S(1)}, u32[]{:S(2)}, u32[]{:S(2)}) %collective-permute-start.1) | collective-permute-done | bytes 1966112 | tf_op jit(solution)/shard_map/ppermute | solution.py:253
  46.1 0.0 collective-permute-start.2
  46.1 0.0 collective-permute-done.3.refs_6_.b_ref
  46.1 0.0 copy-start.9
  46.1 1.3 collective-permute-start.4
  47.4 0.8 collective-permute-start.5
  48.2 1.8 collective-permute-done.2.refs_3_.refs_8_
  50.0 4.3 %copy-done = f32[192,15360]{1,0:T(8,128)S(1)} copy-done((f32[192,15360]{1,0:T(8,128)S(1)}, f32[192,15360]{1,0:T(8,128)}, u32[]{:S(2)}) %copy-start) | copy-done | bytes 11796504
  54.4 1.5 copy-done.4
  55.9 6.5 %project.4.refs_0_ = f32[128,192]{1,0:T(8,128)S(1)} custom-call(f32[192,15360]{1,0:T(8,128)S(1)} %copy-done, f32[2,16,15360]{2,1,0:T(8,128)S(1)} %copy-done.4, f32[2,16,15360]{2,1,0:T(8,128)S(1)} %collective-permute-done.refs_1_.refs_6_, f32[2,16,15360]{2,1,0:T(8,128)S(1)} %collective-permute-done.1.refs_2_.refs_7_, ...), custom_call_target="tpu_custom_call" | custom-call | flops 1000000000 | bytes 1 | tf_op jit(solution)/shard_map/project/pallas_call | solution.py:54
  62.4 2.7 %collective-permute-start.8 = (f32[128,192]{1,0:T(8,128)S(1)}, f32[128,192]{1,0:T(8,128)S(1)}, u32[]{:S(2)}, u32[]{:S(2)}) collective-permute-start(f32[128,192]{1,0:T(8,128)S(1)} %project.4.refs_0_), channel_id=1, source_target_pairs={{0,24},{8,16},{16,8},{24,0},{1,25},{9,17},{17,9},{25,1},{2,26},{10... | collective-permute-start | bytes 294920 | tf_op jit(solution)/shard_map/ppermute | solution.py:239
  65.1 0.5 collective-permute-start.7
  65.6 0.4 collective-permute-start.6
  66.0 28.0 %collective-permute-done.4.a_ref = f32[2,16,15360]{2,1,0:T(8,128)S(1)} collective-permute-done((f32[2,16,15360]{2,1,0:T(8,128)S(1)}, f32[2,16,15360]{2,1,0:T(8,128)S(1)}, u32[]{:S(2)}, u32[]{:S(2)}) %collective-permute-start.4) | collective-permute-done | bytes 1966112 | tf_op jit(solution)/shard_map/ppermute | solution.py:253
  94.0 0.0 collective-permute-start.10
  94.1 0.0 copy-start.5
  94.1 0.0 slice-start
  94.1 0.7 join.3.refs_4_.refs_0_.refs_9_
  94.9 0.0 slice-start.1
  94.9 0.6 collective-permute-start.9
  95.4 1.3 slice.8
  96.8 1.5 collective-permute-start.18
  98.4 2.5 %collective-permute-done.9.refs_5_.refs_1_.refs_10_ = f32[2,16,15360]{2,1,0:T(8,128)S(1)} collective-permute-done((f32[2,16,15360]{2,1,0:T(8,128)S(1)}, f32[2,16,15360]{2,1,0:T(8,128)S(1)}, u32[]{:S(2)}, u32[]{:S(2)}) %collective-permute-start.9) | collective-permute-done | bytes 1966112 | tf_op jit(solution)/shard_map/ppermute | solution.py:253
  100.9 5.5 %cross.1 = f32[128,128]{1,0:T(8,128)S(1)} custom-call(f32[2,16,15360]{2,1,0:T(8,128)S(1)} %copy-done.5, f32[2,16,15360]{2,1,0:T(8,128)S(1)} %collective-permute-done.refs_1_.refs_6_, f32[2,16,15360]{2,1,0:T(8,128)S(1)} %collective-permute-done.1.refs_2_.refs_7_, f32[2,16,15360]{2,1,0:T(8,128)S(1)} %collective-permute-done.2.refs_3_.refs_8_, ...), custom_call_target="tpu_custom_call" | custom-call | flops 1000000000 | bytes 1 | tf_op jit(solution)/shard_map/cross/pallas_call | solution.py:54
  106.3 2.5 %collective-permute-start.13 = (f32[128,128]{1,0:T(8,128)S(1)}, f32[128,128]{1,0:T(8,128)S(1)}, u32[]{:S(2)}, u32[]{:S(2)}) collective-permute-start(f32[128,128]{1,0:T(8,128)S(1)} %cross.1), channel_id=1, source_target_pairs={{0,24},{8,16},{16,8},{24,0},{1,25},{9,17},{17,9},{25,1},{2,26},{10... | collective-permute-start | bytes 196616 | tf_op jit(solution)/shard_map/ppermute | solution.py:239
  108.8 0.5 collective-permute-start.12
  109.3 0.5 collective-permute-start.11
  109.9 1.7 collective-permute-done.13
  111.6 1.5 collective-permute-done.12
  113.1 0.5 collective-permute-done.11
  113.6 0.0 copy-start.14
  113.6 1.4 collective-permute-start.14
  115.1 6.0 %project.5.refs_4_ = f32[64,192]{1,0:T(8,128)S(1)} custom-call(f32[192,15360]{1,0:T(8,128)S(1)} %bitcast.2, f32[2,16,15360]{2,1,0:T(8,128)S(1)} %join.3.refs_4_.refs_0_.refs_9_, f32[2,16,15360]{2,1,0:T(8,128)S(1)} %collective-permute-done.9.refs_5_.refs_1_.refs_10_), custom_call_target="tpu_custom_call" | custom-call | flops 1000000000 | bytes 1 | tf_op jit(solution)/shard_map/project/pallas_call | solution.py:54
  121.1 1.6 collective-permute-start.17
  122.7 0.7 collective-permute-start.16
  123.4 1.3 collective-permute-start.15
  124.7 1.9 %collective-permute-done.17.refs_7_ = f32[64,192]{1,0:T(8,128)S(1)} collective-permute-done((f32[64,192]{1,0:T(8,128)S(1)}, f32[64,192]{1,0:T(8,128)S(1)}, u32[]{:S(2)}, u32[]{:S(2)}) %collective-permute-start.17) | collective-permute-done | bytes 49184 | tf_op jit(solution)/shard_map/ppermute | solution.py:239
  126.6 0.7 collective-permute-done.16.refs_6_
  127.3 0.4 collective-permute-done.15.refs_5_
  127.7 12.3 %collective-permute-done.14.given_ref = f32[128,128]{1,0:T(8,128)S(1)} collective-permute-done((f32[128,128]{1,0:T(8,128)S(1)}, f32[128,128]{1,0:T(8,128)S(1)}, u32[]{:S(2)}, u32[]{:S(2)}) %collective-permute-start.14) | collective-permute-done | bytes 65568 | tf_op jit(solution)/shard_map/ppermute | solution.py:253
  140.0 0.7 prepare.1
  140.6 0.0 copy-start.10
  140.7 1.5 copy-done.10
  142.2 3.1 %join.4.refs_0_.refs_11_ = f32[2,16,12800]{2,1,0:T(8,128)S(1)} custom-call(f32[2,16,12800]{2,1,0:T(8,128)} %collective-permute-done.18.a_ref, f32[2,16,15360]{2,1,0:T(8,128)S(1)} %copy-done.10, f32[192,192]{1,0:T(8,128)S(1)} %get-tuple-element.7.refs_0_.known_ref), custom_call_target="tpu_custom_call" | custom-call | flops 1000000 | bytes 1 | tf_op jit(solution)/shard_map/join/pallas_call | solution.py:54
  145.3 0.1 collective-permute-start.19
  145.4 1.0 slice.9
  146.4 1.3 collective-permute-start.20
  147.7 1.2 collective-permute-done.19.refs_1_.refs_12_
  148.9 4.3 %copy-done.1 = f32[192,15360]{1,0:T(8,128)S(1)} copy-done((f32[192,15360]{1,0:T(8,128)S(1)}, f32[192,15360]{1,0:T(8,128)}, u32[]{:S(2)}) %copy-start.1) | copy-done | bytes 11796504
  153.3 5.0 %project.6.refs_0_ = f32[64,192]{1,0:T(8,128)S(1)} custom-call(f32[192,15360]{1,0:T(8,128)S(1)} %copy-done.1, f32[2,16,12800]{2,1,0:T(8,128)S(1)} %join.4.refs_0_.refs_11_, f32[2,16,12800]{2,1,0:T(8,128)S(1)} %collective-permute-done.19.refs_1_.refs_12_), custom_call_target="tpu_custom_call" | custom-call | flops 1000000000 | bytes 1 | tf_op jit(solution)/shard_map/project/pallas_call | solution.py:54
  158.3 0.1 collective-permute-done.20.a_ref
  158.5 0.1 collective-permute-start.21
  158.6 1.6 collective-permute-done.21.refs_2_.refs_14_
  160.2 0.9 project.7.refs_0_
  161.0 2.5 %collective-permute-start.24 = (f32[64,192]{1,0:T(8,128)S(1)}, f32[64,192]{1,0:T(8,128)S(1)}, u32[]{:S(2)}, u32[]{:S(2)}) collective-permute-start(f32[64,192]{1,0:T(8,128)S(1)} %project.7.refs_0_), channel_id=1, source_target_pairs={{0,24},{8,16},{16,8},{24,0},{1,25},{9,17},{17,9},{25,1},{2,26},{10... | collective-permute-start | bytes 147464 | tf_op jit(solution)/shard_map/ppermute | solution.py:239
  163.6 0.5 collective-permute-start.23
  164.1 0.5 collective-permute-start.22
  164.6 1.7 collective-permute-done.24.refs_3_
  166.3 1.5 collective-permute-done.23.refs_2_
  167.8 0.5 collective-permute-done.22.refs_1_
  168.3 15.4 %update.1 = f32[192,15360]{1,0:T(8,128)} custom-call(f32[192,192]{1,0:T(8,128)S(1)} %get-tuple-element.7.refs_0_.known_ref, f32[3,128,128]{2,1,0:T(8,128)S(1)} %get-tuple-element.8.mats_ref, f32[64,192]{1,0:T(8,128)S(1)} %project.7.refs_0_, f32[64,192]{1,0:T(8,128)S(1)} %collective-permute-done.22.refs_1_, f32[64,192]{1,0:T(8,128)S(1)} %collective-permute-done.23.refs_2_, ...), custom_call_target="tpu_custom_call" | custom-call | flops 1000000000 | bytes 1 | tf_op jit(solution)/shard_map/update/pallas_call | solution.py:54
  (36 shorter events, 0.1 us)
Async XLA Ops:
  0.0 46.1 %collective-permute-start.1 = (f32[2,16,15360]{2,1,0:T(8,128)}, f32[2,16,15360]{2,1,0:T(8,128)S(1)}, u32[]{:S(2)}, u32[]{:S(2)}) collective-permute-start(f32[2,16,15360]{2,1,0:T(8,128)} %refs_5_.1), channel_id=1, source_target_pairs={{0,2},{1,3},{2,0},{3,1},{4,6},{5,7},{6,4},{7,5},{8,10},{9,11},{10,... | collective-permute-start | bytes 5898248 | tf_op jit(solution)/shard_map/ppermute | solution.py:253
  3.0 43.0 %collective-permute-start.3 = (f32[2,16,15360]{2,1,0:T(8,128)}, f32[2,16,15360]{2,1,0:T(8,128)S(1)}, u32[]{:S(2)}, u32[]{:S(2)}) collective-permute-start(f32[2,16,15360]{2,1,0:T(8,128)} %refs_5_.1), channel_id=1, source_target_pairs={{2,4},{3,5},{4,2},{5,3},{10,12},{11,13},{12,10},{13,11},{18,20},{1... | collective-permute-start | bytes 5898248 | tf_op jit(solution)/shard_map/ppermute | solution.py:253
  3.8 44.4 %collective-permute-start = (f32[2,16,15360]{2,1,0:T(8,128)}, f32[2,16,15360]{2,1,0:T(8,128)S(1)}, u32[]{:S(2)}, u32[]{:S(2)}) collective-permute-start(f32[2,16,15360]{2,1,0:T(8,128)} %refs_5_.1), channel_id=1, source_target_pairs={{0,1},{1,0},{2,3},{3,2},{4,5},{5,4},{6,7},{7,6},{8,9},{9,8},{10,11... | collective-permute-start | bytes 5898248 | tf_op jit(solution)/shard_map/ppermute | solution.py:253
  46.1 54.8 %copy-start.6 = (f32[2,16,15360]{2,1,0:T(8,128)}, f32[2,16,15360]{2,1,0:T(8,128)S(1)}, u32[]{:S(2)}) copy-start(f32[2,16,15360]{2,1,0:T(8,128)S(1)} %collective-permute-done.1.refs_2_.refs_7_) | copy-start | bytes 5898244
  46.1 4.0 %collective-permute-start.2 = (f32[2,16,15360]{2,1,0:T(8,128)S(1)}, f32[2,16,15360]{2,1,0:T(8,128)S(1)}, u32[]{:S(2)}, u32[]{:S(2)}) collective-permute-start(f32[2,16,15360]{2,1,0:T(8,128)S(1)} %collective-permute-done.1.refs_2_.refs_7_), channel_id=1, source_target_pairs={{0,1},{1,0},{2,3},{3,2},{4,5},{5,4},{6,7},{7,6},{8,9},{9,8},{10,11... | collective-permute-start | bytes 5898248 | tf_op jit(solution)/shard_map/ppermute | solution.py:253
  46.1 54.8 %copy-start.9 = (f32[2,16,15360]{2,1,0:T(8,128)}, f32[2,16,15360]{2,1,0:T(8,128)S(1)}, u32[]{:S(2)}) copy-start(f32[2,16,15360]{2,1,0:T(8,128)S(1)} %collective-permute-done.3.refs_6_.b_ref) | copy-start | bytes 5898244
  46.1 48.0 %collective-permute-start.4 = (f32[2,16,15360]{2,1,0:T(8,128)S(1)}, f32[2,16,15360]{2,1,0:T(8,128)S(1)}, u32[]{:S(2)}, u32[]{:S(2)}) collective-permute-start(f32[2,16,15360]{2,1,0:T(8,128)S(1)} %collective-permute-done.3.refs_6_.b_ref), channel_id=1, source_target_pairs={{2,0},{3,1},{4,6},{5,7},{10,8},{11,9},{12,14},{13,15},{18,16},{19,... | collective-permute-start | bytes 5898248 | tf_op jit(solution)/shard_map/ppermute | solution.py:253
  47.4 46.7 %collective-permute-start.5 = (f32[2,16,15360]{2,1,0:T(8,128)S(1)}, f32[2,16,15360]{2,1,0:T(8,128)S(1)}, u32[]{:S(2)}, u32[]{:S(2)}) collective-permute-start(f32[2,16,15360]{2,1,0:T(8,128)S(1)} %collective-permute-done.1.refs_2_.refs_7_), channel_id=1, source_target_pairs={{2,4},{3,5},{4,2},{5,3},{10,12},{11,13},{12,10},{13,11},{18,20},{1... | collective-permute-start | bytes 5898248 | tf_op jit(solution)/shard_map/ppermute | solution.py:253
  48.2 52.6 %copy-start.7 = (f32[2,16,15360]{2,1,0:T(8,128)}, f32[2,16,15360]{2,1,0:T(8,128)S(1)}, u32[]{:S(2)}) copy-start(f32[2,16,15360]{2,1,0:T(8,128)S(1)} %collective-permute-done.refs_1_.refs_6_) | copy-start | bytes 5898244
  50.0 4.4 %copy-start = (f32[192,15360]{1,0:T(8,128)S(1)}, f32[192,15360]{1,0:T(8,128)}, u32[]{:S(2)}) copy-start(f32[192,15360]{1,0:T(8,128)} %refs_4_.1) | copy-start | bytes 35389444
  54.4 1.5 copy-start.4
  55.9 44.9 %copy-start.8 = (f32[2,16,15360]{2,1,0:T(8,128)}, f32[2,16,15360]{2,1,0:T(8,128)S(1)}, u32[]{:S(2)}) copy-start(f32[2,16,15360]{2,1,0:T(8,128)S(1)} %collective-permute-done.2.refs_3_.refs_8_) | copy-start | bytes 5898244
  62.4 31.6 %collective-permute-start.8 = (f32[128,192]{1,0:T(8,128)S(1)}, f32[128,192]{1,0:T(8,128)S(1)}, u32[]{:S(2)}, u32[]{:S(2)}) collective-permute-start(f32[128,192]{1,0:T(8,128)S(1)} %project.4.refs_0_), channel_id=1, source_target_pairs={{0,24},{8,16},{16,8},{24,0},{1,25},{9,17},{17,9},{25,1},{2,26},{10... | collective-permute-start | bytes 294920 | tf_op jit(solution)/shard_map/ppermute | solution.py:239
  65.1 28.9 %collective-permute-start.7 = (f32[128,192]{1,0:T(8,128)S(1)}, f32[128,192]{1,0:T(8,128)S(1)}, u32[]{:S(2)}, u32[]{:S(2)}) collective-permute-start(f32[128,192]{1,0:T(8,128)S(1)} %project.4.refs_0_), channel_id=1, source_target_pairs={{0,16},{8,24},{16,0},{24,8},{1,17},{9,25},{17,1},{25,9},{2,18},{10... | collective-permute-start | bytes 294920 | tf_op jit(solution)/shard_map/ppermute | solution.py:239
  65.6 28.4 %collective-permute-start.6 = (f32[128,192]{1,0:T(8,128)S(1)}, f32[128,192]{1,0:T(8,128)S(1)}, u32[]{:S(2)}, u32[]{:S(2)}) collective-permute-start(f32[128,192]{1,0:T(8,128)S(1)} %project.4.refs_0_), channel_id=1, source_target_pairs={{0,8},{8,0},{16,24},{24,16},{1,9},{9,1},{17,25},{25,17},{2,10},{10... | collective-permute-start | bytes 294920 | tf_op jit(solution)/shard_map/ppermute | solution.py:239
  94.0 4.3 %collective-permute-start.10 = (f32[2,16,15360]{2,1,0:T(8,128)S(1)}, f32[2,16,15360]{2,1,0:T(8,128)S(1)}, u32[]{:S(2)}, u32[]{:S(2)}) collective-permute-start(f32[2,16,15360]{2,1,0:T(8,128)S(1)} %collective-permute-done.3.refs_6_.b_ref), channel_id=1, source_target_pairs={{0,1},{1,0},{2,3},{3,2},{4,5},{5,4},{6,7},{7,6},{8,9},{9,8},{10,11... | collective-permute-start | bytes 5898248 | tf_op jit(solution)/shard_map/ppermute | solution.py:253
  94.0 1.4 copy-start.13
  94.1 6.8 %copy-start.5 = (f32[2,16,15360]{2,1,0:T(8,128)S(1)}, f32[2,16,15360]{2,1,0:T(8,128)}, u32[]{:S(2)}) copy-start(f32[2,16,15360]{2,1,0:T(8,128)} %refs_5_.1) | copy-start | bytes 5898244
  94.1 21.0 %slice-start = ((s8[11796480]{0:T(1024)(128)(4,1)}), s8[4194304]{0:T(1024)(128)(4,1)S(1)}, s32[]{:S(2)}) async-start(s8[11796480]{0:T(1024)(128)(4,1)} %bitcast.1), calls=%async_computation | async-start | bytes 8388608
  94.9 20.2 %copy-start.3 = (f32[2,16,15360]{2,1,0:T(8,128)}, f32[2,16,15360]{2,1,0:T(8,128)S(1)}, u32[]{:S(2)}) copy-start(f32[2,16,15360]{2,1,0:T(8,128)S(1)} %join.3.refs_4_.refs_0_.refs_9_) | copy-start | bytes 5898244
  94.9 20.2 %slice-start.1 = ((s8[11796480]{0:T(1024)(128)(4,1)}), s8[4194304]{0:T(1024)(128)(4,1)S(1)}, s32[]{:S(2)}) async-start(s8[11796480]{0:T(1024)(128)(4,1)} %bitcast.1), calls=%async_computation.1 | async-start | bytes 8388608
  94.9 5.9 %collective-permute-start.9 = (f32[2,16,15360]{2,1,0:T(8,128)S(1)}, f32[2,16,15360]{2,1,0:T(8,128)S(1)}, u32[]{:S(2)}, u32[]{:S(2)}) collective-permute-start(f32[2,16,15360]{2,1,0:T(8,128)S(1)} %join.3.refs_4_.refs_0_.refs_9_), channel_id=1, source_target_pairs={{0,1},{1,0},{2,3},{3,2},{4,5},{5,4},{6,7},{7,6},{8,9},{9,8},{10,11... | collective-permute-start | bytes 5898248 | tf_op jit(solution)/shard_map/ppermute | solution.py:253
  96.8 18.3 %slice-start.2 = ((s8[11796480]{0:T(1024)(128)(4,1)}), s8[3407872]{0:T(1024)(128)(4,1)S(1)}, s32[]{:S(2)}) async-start(s8[11796480]{0:T(1024)(128)(4,1)} %bitcast.1), calls=%async_computation.2 | async-start | bytes 6815744
  96.8 43.8 %collective-permute-start.18 = (f32[2,16,12800]{2,1,0:T(8,128)}, f32[2,16,12800]{2,1,0:T(8,128)}, u32[]{:S(2)}, u32[]{:S(2)}) collective-permute-start(f32[2,16,12800]{2,1,0:T(8,128)} %slice.8), channel_id=1, source_target_pairs={{2,0},{3,1},{4,6},{5,7},{10,8},{11,9},{12,14},{13,15},{18,16},{19,... | collective-permute-start | bytes 4915208 | tf_op jit(solution)/shard_map/ppermute | solution.py:253
  100.8 14.2 %copy-start.12 = (f32[2,16,15360]{2,1,0:T(8,128)}, f32[2,16,15360]{2,1,0:T(8,128)S(1)}, u32[]{:S(2)}) copy-start(f32[2,16,15360]{2,1,0:T(8,128)S(1)} %collective-permute-done.9.refs_5_.refs_1_.refs_10_) | copy-start | bytes 5898244
  106.3 5.3 %collective-permute-start.13 = (f32[128,128]{1,0:T(8,128)S(1)}, f32[128,128]{1,0:T(8,128)S(1)}, u32[]{:S(2)}, u32[]{:S(2)}) collective-permute-start(f32[128,128]{1,0:T(8,128)S(1)} %cross.1), channel_id=1, source_target_pairs={{0,24},{8,16},{16,8},{24,0},{1,25},{9,17},{17,9},{25,1},{2,26},{10... | collective-permute-start | bytes 196616 | tf_op jit(solution)/shard_map/ppermute | solution.py:239
  108.8 4.3 %collective-permute-start.12 = (f32[128,128]{1,0:T(8,128)S(1)}, f32[128,128]{1,0:T(8,128)S(1)}, u32[]{:S(2)}, u32[]{:S(2)}) collective-permute-start(f32[128,128]{1,0:T(8,128)S(1)} %cross.1), channel_id=1, source_target_pairs={{0,16},{8,24},{16,0},{24,8},{1,17},{9,25},{17,1},{25,9},{2,18},{10... | collective-permute-start | bytes 196616 | tf_op jit(solution)/shard_map/ppermute | solution.py:239
  109.3 4.3 %collective-permute-start.11 = (f32[128,128]{1,0:T(8,128)S(1)}, f32[128,128]{1,0:T(8,128)S(1)}, u32[]{:S(2)}, u32[]{:S(2)}) collective-permute-start(f32[128,128]{1,0:T(8,128)S(1)} %cross.1), channel_id=1, source_target_pairs={{0,8},{8,0},{16,24},{24,16},{1,9},{9,1},{17,25},{25,17},{2,10},{10... | collective-permute-start | bytes 196616 | tf_op jit(solution)/shard_map/ppermute | solution.py:239
  113.6 26.3 %copy-start.14 = (f32[2,128,128]{2,1,0:T(8,128)S(1)}, f32[2,128,128]{2,1,0:T(8,128)}, u32[]{:S(2)}) copy-start(f32[2,128,128]{2,1,0:T(8,128)} %factors_ref.1) | copy-start | bytes 393220
  113.6 26.3 %collective-permute-start.14 = (f32[128,128]{1,0:T(8,128)S(1)}, f32[128,128]{1,0:T(8,128)S(1)}, u32[]{:S(2)}, u32[]{:S(2)}) collective-permute-start(f32[128,128]{1,0:T(8,128)S(1)} %add_add_fusion.gram_ref), channel_id=1, source_target_pairs={{2,0},{3,1},{4,6},{5,7},{10,8},{11,9},{12,14},{13,15},{18,16},{19,... | collective-permute-start | bytes 196616 | tf_op jit(solution)/shard_map/ppermute | solution.py:253
  121.1 5.5 %collective-permute-start.17 = (f32[64,192]{1,0:T(8,128)S(1)}, f32[64,192]{1,0:T(8,128)S(1)}, u32[]{:S(2)}, u32[]{:S(2)}) collective-permute-start(f32[64,192]{1,0:T(8,128)S(1)} %project.5.refs_4_), channel_id=1, source_target_pairs={{0,24},{8,16},{16,8},{24,0},{1,25},{9,17},{17,9},{25,1},{2,26},{10... | collective-permute-start | bytes 147464 | tf_op jit(solution)/shard_map/ppermute | solution.py:239
  122.7 4.6 %collective-permute-start.16 = (f32[64,192]{1,0:T(8,128)S(1)}, f32[64,192]{1,0:T(8,128)S(1)}, u32[]{:S(2)}, u32[]{:S(2)}) collective-permute-start(f32[64,192]{1,0:T(8,128)S(1)} %project.5.refs_4_), channel_id=1, source_target_pairs={{0,16},{8,24},{16,0},{24,8},{1,17},{9,25},{17,1},{25,9},{2,18},{10... | collective-permute-start | bytes 147464 | tf_op jit(solution)/shard_map/ppermute | solution.py:239
  123.4 4.3 %collective-permute-start.15 = (f32[64,192]{1,0:T(8,128)S(1)}, f32[64,192]{1,0:T(8,128)S(1)}, u32[]{:S(2)}, u32[]{:S(2)}) collective-permute-start(f32[64,192]{1,0:T(8,128)S(1)} %project.5.refs_4_), channel_id=1, source_target_pairs={{0,8},{8,0},{16,24},{24,16},{1,9},{9,1},{17,25},{25,17},{2,10},{10... | collective-permute-start | bytes 147464 | tf_op jit(solution)/shard_map/ppermute | solution.py:239
  140.6 1.5 copy-start.10
  145.3 3.6 %collective-permute-start.19 = (f32[2,16,12800]{2,1,0:T(8,128)S(1)}, f32[2,16,12800]{2,1,0:T(8,128)S(1)}, u32[]{:S(2)}, u32[]{:S(2)}) collective-permute-start(f32[2,16,12800]{2,1,0:T(8,128)S(1)} %join.4.refs_0_.refs_11_), channel_id=1, source_target_pairs={{0,1},{1,0},{2,3},{3,2},{4,5},{5,4},{6,7},{7,6},{8,9},{9,8},{10,11... | collective-permute-start | bytes 4915208 | tf_op jit(solution)/shard_map/ppermute | solution.py:253
  146.4 12.0 %collective-permute-start.20 = (f32[2,16,2560]{2,1,0:T(8,128)S(1)}, f32[2,16,2560]{2,1,0:T(8,128)S(1)}, u32[]{:S(2)}, u32[]{:S(2)}) collective-permute-start(f32[2,16,2560]{2,1,0:T(8,128)S(1)} %slice.9), channel_id=1, source_target_pairs={{2,0},{3,1},{4,6},{5,7},{10,8},{11,9},{12,14},{13,15},{18,16},{19,... | collective-permute-start | bytes 983048 | tf_op jit(solution)/shard_map/ppermute | solution.py:253
  148.9 4.4 %copy-start.1 = (f32[192,15360]{1,0:T(8,128)S(1)}, f32[192,15360]{1,0:T(8,128)}, u32[]{:S(2)}) copy-start(f32[192,15360]{1,0:T(8,128)} %refs_4_.1) | copy-start | bytes 35389444
  153.3 5.2 %copy-start.11 = (f32[2,16,15360]{2,1,0:T(8,128)S(1)}, f32[2,16,15360]{2,1,0:T(8,128)}, u32[]{:S(2)}) copy-start(f32[2,16,15360]{2,1,0:T(8,128)} %copy-done.9) | copy-start | bytes 5898244
  153.3 6.9 %copy-start.2 = (f32[192,15360]{1,0:T(8,128)S(1)}, f32[192,15360]{1,0:T(8,128)}, u32[]{:S(2)}) copy-start(f32[192,15360]{1,0:T(8,128)} %refs_4_.1) | copy-start | bytes 35389444
  158.5 1.7 collective-permute-start.21
  161.0 5.3 %collective-permute-start.24 = (f32[64,192]{1,0:T(8,128)S(1)}, f32[64,192]{1,0:T(8,128)S(1)}, u32[]{:S(2)}, u32[]{:S(2)}) collective-permute-start(f32[64,192]{1,0:T(8,128)S(1)} %project.7.refs_0_), channel_id=1, source_target_pairs={{0,24},{8,16},{16,8},{24,0},{1,25},{9,17},{17,9},{25,1},{2,26},{10... | collective-permute-start | bytes 147464 | tf_op jit(solution)/shard_map/ppermute | solution.py:239
  163.6 4.3 %collective-permute-start.23 = (f32[64,192]{1,0:T(8,128)S(1)}, f32[64,192]{1,0:T(8,128)S(1)}, u32[]{:S(2)}, u32[]{:S(2)}) collective-permute-start(f32[64,192]{1,0:T(8,128)S(1)} %project.7.refs_0_), channel_id=1, source_target_pairs={{0,16},{8,24},{16,0},{24,8},{1,17},{9,25},{17,1},{25,9},{2,18},{10... | collective-permute-start | bytes 147464 | tf_op jit(solution)/shard_map/ppermute | solution.py:239
  164.1 4.3 %collective-permute-start.22 = (f32[64,192]{1,0:T(8,128)S(1)}, f32[64,192]{1,0:T(8,128)S(1)}, u32[]{:S(2)}, u32[]{:S(2)}) collective-permute-start(f32[64,192]{1,0:T(8,128)S(1)} %project.7.refs_0_), channel_id=1, source_target_pairs={{0,8},{8,0},{16,24},{24,16},{1,9},{9,1},{17,25},{25,17},{2,10},{10... | collective-permute-start | bytes 147464 | tf_op jit(solution)/shard_map/ppermute | solution.py:239

commit v3 on v2

v3 whole, which is shorter than its diff:
```python
import functools

import jax
import jax.numpy as jnp
from jax import lax
from jax.experimental import pallas as pl
from jax.experimental.pallas import tpu as pltpu
from jax.sharding import PartitionSpec as P

F32 = jnp.float32
BF16 = jnp.bfloat16
NT = (((1,), (1,)), ((), ()))
NN = (((1,), (0,)), ((), ()))
MIB = 1024 * 1024
TILE = 2560
WIDTHS = (4, 2)
COST = dict(settle=10**6, hold=10**9, join=10**6, take=10**6, project=10**9, cross=10**9, weigh=10**6, apply=10**9, finish=10**9)
FINISH = 16
MADE = jax.ShapeDtypeStruct


def split(x):
    high = x.astype(BF16)
    return high, (x - high.astype(F32)).astype(BF16)


def wide3(left, right):
    (lh, ll), (rh, rl) = left, right
    dot = functools.partial(lax.dot_general, dimension_numbers=NT, preferred_element_type=F32)
    n = rh.shape[0]
    both = dot(lh, jnp.concatenate([rh, rl], axis=0))
    return both[:, :n] + (both[:, n:] + dot(ll, rh))


def exact(left, right, dims=NN):
    return lax.dot_general(left, right, dims, precision=lax.Precision.HIGHEST, preferred_element_type=F32)


def block_rows(refs):
    return jnp.concatenate([r[b] for b in (0, 1) for r in refs], axis=0)


def total(refs):
    a, b, c, d = (r[...] for r in refs)
    return (a + b) + (c + d)


def whole(x):
    return pl.BlockSpec(x.shape, lambda g: (0,) * x.ndim)


def columns(x, at=0):
    lead = x.shape[:-1]
    return pl.BlockSpec(lead + (TILE,), lambda g: (0,) * len(lead) + (at // TILE + g,))


HELD = pl.BlockSpec(memory_space=pltpu.VMEM)


def held(x):
    return pltpu.with_memory_space_constraint(x, pltpu.VMEM)


def tile_of(ref):
    return ref[:, pl.ds(pl.multiple_of(pl.program_id(0) * TILE, TILE), TILE)]


def call(kernel, steps, operands, specs, outs, out_specs, name, scratch=(), vmem=16):
    return pl.pallas_call(
        kernel,
        out_shape=outs,
        grid=(steps,),
        in_specs=specs,
        out_specs=out_specs,
        scratch_shapes=list(scratch),
        compiler_params=pltpu.CompilerParams(vmem_limit_bytes=vmem * MIB),
        cost_estimate=pl.CostEstimate(flops=COST[name], bytes_accessed=1, transcendentals=0),
        name=name,
    )(*operands)


def still(x):
    return pltpu.with_memory_space_constraint(x, pltpu.HBM)


def corner(x):
    lead = x.ndim - 2
    return pl.BlockSpec((1,) * lead + (8, 128), lambda g: (0,) * x.ndim)


def join_kernel(count, a_ref, b_ref, *refs):
    out_ref, cut_ref = refs[-2:]
    out_ref[...] = a_ref[...] + b_ref[...]

    @pl.when(pl.program_id(0) < count)
    def _():
        cut_ref[...] = out_ref[...]


def join(a, b, count, *after):
    out, cut = MADE(a.shape, F32), MADE((*a.shape[:-1], count * TILE), F32)
    return call(
        functools.partial(join_kernel, count),
        a.shape[-1] // TILE,
        [a, b, *after],
        [columns(a), columns(b)] + [corner(y) for y in after],
        [out, cut],
        [columns(out), pl.BlockSpec((*a.shape[:-1], TILE), lambda g: (0, 0, jnp.minimum(g, count - 1)))],
        "join",
    )


def hold_kernel(x_ref, out_ref):
    out_ref[...] = x_ref[...]


def hold(x):
    out = pltpu.VMEM(x.shape, F32)
    return call(hold_kernel, x.shape[-1] // TILE, [still(x)], [columns(x)], out, columns(x), "hold")


def settle_kernel(*refs):
    refs[-1][...] = total(refs[:-1])


def settle(*parts):
    return call(settle_kernel, 1, parts, [whole(x) for x in parts], MADE(parts[0].shape, F32), whole(parts[0]), "settle")


def settle_both_kernel(a_ref, b_ref, c_ref, d_ref, gram_ref, proj_ref):
    n, rows = gram_ref.shape[0], proj_ref.shape[0]
    both = total([a_ref, b_ref, c_ref, d_ref])
    gram_ref[...] = both[:, :n]
    proj_ref[...] = jnp.concatenate([both[:rows, n:], both[rows:, n:]], axis=1)


def settle_both(parts, rows, nev):
    n = parts[0].shape[0]
    outs = [MADE((n, n), F32), MADE((rows, nev), F32)]
    return call(settle_both_kernel, 1, parts, [whole(x) for x in parts], outs, [whole(x) for x in outs], "settle")


def take_kernel(x_ref, *refs):
    refs[-1][...] = x_ref[...]


def take(x, at, width, *after):
    out = jax.ShapeDtypeStruct((*x.shape[:-1], width), F32)
    return call(
        take_kernel, width // TILE, [x, *after], [columns(x, at)] + [corner(y) for y in after], out, columns(out), "take"
    )


def project_kernel(steps, lies, started, slab_ref, *refs):
    before, refs = (refs[0], refs[1:]) if started else (None, refs)
    *pieces, proj_ref, acc_ref = refs
    step = pl.program_id(0)

    @pl.when(step == 0)
    def _():
        acc_ref[...] = jnp.zeros_like(acc_ref)

    acc_ref[...] += wide3(split(tile_of(slab_ref) if lies else slab_ref[...]), split(block_rows(pieces)))

    @pl.when(step == steps - 1)
    def _():
        made = acc_ref[...].T
        proj_ref[...] = made + before[...] if started else made


def project(slab, pieces, at=0, before=None, lies=False):
    nev = slab.shape[0]
    mine, width = pieces[0].shape[1:]
    steps = width // TILE
    rows = 2 * mine * len(pieces)
    out = jax.ShapeDtypeStruct((rows, nev), F32)
    small = [] if before is None else [before]
    return call(
        functools.partial(project_kernel, steps, lies, bool(small)),
        steps,
        [held(slab) if lies else still(slab), *small, *pieces],
        [HELD if lies else columns(slab, at)] + [whole(x) for x in small] + [columns(p) for p in pieces],
        out,
        whole(out),
        "project",
        [pltpu.VMEM((nev, rows), F32)],
    )


def cross_kernel(steps, first, count, slab_ref, *refs):
    *pieces, both_ref, gram_ref, acc_ref = refs
    step = pl.program_id(0)

    @pl.when(step == 0)
    def _():
        gram_ref[...] = jnp.zeros_like(gram_ref)
        acc_ref[...] = jnp.zeros_like(acc_ref)

    high, low = split(block_rows(pieces))
    half = high.shape[0] // 2
    gram_ref[...] += wide3((high[half:], low[half:]), (high[:half], low[:half]))
    mine = half // len(pieces)
    pick = lambda x: jnp.concatenate([x[b * half + first * mine :][: count * mine] for b in (0, 1)], axis=0)
    acc_ref[...] += wide3(split(tile_of(slab_ref)), (pick(high), pick(low)))

    @pl.when(step == steps - 1)
    def _():
        made = acc_ref[...].T
        middle = made.shape[1] // 2
        beside = jnp.concatenate([made[:, :middle], made[:, middle:]], axis=0)
        both_ref[...] = jnp.concatenate([gram_ref[...], beside], axis=1)


def cross(slab, pieces, first, count):
    nev, width = slab.shape
    mine = pieces[0].shape[1]
    n, rows = mine * len(pieces), 2 * mine * count
    out = MADE((n, n + nev // 2), F32)
    return call(
        functools.partial(cross_kernel, width // TILE, first, count),
        width // TILE,
        [held(slab), *pieces],
        [HELD] + [columns(p) for p in pieces],
        out,
        whole(out),
        "cross",
        [pltpu.VMEM((n, n), F32), pltpu.VMEM((nev, rows), F32)],
        vmem=24,
    )


def swap_matrix(n, mask):
    row = lax.broadcasted_iota(jnp.int32, (n, n), 0)
    column = lax.broadcasted_iota(jnp.int32, (n, n), 1)
    return jnp.where(column == jnp.bitwise_xor(row, mask), 1.0, 0.0).astype(F32)


def weigh_kernel(mine, col_ref, factors_ref, gram_ref, given_ref, *refs):
    *sums, high_ref, low_ref, rest_ref = refs
    n = factors_ref.shape[1]
    row = lax.broadcasted_iota(jnp.int32, (n, n), 0)
    column = lax.broadcasted_iota(jnp.int32, (n, n), 1)
    swap = swap_matrix(n, col_ref[0] * mine)
    one, two = (exact(swap, exact(jnp.where(row <= column, factors_ref[b], 0.0), swap)) for b in (0, 1))
    turn = swap_matrix(n, 2 * mine)
    middle = jnp.logical_and(col_ref[0] >= 2, col_ref[0] < 6)
    gram = jnp.where(middle, gram_ref[...], exact(turn, exact(given_ref[...], turn)))
    parts = [x[...] for x in sums]
    known = [jnp.concatenate([x[b * x.shape[0] // 2 :][: x.shape[0] // 2] for x in parts], axis=0) for b in (0, 1)]
    kept = known[0].shape[0]
    none = jnp.zeros((n, n - kept), F32)
    first = jnp.concatenate([exact(one[:, :kept], known[0]), one[:, kept:], none], axis=1)
    second = jnp.concatenate([exact(two[:, :kept], known[1]), none, two[:, kept:]], axis=1)
    second = second - exact(two, exact(gram, first))
    high_ref[...], low_ref[...] = split(jnp.concatenate([first[:kept], second[:kept]], axis=0).T)
    rest_ref[...] = jnp.concatenate([first[kept:], second[kept:]], axis=0)


def weigh(col, factors, gram, given, known0, known1, mine):
    n, nev = 2 * gram.shape[0], known0.shape[1]
    kept = known0.shape[0] + known1.shape[0]
    small = [factors, gram, given, known0, known1]
    outs = [jax.ShapeDtypeStruct((nev + n - kept, kept), BF16)] * 2 + [jax.ShapeDtypeStruct((n - kept, nev + n - kept), F32)]
    return call(
        functools.partial(weigh_kernel, mine),
        1,
        [col[None], *small],
        [pl.BlockSpec(memory_space=pltpu.SMEM)] + [whole(x) for x in small],
        outs,
        [whole(x) for x in outs],
        "weigh",
    )


def apply_kernel(nev, steps, count, high_ref, low_ref, slab_ref, *refs):
    *pieces, a_ref, b_ref, part_ref, xh_ref, xl_ref, last_ref, acc_ref = refs
    step = pl.program_id(0)
    high, low = split(block_rows(pieces))
    left = jnp.concatenate([high_ref[...], low_ref[...], high_ref[...]], axis=1)
    made = lax.dot_general(left, jnp.concatenate([high, high, low], axis=0), NN, preferred_element_type=F32)
    part_ref[...] = slab_ref[...] - made[:nev]
    xh_ref[...], xl_ref[...] = split(made[nev:])

    @pl.when(step == 0)
    def _():
        acc_ref[...] = jnp.zeros_like(acc_ref)

    @pl.when(step < count)
    def _():
        acc_ref[...] += wide3(split(slab_ref[...]), split(block_rows([a_ref, b_ref])))

    @pl.when(step == steps - 1)
    def _():
        last_ref[...] = acc_ref[...].T


def apply(high, low, slab, pieces, late):
    nev, width = slab.shape
    rest, count = high.shape[0] - nev, late[0].shape[-1] // TILE
    outs = [pltpu.VMEM(slab.shape, F32)] + [pltpu.VMEM((rest, width), BF16)] * 2
    last = MADE((rest, nev), F32)
    steps = width // TILE
    return call(
        functools.partial(apply_kernel, nev, steps, count),
        steps,
        [high, low, still(slab), *[still(x) for x in pieces], *late],
        [whole(high), whole(low), columns(slab)]
        + [columns(x) for x in pieces]
        + [pl.BlockSpec((*x.shape[:-1], TILE), lambda g: (0, 0, jnp.minimum(g, count - 1))) for x in late],
        outs + [last],
        [columns(x) for x in outs] + [whole(last)],
        "apply",
        [pltpu.VMEM((nev, rest), F32)],
        vmem=22,
    )


def finish_kernel(starts, part_ref, xh_ref, xl_ref, rest_ref, *refs):
    lasts, (*pieces, out_ref, left_ref) = refs[:4], refs[4:]
    step = pl.program_id(0)
    nev = part_ref.shape[0]

    @pl.when(step == 0)
    def _():
        last = total(lasts)
        more = rest_ref[:, :nev] + exact(rest_ref[:, nev:], last)
        high, low = split(jnp.concatenate([last, more], axis=0).T)
        left_ref[...] = jnp.concatenate([high, low, high], axis=1)

    each = len(pieces) // (len(starts) - 1)
    for i in range(len(starts) - 1):

        @pl.when(jnp.logical_and(step >= starts[i], step < starts[i + 1]))
        def _():
            high, low = split(block_rows(pieces[each * i : each * (i + 1)]))
            high, low = jnp.concatenate([tile_of(xh_ref), high], axis=0), jnp.concatenate([tile_of(xl_ref), low], axis=0)
            right = jnp.concatenate([high, high, low], axis=0)
            out_ref[...] = tile_of(part_ref) - lax.dot_general(left_ref[...], right, NN, preferred_element_type=F32)


def finish(part, xh, xl, rest, lasts, parts):
    nev, width = part.shape
    starts, specs = [0], []
    for pieces in parts:
        first, count = starts[-1], pieces[0].shape[-1] // TILE
        starts.append(first + count)
        specs += [
            pl.BlockSpec((*x.shape[:-1], TILE), lambda g, first=first, count=count: (0, 0, jnp.clip(g - first, 0, count - 1)))
            for x in pieces
        ]
    out = jax.ShapeDtypeStruct(part.shape, F32)
    return call(
        functools.partial(finish_kernel, starts),
        width // TILE,
        [held(part), held(xh), held(xl), rest, *lasts, *[x for pieces in parts for x in pieces]],
        [HELD] * 3 + [whole(rest)] + [whole(x) for x in lasts] + specs,
        out,
        columns(out),
        "finish",
        [pltpu.VMEM((nev, 6 * rest.shape[0]), BF16)],
        vmem=FINISH,
    )


def others(x):
    return [lax.ppermute(x, "row", [(i, i ^ k) for i in range(4)]) for k in (1, 2, 3)]


def cores(pairs):
    return [(2 * a + c, 2 * b + c) for a, b in pairs for c in (0, 1)]


PAIR = cores([(0, 1), (1, 0), (2, 3), (3, 2)])
MIDDLE = cores([(1, 2), (2, 1)])
OUTWARD = cores([(1, 0), (2, 3)])
SIBLING = [(i, i ^ 1) for i in range(8)]


def along(x, pairs):
    return lax.ppermute(x, "col", pairs)


def line_of_four(slab, householder, factors):
    col = lax.axis_index("col")
    mine, width = householder.shape[1:]
    swap = lambda x: along(x, SIBLING)
    other = swap(householder)

    beside, inner = along(householder, PAIR), along(householder, MIDDLE)
    across, outer = along(beside, MIDDLE), along(inner, OUTWARD)
    inner2 = swap(inner)

    kept = hold(slab)
    near = [householder, other, beside, swap(beside)]
    p0 = project(kept, near, lies=True)
    known0 = settle(p0, *others(p0))
    stretches = [(sum(WIDTHS[:i]) * TILE, w * TILE) for i, w in enumerate(WIDTHS)]
    third, cut = join(across, outer, WIDTHS[0], known0)
    fourth = [along(cut, PAIR)]
    near += [third, swap(third)]
    both = cross(kept, near + [inner, inner2], 4, 2)
    gram, known1 = settle_both([both, *others(both)], 4 * mine, slab.shape[0])
    given = along(gram, OUTWARD)
    fourth += [along(take(third, *stretch, given), PAIR) for stretch in stretches[1:]]
    high, low, rest = weigh(col, factors, gram, given, known0, known1, mine)

    fourth[0] = take(fourth[0], 0, stretches[0][1], given)
    parts = [[fourth[0], swap(fourth[0])]]
    *parted, last = apply(high, low, slab, near, parts[0])
    for (at, w), x in zip(stretches[1:], fourth[1:]):
        x = take(x, 0, w, last)
        parts.append([x, swap(x)])
        last = project(slab, parts[-1], at, last)
    return finish(*parted, rest, [last, *others(last)], parts)


def any_mesh(slab, householder, factors):
    upper = jnp.triu(factors)
    for block in range(householder.shape[0]):
        vectors = lax.all_gather(householder[block], "col", axis=0, tiled=True)
        projection = lax.psum(exact(vectors, slab, NT), "row")
        coeffs = exact(upper[block], projection)
        slab = slab - exact(coeffs, vectors, (((0,), (0,)), ((), ())))
    return slab


def solution(mesh):
    small = mesh.shape["col"] == 8 and mesh.shape["row"] == 4
    return jax.shard_map(
        line_of_four if small else any_mesh,
        mesh=mesh,
        in_specs=(P("col", "row"), P(None, "col", "row"), P()),
        out_specs=P("col", "row"),
        check_vma=False,
    )
```

time: 184 us -> 170 us (0.924)
  local copies, waits for them, and re-layouts: 14.2 us -> 0.03 us
  Pallas kernels: 43.8 us -> 51.9 us
  waiting for transfers between devices: 100 us -> 95.2 us
  starting transfers between devices: 25.2 us -> 22.6 us
    unnamed x36 -> x14, local copies, waits for them, and re-layouts: 11.9 us -> 0.03 us
    ppermute x13, waiting for transfers between devices: 89.7 us -> 79.3 us  [along(): return lax.ppermute(x, 'col', pairs)]
    pallas_call x10 -> x13, Pallas kernels: 43.8 us -> 51.9 us  [call(): pl.pallas_call(kernel, out_shape=outs, grid=(steps,), in_specs=specs, out...]
    ppermute x12 -> x9, waiting for transfers between devices: 10.5 us -> 15.9 us  [others(): lax.ppermute(x, 'row', [(i, i ^ k) for i in range(4)])]
    ppermute x12 -> x9, starting transfers between devices: 14.2 us -> 10.7 us  [others(): lax.ppermute(x, 'row', [(i, i ^ k) for i in range(4)])]
    slice x2 -> x0, local copies, waits for them, and re-layouts: 2.34 us -> none  [line_of_four(): across[:, :, at:at + w]]
  transfers between devices with their start and end apart: 25 -> 22, of which waited for: 17 -> 16; matrix products, arithmetic and copies ran while one was open for 1% -> 0% of each run, Pallas kernels for 13% -> 23%
where the time goes in v3:
time: 170 us
  waiting for transfers between devices  95.2 us (56%)
  Pallas kernels  51.9 us (31%)
  starting transfers between devices  22.6 us (13%)
    ppermute x13, waiting for transfers between devices, along(): return lax.ppermute(x, 'col', pairs)  79.3 us
    pallas_call x13, Pallas kernels, call(): pl.pallas_call(kernel, out_shape=outs, grid=(steps,), in_specs=specs, out...  51.9 us
    ppermute x9, waiting for transfers between devices, others(): lax.ppermute(x, 'row', [(i, i ^ k) for i in range(4)])  15.9 us
    ppermute x13, starting transfers between devices, along(): return lax.ppermute(x, 'col', pairs)  11.9 us
    ppermute x9, starting transfers between devices, others(): lax.ppermute(x, 'row', [(i, i ^ k) for i in range(4)])  10.7 us
  transfers between devices with their start and end apart: 22, of which 16 were waited for; matrix products, arithmetic and copies ran while one was open for 0% of the time, Pallas kernels for 23%

profile of v3, /device:TPU:0, one launch (start us, length us, event | category | flops | bytes accessed | tf_op | source)
XLA Modules:
  0.0 170.0 jit_solution(13457781301065694695)
XLA Ops:
  0.0 3.0 %collective-permute-start.1 = (f32[2,16,15360]{2,1,0:T(8,128)}, f32[2,16,15360]{2,1,0:T(8,128)S(1)}, u32[]{:S(2)}, u32[]{:S(2)}) collective-permute-start(f32[2,16,15360]{2,1,0:T(8,128)} %refs_0_.5), channel_id=1, source_target_pairs={{0,2},{1,3},{2,0},{3,1},{4,6},{5,7},{6,4},{7,5},{8,10},{9,11},{10,... | collective-permute-start | bytes 5898248 | tf_op jit(solution)/shard_map/ppermute | solution.py:380
  3.0 0.8 collective-permute-start.4
  3.8 0.1 collective-permute-start
  3.9 42.2 %collective-permute-done.1.refs_2_ = f32[2,16,15360]{2,1,0:T(8,128)S(1)} collective-permute-done((f32[2,16,15360]{2,1,0:T(8,128)}, f32[2,16,15360]{2,1,0:T(8,128)S(1)}, u32[]{:S(2)}, u32[]{:S(2)}) %collective-permute-start.1) | collective-permute-done | bytes 1966112 | tf_op jit(solution)/shard_map/ppermute | solution.py:380
  46.1 0.0 collective-permute-start.2
  46.1 0.0 collective-permute-done.4.refs_6_
  46.1 1.3 collective-permute-start.5
  47.4 0.8 collective-permute-start.3
  48.2 6.3 %hold.1.slab_ref = f32[192,15360]{1,0:T(8,128)S(1)} custom-call(f32[192,15360]{1,0:T(8,128)} %slab_ref.3), custom_call_target="tpu_custom_call" | custom-call | flops 1000000000 | bytes 1 | tf_op jit(solution)/shard_map/hold/pallas_call | solution.py:69
  54.5 0.0 collective-permute-done.refs_1_
  54.5 0.0 copy-start.2
  54.6 0.0 collective-permute-done.2.refs_3_
  54.6 0.0 copy-done
  54.6 0.0 copy-start.3
  54.6 5.7 %project.2.refs_0_ = f32[128,192]{1,0:T(8,128)S(1)} custom-call(f32[192,15360]{1,0:T(8,128)S(1)} %hold.1.slab_ref, f32[2,16,15360]{2,1,0:T(8,128)S(1)} %copy-done, f32[2,16,15360]{2,1,0:T(8,128)S(1)} %collective-permute-done.refs_1_, f32[2,16,15360]{2,1,0:T(8,128)S(1)} %collective-permute-done.1.refs_2_, f32[2,16,15360]{2,1,0:T(8,128)S(1)} %collective-permute-done.2.refs_3_), custom_call_target="tpu_custom_call" | custom-call | flops 1000000000 | bytes 1 | tf_op jit(solution)/shard_map/project/pallas_call | solution.py:69
  60.3 2.6 %collective-permute-start.8 = (f32[128,192]{1,0:T(8,128)S(1)}, f32[128,192]{1,0:T(8,128)S(1)}, u32[]{:S(2)}, u32[]{:S(2)}) collective-permute-start(f32[128,192]{1,0:T(8,128)S(1)} %project.2.refs_0_), channel_id=1, source_target_pairs={{0,24},{8,16},{16,8},{24,0},{1,25},{9,17},{17,9},{25,1},{2,26},{10... | collective-permute-start | bytes 294920 | tf_op jit(solution)/shard_map/ppermute | solution.py:366
  62.9 0.5 collective-permute-start.7
  63.4 0.4 collective-permute-start.6
  63.9 3.5 %collective-permute-done.8.refs_3_ = f32[128,192]{1,0:T(8,128)S(1)} collective-permute-done((f32[128,192]{1,0:T(8,128)S(1)}, f32[128,192]{1,0:T(8,128)S(1)}, u32[]{:S(2)}, u32[]{:S(2)}) %collective-permute-start.8) | collective-permute-done | bytes 98336 | tf_op jit(solution)/shard_map/ppermute | solution.py:366
  67.4 0.0 collective-permute-start.10
  67.4 2.6 %collective-permute-done.7.refs_2_ = f32[128,192]{1,0:T(8,128)S(1)} collective-permute-done((f32[128,192]{1,0:T(8,128)S(1)}, f32[128,192]{1,0:T(8,128)S(1)}, u32[]{:S(2)}, u32[]{:S(2)}) %collective-permute-start.7) | collective-permute-done | bytes 98336 | tf_op jit(solution)/shard_map/ppermute | solution.py:366
  70.0 0.2 collective-permute-done.6.refs_1_
  70.2 23.8 %collective-permute-done.5.b_ref = f32[2,16,15360]{2,1,0:T(8,128)S(1)} collective-permute-done((f32[2,16,15360]{2,1,0:T(8,128)S(1)}, f32[2,16,15360]{2,1,0:T(8,128)S(1)}, u32[]{:S(2)}, u32[]{:S(2)}) %collective-permute-start.5) | collective-permute-done | bytes 1966112 | tf_op jit(solution)/shard_map/ppermute | solution.py:380
  94.0 0.0 collective-permute-done.3.a_ref
  94.0 1.0 join.1
  95.0 0.0 copy-start.4
  95.0 0.1 collective-permute-start.9
  95.1 4.1 %collective-permute-start.15 = (f32[2,16,10240]{2,1,0:T(8,128)S(1)}, f32[2,16,10240]{2,1,0:T(8,128)S(1)}, u32[]{:S(2)}, u32[]{:S(2)}) collective-permute-start(f32[2,16,10240]{2,1,0:T(8,128)S(1)} %get-tuple-element.21), channel_id=1, source_target_pairs={{0,2},{1,3},{2,0},{3,1},{4,6},{5,7},{6,4},{7,5},{8,10},{9,11},{10,... | collective-permute-start | bytes 3932168 | tf_op jit(solution)/shard_map/ppermute | solution.py:380
  99.2 0.0 collective-permute-done.10.refs_7_
  99.2 0.0 collective-permute-done.9.refs_5_
  99.2 0.0 copy-done.1
  99.2 0.0 copy-done.2
  99.2 0.0 copy-done.3
  99.3 9.6 %cross.1.a_ref = f32[128,224]{1,0:T(8,128)S(1)} custom-call(f32[192,15360]{1,0:T(8,128)S(1)} %hold.1.slab_ref, f32[2,16,15360]{2,1,0:T(8,128)S(1)} %copy-done, f32[2,16,15360]{2,1,0:T(8,128)S(1)} %collective-permute-done.refs_1_, f32[2,16,15360]{2,1,0:T(8,128)S(1)} %collective-permute-done.1.refs_2_, f32[2,16,15360]{2,1,0:T(8,128)S(1)} %collective-permute-done.2.refs_3_, ...), custom_call_target="tpu_custom_call" | custom-call | flops 1000000000 | bytes 1 | tf_op jit(solution)/shard_map/cross/pallas_call | solution.py:69
  108.8 2.5 %collective-permute-start.13 = (f32[128,224]{1,0:T(8,128)S(1)}, f32[128,224]{1,0:T(8,128)S(1)}, u32[]{:S(2)}, u32[]{:S(2)}) collective-permute-start(f32[128,224]{1,0:T(8,128)S(1)} %cross.1.a_ref), channel_id=1, source_target_pairs={{0,24},{8,16},{16,8},{24,0},{1,25},{9,17},{17,9},{25,1},{2,26},{10... | collective-permute-start | bytes 344072 | tf_op jit(solution)/shard_map/ppermute | solution.py:366
  111.4 0.5 collective-permute-start.12
  111.9 0.5 collective-permute-start.11
  112.4 3.3 %collective-permute-done.13.d_ref = f32[128,224]{1,0:T(8,128)S(1)} collective-permute-done((f32[128,224]{1,0:T(8,128)S(1)}, f32[128,224]{1,0:T(8,128)S(1)}, u32[]{:S(2)}, u32[]{:S(2)}) %collective-permute-start.13) | collective-permute-done | bytes 114720 | tf_op jit(solution)/shard_map/ppermute | solution.py:366
  115.7 2.5 %collective-permute-done.12.c_ref = f32[128,224]{1,0:T(8,128)S(1)} collective-permute-done((f32[128,224]{1,0:T(8,128)S(1)}, f32[128,224]{1,0:T(8,128)S(1)}, u32[]{:S(2)}, u32[]{:S(2)}) %collective-permute-start.12) | collective-permute-done | bytes 114720 | tf_op jit(solution)/shard_map/ppermute | solution.py:366
  118.2 0.1 collective-permute-done.11.b_ref
  118.3 0.1 settle.3
  118.4 1.3 collective-permute-start.14
  119.7 9.2 %collective-permute-done.15.x_ref = f32[2,16,10240]{2,1,0:T(8,128)S(1)} collective-permute-done((f32[2,16,10240]{2,1,0:T(8,128)S(1)}, f32[2,16,10240]{2,1,0:T(8,128)S(1)}, u32[]{:S(2)}, u32[]{:S(2)}) %collective-permute-start.15) | collective-permute-done | bytes 1310752 | tf_op jit(solution)/shard_map/ppermute | solution.py:380
  128.9 1.1 collective-permute-done.14.given_ref.refs_0_
  130.0 0.4 take.3.refs_6_.refs_4_
  130.4 0.0 copy-start.6
  130.4 0.1 collective-permute-start.16
  130.5 1.0 take.4
  131.5 0.4 collective-permute-start.17
  131.8 1.5 weigh.1
  133.3 0.1 collective-permute-done.16.refs_7_.refs_5_
  133.5 14.7 %apply.1 = (f32[192,15360]{1,0:T(8,128)S(1)}, bf16[64,15360]{1,0:T(8,128)(2,1)S(1)}, bf16[64,15360]{1,0:T(8,128)(2,1)S(1)}, f32[64,192]{1,0:T(8,128)S(1)}) custom-call(bf16[256,192]{1,0:T(8,128)(2,1)S(1)} %get-tuple-element.19.high_ref, bf16[256,192]{1,0:T(8,128)(2,1)S(1)} %get-tuple-element.20.low_ref, f32[192,15360]{1,0:T(8,128)} %slab_ref.3, ...), custom_call_target="tpu_custom_call" | custom-call | flops 1000000000 | bytes 1 | tf_op jit(solution)/shard_map/apply/pallas_call | solution.py:69
  148.2 0.7 collective-permute-done.17.x_ref
  148.9 1.1 take.5.refs_1_.refs_6_
  150.0 0.1 collective-permute-start.18
  150.1 2.1 %collective-permute-done.18.refs_2_.refs_7_ = f32[2,16,5120]{2,1,0:T(8,128)S(1)} collective-permute-done((f32[2,16,5120]{2,1,0:T(8,128)S(1)}, f32[2,16,5120]{2,1,0:T(8,128)S(1)}, u32[]{:S(2)}, u32[]{:S(2)}) %collective-permute-start.18) | collective-permute-done | bytes 655392 | tf_op jit(solution)/shard_map/ppermute | solution.py:380
  152.2 3.3 %project.3.refs_0_ = f32[64,192]{1,0:T(8,128)S(1)} custom-call(f32[192,15360]{1,0:T(8,128)} %slab_ref.3, f32[64,192]{1,0:T(8,128)S(1)} %get-tuple-element.26.refs_0_, f32[2,16,5120]{2,1,0:T(8,128)S(1)} %take.5.refs_1_.refs_6_, f32[2,16,5120]{2,1,0:T(8,128)S(1)} %collective-permute-done.18.refs_2_.refs_7_), custom_call_target="tpu_custom_call" | custom-call | flops 1000000000 | bytes 1 | tf_op jit(solution)/shard_map/project/pallas_call | solution.py:69
  155.5 2.5 %collective-permute-start.21 = (f32[64,192]{1,0:T(8,128)S(1)}, f32[64,192]{1,0:T(8,128)S(1)}, u32[]{:S(2)}, u32[]{:S(2)}) collective-permute-start(f32[64,192]{1,0:T(8,128)S(1)} %project.3.refs_0_), channel_id=1, source_target_pairs={{0,24},{8,16},{16,8},{24,0},{1,25},{9,17},{17,9},{25,1},{2,26},{10... | collective-permute-start | bytes 147464 | tf_op jit(solution)/shard_map/ppermute | solution.py:366
  158.0 0.5 collective-permute-start.20
  158.5 0.5 collective-permute-start.19
  159.0 1.7 %collective-permute-done.21.refs_3_ = f32[64,192]{1,0:T(8,128)S(1)} collective-permute-done((f32[64,192]{1,0:T(8,128)S(1)}, f32[64,192]{1,0:T(8,128)S(1)}, u32[]{:S(2)}, u32[]{:S(2)}) %collective-permute-start.21) | collective-permute-done | bytes 49184 | tf_op jit(solution)/shard_map/ppermute | solution.py:366
  160.7 1.5 collective-permute-done.20.refs_2_
  162.2 0.5 collective-permute-done.19.refs_1_
  162.8 7.3 %finish.1 = f32[192,15360]{1,0:T(8,128)} custom-call(f32[192,15360]{1,0:T(8,128)S(1)} %get-tuple-element.22.part_ref, bf16[64,15360]{1,0:T(8,128)(2,1)S(1)} %get-tuple-element.23.xh_ref, bf16[64,15360]{1,0:T(8,128)(2,1)S(1)} %get-tuple-element.24.xl_ref, f32[64,256]{1,0:T(8,128)S(1)} %get-tuple-element.25.rest_ref, f32[64,192]{1,0:T(8,128)S(1)} %project.3.refs_0_, ...), custom_call_target="tpu_custom_call" | custom-call | flops 1000000000 | bytes 1 | tf_op jit(solution)/shard_map/finish/pallas_call | solution.py:69
  (7 shorter events, 0.0 us)
Async XLA Ops:
  0.0 54.6 %copy-start = (f32[2,16,15360]{2,1,0:T(8,128)S(1)}, f32[2,16,15360]{2,1,0:T(8,128)}, u32[]{:S(2)}) copy-start(f32[2,16,15360]{2,1,0:T(8,128)} %refs_0_.5) | copy-start | bytes 5898244
  0.0 46.1 %collective-permute-start.1 = (f32[2,16,15360]{2,1,0:T(8,128)}, f32[2,16,15360]{2,1,0:T(8,128)S(1)}, u32[]{:S(2)}, u32[]{:S(2)}) collective-permute-start(f32[2,16,15360]{2,1,0:T(8,128)} %refs_0_.5), channel_id=1, source_target_pairs={{0,2},{1,3},{2,0},{3,1},{4,6},{5,7},{6,4},{7,5},{8,10},{9,11},{10,... | collective-permute-start | bytes 5898248 | tf_op jit(solution)/shard_map/ppermute | solution.py:380
  3.0 43.1 %collective-permute-start.4 = (f32[2,16,15360]{2,1,0:T(8,128)}, f32[2,16,15360]{2,1,0:T(8,128)S(1)}, u32[]{:S(2)}, u32[]{:S(2)}) collective-permute-start(f32[2,16,15360]{2,1,0:T(8,128)} %refs_0_.5), channel_id=1, source_target_pairs={{2,4},{3,5},{4,2},{5,3},{10,12},{11,13},{12,10},{13,11},{18,20},{1... | collective-permute-start | bytes 5898248 | tf_op jit(solution)/shard_map/ppermute | solution.py:380
  3.8 50.7 %collective-permute-start = (f32[2,16,15360]{2,1,0:T(8,128)}, f32[2,16,15360]{2,1,0:T(8,128)S(1)}, u32[]{:S(2)}, u32[]{:S(2)}) collective-permute-start(f32[2,16,15360]{2,1,0:T(8,128)} %refs_0_.5), channel_id=1, source_target_pairs={{0,1},{1,0},{2,3},{3,2},{4,5},{5,4},{6,7},{7,6},{8,9},{9,8},{10,11... | collective-permute-start | bytes 5898248 | tf_op jit(solution)/shard_map/ppermute | solution.py:380
  46.1 53.1 %copy-start.1 = (f32[2,16,15360]{2,1,0:T(8,128)}, f32[2,16,15360]{2,1,0:T(8,128)S(1)}, u32[]{:S(2)}) copy-start(f32[2,16,15360]{2,1,0:T(8,128)S(1)} %collective-permute-done.1.refs_2_) | copy-start | bytes 5898244
  46.1 8.4 %collective-permute-start.2 = (f32[2,16,15360]{2,1,0:T(8,128)S(1)}, f32[2,16,15360]{2,1,0:T(8,128)S(1)}, u32[]{:S(2)}, u32[]{:S(2)}) collective-permute-start(f32[2,16,15360]{2,1,0:T(8,128)S(1)} %collective-permute-done.1.refs_2_), channel_id=1, source_target_pairs={{0,1},{1,0},{2,3},{3,2},{4,5},{5,4},{6,7},{7,6},{8,9},{9,8},{10,11... | collective-permute-start | bytes 5898248 | tf_op jit(solution)/shard_map/ppermute | solution.py:380
  46.1 47.9 %collective-permute-start.5 = (f32[2,16,15360]{2,1,0:T(8,128)S(1)}, f32[2,16,15360]{2,1,0:T(8,128)S(1)}, u32[]{:S(2)}, u32[]{:S(2)}) collective-permute-start(f32[2,16,15360]{2,1,0:T(8,128)S(1)} %collective-permute-done.4.refs_6_), channel_id=1, source_target_pairs={{2,0},{3,1},{4,6},{5,7},{10,8},{11,9},{12,14},{13,15},{18,16},{19,... | collective-permute-start | bytes 5898248 | tf_op jit(solution)/shard_map/ppermute | solution.py:380
  47.4 46.6 %collective-permute-start.3 = (f32[2,16,15360]{2,1,0:T(8,128)S(1)}, f32[2,16,15360]{2,1,0:T(8,128)S(1)}, u32[]{:S(2)}, u32[]{:S(2)}) collective-permute-start(f32[2,16,15360]{2,1,0:T(8,128)S(1)} %collective-permute-done.1.refs_2_), channel_id=1, source_target_pairs={{2,4},{3,5},{4,2},{5,3},{10,12},{11,13},{12,10},{13,11},{18,20},{1... | collective-permute-start | bytes 5898248 | tf_op jit(solution)/shard_map/ppermute | solution.py:380
  54.5 44.7 %copy-start.2 = (f32[2,16,15360]{2,1,0:T(8,128)}, f32[2,16,15360]{2,1,0:T(8,128)S(1)}, u32[]{:S(2)}) copy-start(f32[2,16,15360]{2,1,0:T(8,128)S(1)} %collective-permute-done.refs_1_) | copy-start | bytes 5898244
  54.6 44.7 %copy-start.3 = (f32[2,16,15360]{2,1,0:T(8,128)}, f32[2,16,15360]{2,1,0:T(8,128)S(1)}, u32[]{:S(2)}) copy-start(f32[2,16,15360]{2,1,0:T(8,128)S(1)} %collective-permute-done.2.refs_3_) | copy-start | bytes 5898244
  60.3 7.1 %collective-permute-start.8 = (f32[128,192]{1,0:T(8,128)S(1)}, f32[128,192]{1,0:T(8,128)S(1)}, u32[]{:S(2)}, u32[]{:S(2)}) collective-permute-start(f32[128,192]{1,0:T(8,128)S(1)} %project.2.refs_0_), channel_id=1, source_target_pairs={{0,24},{8,16},{16,8},{24,0},{1,25},{9,17},{17,9},{25,1},{2,26},{10... | collective-permute-start | bytes 294920 | tf_op jit(solution)/shard_map/ppermute | solution.py:366
  62.9 7.1 %collective-permute-start.7 = (f32[128,192]{1,0:T(8,128)S(1)}, f32[128,192]{1,0:T(8,128)S(1)}, u32[]{:S(2)}, u32[]{:S(2)}) collective-permute-start(f32[128,192]{1,0:T(8,128)S(1)} %project.2.refs_0_), channel_id=1, source_target_pairs={{0,16},{8,24},{16,0},{24,8},{1,17},{9,25},{17,1},{25,9},{2,18},{10... | collective-permute-start | bytes 294920 | tf_op jit(solution)/shard_map/ppermute | solution.py:366
  63.4 6.8 %collective-permute-start.6 = (f32[128,192]{1,0:T(8,128)S(1)}, f32[128,192]{1,0:T(8,128)S(1)}, u32[]{:S(2)}, u32[]{:S(2)}) collective-permute-start(f32[128,192]{1,0:T(8,128)S(1)} %project.2.refs_0_), channel_id=1, source_target_pairs={{0,8},{8,0},{16,24},{24,16},{1,9},{9,1},{17,25},{25,17},{2,10},{10... | collective-permute-start | bytes 294920 | tf_op jit(solution)/shard_map/ppermute | solution.py:366
  67.4 31.8 %collective-permute-start.10 = (f32[2,16,15360]{2,1,0:T(8,128)S(1)}, f32[2,16,15360]{2,1,0:T(8,128)S(1)}, u32[]{:S(2)}, u32[]{:S(2)}) collective-permute-start(f32[2,16,15360]{2,1,0:T(8,128)S(1)} %collective-permute-done.4.refs_6_), channel_id=1, source_target_pairs={{0,1},{1,0},{2,3},{3,2},{4,5},{5,4},{6,7},{7,6},{8,9},{9,8},{10,11... | collective-permute-start | bytes 5898248 | tf_op jit(solution)/shard_map/ppermute | solution.py:380
  95.0 35.4 %copy-start.4 = (f32[2,16,15360]{2,1,0:T(8,128)}, f32[2,16,15360]{2,1,0:T(8,128)S(1)}, u32[]{:S(2)}) copy-start(f32[2,16,15360]{2,1,0:T(8,128)S(1)} %get-tuple-element.16.refs_4_.x_ref) | copy-start | bytes 5898244
  95.0 4.2 %collective-permute-start.9 = (f32[2,16,15360]{2,1,0:T(8,128)S(1)}, f32[2,16,15360]{2,1,0:T(8,128)S(1)}, u32[]{:S(2)}, u32[]{:S(2)}) collective-permute-start(f32[2,16,15360]{2,1,0:T(8,128)S(1)} %get-tuple-element.16.refs_4_.x_ref), channel_id=1, source_target_pairs={{0,1},{1,0},{2,3},{3,2},{4,5},{5,4},{6,7},{7,6},{8,9},{9,8},{10,11... | collective-permute-start | bytes 5898248 | tf_op jit(solution)/shard_map/ppermute | solution.py:380
  95.1 33.8 %collective-permute-start.15 = (f32[2,16,10240]{2,1,0:T(8,128)S(1)}, f32[2,16,10240]{2,1,0:T(8,128)S(1)}, u32[]{:S(2)}, u32[]{:S(2)}) collective-permute-start(f32[2,16,10240]{2,1,0:T(8,128)S(1)} %get-tuple-element.21), channel_id=1, source_target_pairs={{0,2},{1,3},{2,0},{3,1},{4,6},{5,7},{6,4},{7,5},{8,10},{9,11},{10,... | collective-permute-start | bytes 3932168 | tf_op jit(solution)/shard_map/ppermute | solution.py:380
  99.3 9.6 %copy-start.5 = (f32[2,16,15360]{2,1,0:T(8,128)}, f32[2,16,15360]{2,1,0:T(8,128)S(1)}, u32[]{:S(2)}) copy-start(f32[2,16,15360]{2,1,0:T(8,128)S(1)} %collective-permute-done.9.refs_5_) | copy-start | bytes 5898244
  108.8 6.8 %collective-permute-start.13 = (f32[128,224]{1,0:T(8,128)S(1)}, f32[128,224]{1,0:T(8,128)S(1)}, u32[]{:S(2)}, u32[]{:S(2)}) collective-permute-start(f32[128,224]{1,0:T(8,128)S(1)} %cross.1.a_ref), channel_id=1, source_target_pairs={{0,24},{8,16},{16,8},{24,0},{1,25},{9,17},{17,9},{25,1},{2,26},{10... | collective-permute-start | bytes 344072 | tf_op jit(solution)/shard_map/ppermute | solution.py:366
  111.4 6.8 %collective-permute-start.12 = (f32[128,224]{1,0:T(8,128)S(1)}, f32[128,224]{1,0:T(8,128)S(1)}, u32[]{:S(2)}, u32[]{:S(2)}) collective-permute-start(f32[128,224]{1,0:T(8,128)S(1)} %cross.1.a_ref), channel_id=1, source_target_pairs={{0,16},{8,24},{16,0},{24,8},{1,17},{9,25},{17,1},{25,9},{2,18},{10... | collective-permute-start | bytes 344072 | tf_op jit(solution)/shard_map/ppermute | solution.py:366
  111.9 6.4 %collective-permute-start.11 = (f32[128,224]{1,0:T(8,128)S(1)}, f32[128,224]{1,0:T(8,128)S(1)}, u32[]{:S(2)}, u32[]{:S(2)}) collective-permute-start(f32[128,224]{1,0:T(8,128)S(1)} %cross.1.a_ref), channel_id=1, source_target_pairs={{0,8},{8,0},{16,24},{24,16},{1,9},{9,1},{17,25},{25,17},{2,10},{10... | collective-permute-start | bytes 344072 | tf_op jit(solution)/shard_map/ppermute | solution.py:366
  118.4 11.6 %collective-permute-start.14 = (f32[128,128]{1,0:T(8,128)S(1)}, f32[128,128]{1,0:T(8,128)S(1)}, u32[]{:S(2)}, u32[]{:S(2)}) collective-permute-start(f32[128,128]{1,0:T(8,128)S(1)} %get-tuple-element.17.gram_ref), channel_id=1, source_target_pairs={{2,0},{3,1},{4,6},{5,7},{10,8},{11,9},{12,14},{13,15},{18,16},{19,... | collective-permute-start | bytes 196616 | tf_op jit(solution)/shard_map/ppermute | solution.py:380
  130.4 1.5 copy-start.6
  130.4 3.1 %collective-permute-start.16 = (f32[2,16,10240]{2,1,0:T(8,128)S(1)}, f32[2,16,10240]{2,1,0:T(8,128)S(1)}, u32[]{:S(2)}, u32[]{:S(2)}) collective-permute-start(f32[2,16,10240]{2,1,0:T(8,128)S(1)} %take.3.refs_6_.refs_4_), channel_id=1, source_target_pairs={{0,1},{1,0},{2,3},{3,2},{4,5},{5,4},{6,7},{7,6},{8,9},{9,8},{10,11... | collective-permute-start | bytes 3932168 | tf_op jit(solution)/shard_map/ppermute | solution.py:380
  131.5 17.4 %collective-permute-start.17 = (f32[2,16,5120]{2,1,0:T(8,128)}, f32[2,16,5120]{2,1,0:T(8,128)}, u32[]{:S(2)}, u32[]{:S(2)}) collective-permute-start(f32[2,16,5120]{2,1,0:T(8,128)} %take.4), channel_id=1, source_target_pairs={{0,2},{1,3},{2,0},{3,1},{4,6},{5,7},{6,4},{7,5},{8,10},{9,11},{10,... | collective-permute-start | bytes 1966088 | tf_op jit(solution)/shard_map/ppermute | solution.py:380
  150.0 2.2 %collective-permute-start.18 = (f32[2,16,5120]{2,1,0:T(8,128)S(1)}, f32[2,16,5120]{2,1,0:T(8,128)S(1)}, u32[]{:S(2)}, u32[]{:S(2)}) collective-permute-start(f32[2,16,5120]{2,1,0:T(8,128)S(1)} %take.5.refs_1_.refs_6_), channel_id=1, source_target_pairs={{0,1},{1,0},{2,3},{3,2},{4,5},{5,4},{6,7},{7,6},{8,9},{9,8},{10,11... | collective-permute-start | bytes 1966088 | tf_op jit(solution)/shard_map/ppermute | solution.py:380
  155.5 5.3 %collective-permute-start.21 = (f32[64,192]{1,0:T(8,128)S(1)}, f32[64,192]{1,0:T(8,128)S(1)}, u32[]{:S(2)}, u32[]{:S(2)}) collective-permute-start(f32[64,192]{1,0:T(8,128)S(1)} %project.3.refs_0_), channel_id=1, source_target_pairs={{0,24},{8,16},{16,8},{24,0},{1,25},{9,17},{17,9},{25,1},{2,26},{10... | collective-permute-start | bytes 147464 | tf_op jit(solution)/shard_map/ppermute | solution.py:366
  158.0 4.3 %collective-permute-start.20 = (f32[64,192]{1,0:T(8,128)S(1)}, f32[64,192]{1,0:T(8,128)S(1)}, u32[]{:S(2)}, u32[]{:S(2)}) collective-permute-start(f32[64,192]{1,0:T(8,128)S(1)} %project.3.refs_0_), channel_id=1, source_target_pairs={{0,16},{8,24},{16,0},{24,8},{1,17},{9,25},{17,1},{25,9},{2,18},{10... | collective-permute-start | bytes 147464 | tf_op jit(solution)/shard_map/ppermute | solution.py:366
  158.5 4.3 %collective-permute-start.19 = (f32[64,192]{1,0:T(8,128)S(1)}, f32[64,192]{1,0:T(8,128)S(1)}, u32[]{:S(2)}, u32[]{:S(2)}) collective-permute-start(f32[64,192]{1,0:T(8,128)S(1)} %project.3.refs_0_), channel_id=1, source_target_pairs={{0,8},{8,0},{16,24},{24,16},{1,9},{9,1},{17,25},{25,17},{2,10},{10... | collective-permute-start | bytes 147464 | tf_op jit(solution)/shard_map/ppermute | solution.py:366

commit v4 on v3

--- a/solution.py
+++ b/solution.py
@@ -13,9 +13,10 @@
 NN = (((1,), (0,)), ((), ()))
 MIB = 1024 * 1024
 TILE = 2560
+FTILE = 5120
 WIDTHS = (4, 2)
 COST = dict(settle=10**6, hold=10**9, join=10**6, take=10**6, project=10**9, cross=10**9, weigh=10**6, apply=10**9, finish=10**9)
-FINISH = 16
+FINISH = 24
 MADE = jax.ShapeDtypeStruct
 
 
@@ -49,9 +50,9 @@
     return pl.BlockSpec(x.shape, lambda g: (0,) * x.ndim)
 
 
-def columns(x, at=0):
+def columns(x, at=0, tile=TILE):
     lead = x.shape[:-1]
-    return pl.BlockSpec(lead + (TILE,), lambda g: (0,) * len(lead) + (at // TILE + g,))
+    return pl.BlockSpec(lead + (tile,), lambda g: (0,) * len(lead) + (at // tile + g,))
 
 
 HELD = pl.BlockSpec(memory_space=pltpu.VMEM)
@@ -61,8 +62,8 @@
     return pltpu.with_memory_space_constraint(x, pltpu.VMEM)
 
 
-def tile_of(ref):
-    return ref[:, pl.ds(pl.multiple_of(pl.program_id(0) * TILE, TILE), TILE)]
+def tile_of(ref, tile=TILE):
+    return ref[:, pl.ds(pl.multiple_of(pl.program_id(0) * tile, tile), tile)]
 
 
 def call(kernel, steps, operands, specs, outs, out_specs, name, scratch=(), vmem=16):
@@ -333,29 +334,29 @@
         @pl.when(jnp.logical_and(step >= starts[i], step < starts[i + 1]))
         def _():
             high, low = split(block_rows(pieces[each * i : each * (i + 1)]))
-            high, low = jnp.concatenate([tile_of(xh_ref), high], axis=0), jnp.concatenate([tile_of(xl_ref), low], axis=0)
+            high, low = jnp.concatenate([tile_of(xh_ref, FTILE), high], axis=0), jnp.concatenate([tile_of(xl_ref, FTILE), low], axis=0)
             right = jnp.concatenate([high, high, low], axis=0)
-            out_ref[...] = tile_of(part_ref) - lax.dot_general(left_ref[...], right, NN, preferred_element_type=F32)
+            out_ref[...] = tile_of(part_ref, FTILE) - lax.dot_general(left_ref[...], right, NN, preferred_element_type=F32)
 
 
 def finish(part, xh, xl, rest, lasts, parts):
     nev, width = part.shape
     starts, specs = [0], []
     for pieces in parts:
-        first, count = starts[-1], pieces[0].shape[-1] // TILE
+        first, count = starts[-1], pieces[0].shape[-1] // FTILE
         starts.append(first + count)
         specs += [
-            pl.BlockSpec((*x.shape[:-1], TILE), lambda g, first=first, count=count: (0, 0, jnp.clip(g - first, 0, count - 1)))
+            pl.BlockSpec((*x.shape[:-1], FTILE), lambda g, first=first, count=count: (0, 0, jnp.clip(g - first, 0, count - 1)))
             for x in pieces
         ]
     out = jax.ShapeDtypeStruct(part.shape, F32)
     return call(
         functools.partial(finish_kernel, starts),
-        width // TILE,
+        width // FTILE,
         [held(part), held(xh), held(xl), rest, *lasts, *[x for pieces in parts for x in pieces]],
         [HELD] * 3 + [whole(rest)] + [whole(x) for x in lasts] + specs,
         out,
-        columns(out),
+        columns(out, 0, FTILE),
         "finish",
         [pltpu.VMEM((nev, 6 * rest.shape[0]), BF16)],
         vmem=FINISH,
@@ -395,7 +396,8 @@
     p0 = project(kept, near, lies=True)
     known0 = settle(p0, *others(p0))
     stretches = [(sum(WIDTHS[:i]) * TILE, w * TILE) for i, w in enumerate(WIDTHS)]
-    third, cut = join(across, outer, WIDTHS[0], known0)
+    across = take(across, 0, width, known0)
+    third, cut = join(across, outer, WIDTHS[0])
     fourth = [along(cut, PAIR)]
     near += [third, swap(third)]
     both = cross(kept, near + [inner, inner2], 4, 2)

time: 170 us -> 169 us (level)
  starting transfers between devices: 22.6 us -> 18.2 us
  waiting for transfers between devices: 95.2 us -> 98.5 us
    ppermute x13, starting transfers between devices: 11.9 us -> 7.51 us  [along(): return lax.ppermute(x, 'col', pairs)]
    ppermute x13, waiting for transfers between devices: 79.3 us -> 82.7 us  [along(): return lax.ppermute(x, 'col', pairs)]
    pallas_call x13 -> x14, Pallas kernels: 51.9 us -> 52 us  [call(): pl.pallas_call(kernel, out_shape=outs, grid=(steps,), in_specs=specs, out...]
  transfers between devices with their start and end apart: 22 -> 22, of which waited for: 16 -> 17; matrix products, arithmetic and copies ran while one was open for 0% -> 0% of each run, Pallas kernels for 23% -> 24%
where the time goes in v4:
time: 169 us
  waiting for transfers between devices  98.5 us (58%)
  Pallas kernels  52 us (31%)
  starting transfers between devices  18.2 us (11%)
    ppermute x13, waiting for transfers between devices, along(): return lax.ppermute(x, 'col', pairs)  82.7 us
    pallas_call x14, Pallas kernels, call(): pl.pallas_call(kernel, out_shape=outs, grid=(steps,), in_specs=specs, out...  52 us
    ppermute x9, waiting for transfers between devices, others(): lax.ppermute(x, 'row', [(i, i ^ k) for i in range(4)])  15.9 us
    ppermute x9, starting transfers between devices, others(): lax.ppermute(x, 'row', [(i, i ^ k) for i in range(4)])  10.7 us
    ppermute x13, starting transfers between devices, along(): return lax.ppermute(x, 'col', pairs)  7.51 us
  transfers between devices with their start and end apart: 22, of which 17 were waited for; matrix products, arithmetic and copies ran while one was open for 0% of the time, Pallas kernels for 24%

profile of v4, /device:TPU:0, one launch (start us, length us, event | category | flops | bytes accessed | tf_op | source)
XLA Modules:
  0.0 169.0 jit_solution(1128037290792818939)
XLA Ops:
  0.0 3.0 %collective-permute-start.1 = (f32[2,16,15360]{2,1,0:T(8,128)}, f32[2,16,15360]{2,1,0:T(8,128)S(1)}, u32[]{:S(2)}, u32[]{:S(2)}) collective-permute-start(f32[2,16,15360]{2,1,0:T(8,128)} %refs_0_.5), channel_id=1, source_target_pairs={{0,2},{1,3},{2,0},{3,1},{4,6},{5,7},{6,4},{7,5},{8,10},{9,11},{10,... | collective-permute-start | bytes 5898248 | tf_op jit(solution)/shard_map/ppermute | solution.py:381
  3.0 0.8 collective-permute-start.7
  3.8 0.1 collective-permute-start
  3.9 42.2 %collective-permute-done.1.refs_2_ = f32[2,16,15360]{2,1,0:T(8,128)S(1)} collective-permute-done((f32[2,16,15360]{2,1,0:T(8,128)}, f32[2,16,15360]{2,1,0:T(8,128)S(1)}, u32[]{:S(2)}, u32[]{:S(2)}) %collective-permute-start.1) | collective-permute-done | bytes 1966112 | tf_op jit(solution)/shard_map/ppermute | solution.py:381
  46.1 0.0 collective-permute-start.2
  46.1 0.8 collective-permute-start.3
  46.9 0.0 collective-permute-done.7.refs_6_
  46.9 1.3 collective-permute-start.8
  48.2 6.3 %hold.1.slab_ref = f32[192,15360]{1,0:T(8,128)S(1)} custom-call(f32[192,15360]{1,0:T(8,128)} %slab_ref.3), custom_call_target="tpu_custom_call" | custom-call | flops 1000000000 | bytes 1 | tf_op jit(solution)/shard_map/hold/pallas_call | solution.py:70
  54.5 0.0 collective-permute-done.refs_1_
  54.5 0.0 copy-start.2
  54.6 0.0 collective-permute-done.2.refs_3_
  54.6 0.0 copy-done
  54.6 0.0 copy-start.3
  54.6 5.7 %project.2.refs_0_ = f32[128,192]{1,0:T(8,128)S(1)} custom-call(f32[192,15360]{1,0:T(8,128)S(1)} %hold.1.slab_ref, f32[2,16,15360]{2,1,0:T(8,128)S(1)} %copy-done, f32[2,16,15360]{2,1,0:T(8,128)S(1)} %collective-permute-done.refs_1_, f32[2,16,15360]{2,1,0:T(8,128)S(1)} %collective-permute-done.1.refs_2_, f32[2,16,15360]{2,1,0:T(8,128)S(1)} %collective-permute-done.2.refs_3_), custom_call_target="tpu_custom_call" | custom-call | flops 1000000000 | bytes 1 | tf_op jit(solution)/shard_map/project/pallas_call | solution.py:70
  60.3 2.6 %collective-permute-start.6 = (f32[128,192]{1,0:T(8,128)S(1)}, f32[128,192]{1,0:T(8,128)S(1)}, u32[]{:S(2)}, u32[]{:S(2)}) collective-permute-start(f32[128,192]{1,0:T(8,128)S(1)} %project.2.refs_0_), channel_id=1, source_target_pairs={{0,24},{8,16},{16,8},{24,0},{1,25},{9,17},{17,9},{25,1},{2,26},{10... | collective-permute-start | bytes 294920 | tf_op jit(solution)/shard_map/ppermute | solution.py:367
  62.9 0.5 collective-permute-start.5
  63.4 0.4 collective-permute-start.4
  63.9 3.5 %collective-permute-done.6.refs_3_ = f32[128,192]{1,0:T(8,128)S(1)} collective-permute-done((f32[128,192]{1,0:T(8,128)S(1)}, f32[128,192]{1,0:T(8,128)S(1)}, u32[]{:S(2)}, u32[]{:S(2)}) %collective-permute-start.6) | collective-permute-done | bytes 98336 | tf_op jit(solution)/shard_map/ppermute | solution.py:367
  67.4 0.0 collective-permute-start.10
  67.4 2.6 %collective-permute-done.5.refs_2_ = f32[128,192]{1,0:T(8,128)S(1)} collective-permute-done((f32[128,192]{1,0:T(8,128)S(1)}, f32[128,192]{1,0:T(8,128)S(1)}, u32[]{:S(2)}, u32[]{:S(2)}) %collective-permute-start.5) | collective-permute-done | bytes 98336 | tf_op jit(solution)/shard_map/ppermute | solution.py:367
  70.0 0.2 collective-permute-done.4.refs_1_
  70.2 0.0 collective-permute-done.3.x_ref
  70.2 0.5 take.4.a_ref
  70.8 25.0 %collective-permute-done.8.b_ref = f32[2,16,15360]{2,1,0:T(8,128)S(1)} collective-permute-done((f32[2,16,15360]{2,1,0:T(8,128)S(1)}, f32[2,16,15360]{2,1,0:T(8,128)S(1)}, u32[]{:S(2)}, u32[]{:S(2)}) %collective-permute-start.8) | collective-permute-done | bytes 1966112 | tf_op jit(solution)/shard_map/ppermute | solution.py:381
  95.8 1.0 join.1
  96.8 0.1 collective-permute-start.9
  96.8 0.1 collective-permute-start.15
  96.9 0.0 collective-permute-done.10.refs_7_
  96.9 3.9 %collective-permute-done.9.refs_5_ = f32[2,16,15360]{2,1,0:T(8,128)S(1)} collective-permute-done((f32[2,16,15360]{2,1,0:T(8,128)S(1)}, f32[2,16,15360]{2,1,0:T(8,128)S(1)}, u32[]{:S(2)}, u32[]{:S(2)}) %collective-permute-start.9) | collective-permute-done | bytes 1966112 | tf_op jit(solution)/shard_map/ppermute | solution.py:381
  100.8 0.0 copy-start.5
  100.8 9.6 %cross.1.a_ref = f32[128,224]{1,0:T(8,128)S(1)} custom-call(f32[192,15360]{1,0:T(8,128)S(1)} %hold.1.slab_ref, f32[2,16,15360]{2,1,0:T(8,128)S(1)} %copy-done, f32[2,16,15360]{2,1,0:T(8,128)S(1)} %collective-permute-done.refs_1_, f32[2,16,15360]{2,1,0:T(8,128)S(1)} %collective-permute-done.1.refs_2_, f32[2,16,15360]{2,1,0:T(8,128)S(1)} %collective-permute-done.2.refs_3_, ...), custom_call_target="tpu_custom_call" | custom-call | flops 1000000000 | bytes 1 | tf_op jit(solution)/shard_map/cross/pallas_call | solution.py:70
  110.4 0.0 copy-done.5
  110.4 2.5 %collective-permute-start.13 = (f32[128,224]{1,0:T(8,128)S(1)}, f32[128,224]{1,0:T(8,128)S(1)}, u32[]{:S(2)}, u32[]{:S(2)}) collective-permute-start(f32[128,224]{1,0:T(8,128)S(1)} %cross.1.a_ref), channel_id=1, source_target_pairs={{0,24},{8,16},{16,8},{24,0},{1,25},{9,17},{17,9},{25,1},{2,26},{10... | collective-permute-start | bytes 344072 | tf_op jit(solution)/shard_map/ppermute | solution.py:367
  112.9 0.5 collective-permute-start.12
  113.4 0.5 collective-permute-start.11
  114.0 3.2 %collective-permute-done.13.d_ref = f32[128,224]{1,0:T(8,128)S(1)} collective-permute-done((f32[128,224]{1,0:T(8,128)S(1)}, f32[128,224]{1,0:T(8,128)S(1)}, u32[]{:S(2)}, u32[]{:S(2)}) %collective-permute-start.13) | collective-permute-done | bytes 114720 | tf_op jit(solution)/shard_map/ppermute | solution.py:367
  117.2 2.5 %collective-permute-done.12.c_ref = f32[128,224]{1,0:T(8,128)S(1)} collective-permute-done((f32[128,224]{1,0:T(8,128)S(1)}, f32[128,224]{1,0:T(8,128)S(1)}, u32[]{:S(2)}, u32[]{:S(2)}) %collective-permute-start.12) | collective-permute-done | bytes 114720 | tf_op jit(solution)/shard_map/ppermute | solution.py:367
  119.7 0.1 collective-permute-done.11.b_ref
  119.8 0.1 settle.3
  119.9 1.3 collective-permute-start.14
  121.2 7.3 %collective-permute-done.15.x_ref = f32[2,16,10240]{2,1,0:T(8,128)S(1)} collective-permute-done((f32[2,16,10240]{2,1,0:T(8,128)S(1)}, f32[2,16,10240]{2,1,0:T(8,128)S(1)}, u32[]{:S(2)}, u32[]{:S(2)}) %collective-permute-start.15) | collective-permute-done | bytes 1310752 | tf_op jit(solution)/shard_map/ppermute | solution.py:381
  128.5 1.0 collective-permute-done.14.given_ref.refs_0_
  129.4 0.4 take.5.refs_6_.refs_4_
  129.8 0.0 copy-start.6
  129.8 0.1 collective-permute-start.16
  129.9 1.0 take.6
  130.9 0.0 collective-permute-start.17
  130.9 0.0 copy-done.6
  130.9 1.5 weigh.1
  132.4 0.5 collective-permute-done.16.refs_7_.refs_5_
  132.9 14.7 %apply.1 = (f32[192,15360]{1,0:T(8,128)S(1)}, bf16[64,15360]{1,0:T(8,128)(2,1)S(1)}, bf16[64,15360]{1,0:T(8,128)(2,1)S(1)}, f32[64,192]{1,0:T(8,128)S(1)}) custom-call(bf16[256,192]{1,0:T(8,128)(2,1)S(1)} %get-tuple-element.19.high_ref, bf16[256,192]{1,0:T(8,128)(2,1)S(1)} %get-tuple-element.20.low_ref, f32[192,15360]{1,0:T(8,128)} %slab_ref.3, ...), custom_call_target="tpu_custom_call" | custom-call | flops 1000000000 | bytes 1 | tf_op jit(solution)/shard_map/apply/pallas_call | solution.py:70
  147.7 0.7 collective-permute-done.17.x_ref
  148.3 1.1 take.7.refs_1_.refs_6_
  149.5 0.1 collective-permute-start.18
  149.6 2.1 %collective-permute-done.18.refs_2_.refs_7_ = f32[2,16,5120]{2,1,0:T(8,128)S(1)} collective-permute-done((f32[2,16,5120]{2,1,0:T(8,128)S(1)}, f32[2,16,5120]{2,1,0:T(8,128)S(1)}, u32[]{:S(2)}, u32[]{:S(2)}) %collective-permute-start.18) | collective-permute-done | bytes 655392 | tf_op jit(solution)/shard_map/ppermute | solution.py:381
  151.6 3.3 %project.3.refs_0_ = f32[64,192]{1,0:T(8,128)S(1)} custom-call(f32[192,15360]{1,0:T(8,128)} %slab_ref.3, f32[64,192]{1,0:T(8,128)S(1)} %get-tuple-element.26.refs_0_, f32[2,16,5120]{2,1,0:T(8,128)S(1)} %take.7.refs_1_.refs_6_, f32[2,16,5120]{2,1,0:T(8,128)S(1)} %collective-permute-done.18.refs_2_.refs_7_), custom_call_target="tpu_custom_call" | custom-call | flops 1000000000 | bytes 1 | tf_op jit(solution)/shard_map/project/pallas_call | solution.py:70
  154.9 2.5 %collective-permute-start.21 = (f32[64,192]{1,0:T(8,128)S(1)}, f32[64,192]{1,0:T(8,128)S(1)}, u32[]{:S(2)}, u32[]{:S(2)}) collective-permute-start(f32[64,192]{1,0:T(8,128)S(1)} %project.3.refs_0_), channel_id=1, source_target_pairs={{0,24},{8,16},{16,8},{24,0},{1,25},{9,17},{17,9},{25,1},{2,26},{10... | collective-permute-start | bytes 147464 | tf_op jit(solution)/shard_map/ppermute | solution.py:367
  157.4 0.5 collective-permute-start.20
  157.9 0.5 collective-permute-start.19
  158.5 1.7 %collective-permute-done.21.refs_3_ = f32[64,192]{1,0:T(8,128)S(1)} collective-permute-done((f32[64,192]{1,0:T(8,128)S(1)}, f32[64,192]{1,0:T(8,128)S(1)}, u32[]{:S(2)}, u32[]{:S(2)}) %collective-permute-start.21) | collective-permute-done | bytes 49184 | tf_op jit(solution)/shard_map/ppermute | solution.py:367
  160.2 1.5 collective-permute-done.20.refs_2_
  161.7 0.5 collective-permute-done.19.refs_1_
  162.2 6.8 %finish.1 = f32[192,15360]{1,0:T(8,128)} custom-call(f32[192,15360]{1,0:T(8,128)S(1)} %get-tuple-element.22.part_ref, bf16[64,15360]{1,0:T(8,128)(2,1)S(1)} %get-tuple-element.23.xh_ref, bf16[64,15360]{1,0:T(8,128)(2,1)S(1)} %get-tuple-element.24.xl_ref, f32[64,256]{1,0:T(8,128)S(1)} %get-tuple-element.25.rest_ref, f32[64,192]{1,0:T(8,128)S(1)} %project.3.refs_0_, ...), custom_call_target="tpu_custom_call" | custom-call | flops 1000000000 | bytes 1 | tf_op jit(solution)/shard_map/finish/pallas_call | solution.py:70
  (8 shorter events, 0.0 us)
Async XLA Ops:
  0.0 54.6 %copy-start = (f32[2,16,15360]{2,1,0:T(8,128)S(1)}, f32[2,16,15360]{2,1,0:T(8,128)}, u32[]{:S(2)}) copy-start(f32[2,16,15360]{2,1,0:T(8,128)} %refs_0_.5) | copy-start | bytes 5898244
  0.0 46.1 %collective-permute-start.1 = (f32[2,16,15360]{2,1,0:T(8,128)}, f32[2,16,15360]{2,1,0:T(8,128)S(1)}, u32[]{:S(2)}, u32[]{:S(2)}) collective-permute-start(f32[2,16,15360]{2,1,0:T(8,128)} %refs_0_.5), channel_id=1, source_target_pairs={{0,2},{1,3},{2,0},{3,1},{4,6},{5,7},{6,4},{7,5},{8,10},{9,11},{10,... | collective-permute-start | bytes 5898248 | tf_op jit(solution)/shard_map/ppermute | solution.py:381
  3.0 43.9 %collective-permute-start.7 = (f32[2,16,15360]{2,1,0:T(8,128)}, f32[2,16,15360]{2,1,0:T(8,128)S(1)}, u32[]{:S(2)}, u32[]{:S(2)}) collective-permute-start(f32[2,16,15360]{2,1,0:T(8,128)} %refs_0_.5), channel_id=1, source_target_pairs={{2,4},{3,5},{4,2},{5,3},{10,12},{11,13},{12,10},{13,11},{18,20},{1... | collective-permute-start | bytes 5898248 | tf_op jit(solution)/shard_map/ppermute | solution.py:381
  3.8 50.7 %collective-permute-start = (f32[2,16,15360]{2,1,0:T(8,128)}, f32[2,16,15360]{2,1,0:T(8,128)S(1)}, u32[]{:S(2)}, u32[]{:S(2)}) collective-permute-start(f32[2,16,15360]{2,1,0:T(8,128)} %refs_0_.5), channel_id=1, source_target_pairs={{0,1},{1,0},{2,3},{3,2},{4,5},{5,4},{6,7},{7,6},{8,9},{9,8},{10,11... | collective-permute-start | bytes 5898248 | tf_op jit(solution)/shard_map/ppermute | solution.py:381
  46.1 54.7 %copy-start.1 = (f32[2,16,15360]{2,1,0:T(8,128)}, f32[2,16,15360]{2,1,0:T(8,128)S(1)}, u32[]{:S(2)}) copy-start(f32[2,16,15360]{2,1,0:T(8,128)S(1)} %collective-permute-done.1.refs_2_) | copy-start | bytes 5898244
  46.1 8.4 %collective-permute-start.2 = (f32[2,16,15360]{2,1,0:T(8,128)S(1)}, f32[2,16,15360]{2,1,0:T(8,128)S(1)}, u32[]{:S(2)}, u32[]{:S(2)}) collective-permute-start(f32[2,16,15360]{2,1,0:T(8,128)S(1)} %collective-permute-done.1.refs_2_), channel_id=1, source_target_pairs={{0,1},{1,0},{2,3},{3,2},{4,5},{5,4},{6,7},{7,6},{8,9},{9,8},{10,11... | collective-permute-start | bytes 5898248 | tf_op jit(solution)/shard_map/ppermute | solution.py:381
  46.1 24.1 %collective-permute-start.3 = (f32[2,16,15360]{2,1,0:T(8,128)S(1)}, f32[2,16,15360]{2,1,0:T(8,128)S(1)}, u32[]{:S(2)}, u32[]{:S(2)}) collective-permute-start(f32[2,16,15360]{2,1,0:T(8,128)S(1)} %collective-permute-done.1.refs_2_), channel_id=1, source_target_pairs={{2,4},{3,5},{4,2},{5,3},{10,12},{11,13},{12,10},{13,11},{18,20},{1... | collective-permute-start | bytes 5898248 | tf_op jit(solution)/shard_map/ppermute | solution.py:381
  46.9 48.9 %collective-permute-start.8 = (f32[2,16,15360]{2,1,0:T(8,128)S(1)}, f32[2,16,15360]{2,1,0:T(8,128)S(1)}, u32[]{:S(2)}, u32[]{:S(2)}) collective-permute-start(f32[2,16,15360]{2,1,0:T(8,128)S(1)} %collective-permute-done.7.refs_6_), channel_id=1, source_target_pairs={{2,0},{3,1},{4,6},{5,7},{10,8},{11,9},{12,14},{13,15},{18,16},{19,... | collective-permute-start | bytes 5898248 | tf_op jit(solution)/shard_map/ppermute | solution.py:381
  54.5 46.3 %copy-start.2 = (f32[2,16,15360]{2,1,0:T(8,128)}, f32[2,16,15360]{2,1,0:T(8,128)S(1)}, u32[]{:S(2)}) copy-start(f32[2,16,15360]{2,1,0:T(8,128)S(1)} %collective-permute-done.refs_1_) | copy-start | bytes 5898244
  54.6 46.2 %copy-start.3 = (f32[2,16,15360]{2,1,0:T(8,128)}, f32[2,16,15360]{2,1,0:T(8,128)S(1)}, u32[]{:S(2)}) copy-start(f32[2,16,15360]{2,1,0:T(8,128)S(1)} %collective-permute-done.2.refs_3_) | copy-start | bytes 5898244
  60.3 7.0 %collective-permute-start.6 = (f32[128,192]{1,0:T(8,128)S(1)}, f32[128,192]{1,0:T(8,128)S(1)}, u32[]{:S(2)}, u32[]{:S(2)}) collective-permute-start(f32[128,192]{1,0:T(8,128)S(1)} %project.2.refs_0_), channel_id=1, source_target_pairs={{0,24},{8,16},{16,8},{24,0},{1,25},{9,17},{17,9},{25,1},{2,26},{10... | collective-permute-start | bytes 294920 | tf_op jit(solution)/shard_map/ppermute | solution.py:367
  62.9 7.1 %collective-permute-start.5 = (f32[128,192]{1,0:T(8,128)S(1)}, f32[128,192]{1,0:T(8,128)S(1)}, u32[]{:S(2)}, u32[]{:S(2)}) collective-permute-start(f32[128,192]{1,0:T(8,128)S(1)} %project.2.refs_0_), channel_id=1, source_target_pairs={{0,16},{8,24},{16,0},{24,8},{1,17},{9,25},{17,1},{25,9},{2,18},{10... | collective-permute-start | bytes 294920 | tf_op jit(solution)/shard_map/ppermute | solution.py:367
  63.4 6.8 %collective-permute-start.4 = (f32[128,192]{1,0:T(8,128)S(1)}, f32[128,192]{1,0:T(8,128)S(1)}, u32[]{:S(2)}, u32[]{:S(2)}) collective-permute-start(f32[128,192]{1,0:T(8,128)S(1)} %project.2.refs_0_), channel_id=1, source_target_pairs={{0,8},{8,0},{16,24},{24,16},{1,9},{9,1},{17,25},{25,17},{2,10},{10... | collective-permute-start | bytes 294920 | tf_op jit(solution)/shard_map/ppermute | solution.py:367
  67.4 29.6 %collective-permute-start.10 = (f32[2,16,15360]{2,1,0:T(8,128)S(1)}, f32[2,16,15360]{2,1,0:T(8,128)S(1)}, u32[]{:S(2)}, u32[]{:S(2)}) collective-permute-start(f32[2,16,15360]{2,1,0:T(8,128)S(1)} %collective-permute-done.7.refs_6_), channel_id=1, source_target_pairs={{0,1},{1,0},{2,3},{3,2},{4,5},{5,4},{6,7},{7,6},{8,9},{9,8},{10,11... | collective-permute-start | bytes 5898248 | tf_op jit(solution)/shard_map/ppermute | solution.py:381
  96.8 33.1 %copy-start.4 = (f32[2,16,15360]{2,1,0:T(8,128)}, f32[2,16,15360]{2,1,0:T(8,128)S(1)}, u32[]{:S(2)}) copy-start(f32[2,16,15360]{2,1,0:T(8,128)S(1)} %get-tuple-element.16.refs_4_.x_ref) | copy-start | bytes 5898244
  96.8 4.0 %collective-permute-start.9 = (f32[2,16,15360]{2,1,0:T(8,128)S(1)}, f32[2,16,15360]{2,1,0:T(8,128)S(1)}, u32[]{:S(2)}, u32[]{:S(2)}) collective-permute-start(f32[2,16,15360]{2,1,0:T(8,128)S(1)} %get-tuple-element.16.refs_4_.x_ref), channel_id=1, source_target_pairs={{0,1},{1,0},{2,3},{3,2},{4,5},{5,4},{6,7},{7,6},{8,9},{9,8},{10,11... | collective-permute-start | bytes 5898248 | tf_op jit(solution)/shard_map/ppermute | solution.py:381
  96.8 31.6 %collective-permute-start.15 = (f32[2,16,10240]{2,1,0:T(8,128)S(1)}, f32[2,16,10240]{2,1,0:T(8,128)S(1)}, u32[]{:S(2)}, u32[]{:S(2)}) collective-permute-start(f32[2,16,10240]{2,1,0:T(8,128)S(1)} %get-tuple-element.21), channel_id=1, source_target_pairs={{0,2},{1,3},{2,0},{3,1},{4,6},{5,7},{6,4},{7,5},{8,10},{9,11},{10,... | collective-permute-start | bytes 3932168 | tf_op jit(solution)/shard_map/ppermute | solution.py:381
  100.8 9.6 %copy-start.5 = (f32[2,16,15360]{2,1,0:T(8,128)}, f32[2,16,15360]{2,1,0:T(8,128)S(1)}, u32[]{:S(2)}) copy-start(f32[2,16,15360]{2,1,0:T(8,128)S(1)} %collective-permute-done.9.refs_5_) | copy-start | bytes 5898244
  110.4 6.8 %collective-permute-start.13 = (f32[128,224]{1,0:T(8,128)S(1)}, f32[128,224]{1,0:T(8,128)S(1)}, u32[]{:S(2)}, u32[]{:S(2)}) collective-permute-start(f32[128,224]{1,0:T(8,128)S(1)} %cross.1.a_ref), channel_id=1, source_target_pairs={{0,24},{8,16},{16,8},{24,0},{1,25},{9,17},{17,9},{25,1},{2,26},{10... | collective-permute-start | bytes 344072 | tf_op jit(solution)/shard_map/ppermute | solution.py:367
  112.9 6.8 %collective-permute-start.12 = (f32[128,224]{1,0:T(8,128)S(1)}, f32[128,224]{1,0:T(8,128)S(1)}, u32[]{:S(2)}, u32[]{:S(2)}) collective-permute-start(f32[128,224]{1,0:T(8,128)S(1)} %cross.1.a_ref), channel_id=1, source_target_pairs={{0,16},{8,24},{16,0},{24,8},{1,17},{9,25},{17,1},{25,9},{2,18},{10... | collective-permute-start | bytes 344072 | tf_op jit(solution)/shard_map/ppermute | solution.py:367
  113.4 6.4 %collective-permute-start.11 = (f32[128,224]{1,0:T(8,128)S(1)}, f32[128,224]{1,0:T(8,128)S(1)}, u32[]{:S(2)}, u32[]{:S(2)}) collective-permute-start(f32[128,224]{1,0:T(8,128)S(1)} %cross.1.a_ref), channel_id=1, source_target_pairs={{0,8},{8,0},{16,24},{24,16},{1,9},{9,1},{17,25},{25,17},{2,10},{10... | collective-permute-start | bytes 344072 | tf_op jit(solution)/shard_map/ppermute | solution.py:367
  119.9 9.6 %collective-permute-start.14 = (f32[128,128]{1,0:T(8,128)S(1)}, f32[128,128]{1,0:T(8,128)S(1)}, u32[]{:S(2)}, u32[]{:S(2)}) collective-permute-start(f32[128,128]{1,0:T(8,128)S(1)} %get-tuple-element.17.gram_ref), channel_id=1, source_target_pairs={{2,0},{3,1},{4,6},{5,7},{10,8},{11,9},{12,14},{13,15},{18,16},{19,... | collective-permute-start | bytes 196616 | tf_op jit(solution)/shard_map/ppermute | solution.py:381
  129.8 1.1 copy-start.6
  129.8 3.1 %collective-permute-start.16 = (f32[2,16,10240]{2,1,0:T(8,128)S(1)}, f32[2,16,10240]{2,1,0:T(8,128)S(1)}, u32[]{:S(2)}, u32[]{:S(2)}) collective-permute-start(f32[2,16,10240]{2,1,0:T(8,128)S(1)} %take.5.refs_6_.refs_4_), channel_id=1, source_target_pairs={{0,1},{1,0},{2,3},{3,2},{4,5},{5,4},{6,7},{7,6},{8,9},{9,8},{10,11... | collective-permute-start | bytes 3932168 | tf_op jit(solution)/shard_map/ppermute | solution.py:381
  130.9 17.4 %collective-permute-start.17 = (f32[2,16,5120]{2,1,0:T(8,128)}, f32[2,16,5120]{2,1,0:T(8,128)}, u32[]{:S(2)}, u32[]{:S(2)}) collective-permute-start(f32[2,16,5120]{2,1,0:T(8,128)} %take.6), channel_id=1, source_target_pairs={{0,2},{1,3},{2,0},{3,1},{4,6},{5,7},{6,4},{7,5},{8,10},{9,11},{10,... | collective-permute-start | bytes 1966088 | tf_op jit(solution)/shard_map/ppermute | solution.py:381
  149.5 2.2 %collective-permute-start.18 = (f32[2,16,5120]{2,1,0:T(8,128)S(1)}, f32[2,16,5120]{2,1,0:T(8,128)S(1)}, u32[]{:S(2)}, u32[]{:S(2)}) collective-permute-start(f32[2,16,5120]{2,1,0:T(8,128)S(1)} %take.7.refs_1_.refs_6_), channel_id=1, source_target_pairs={{0,1},{1,0},{2,3},{3,2},{4,5},{5,4},{6,7},{7,6},{8,9},{9,8},{10,11... | collective-permute-start | bytes 1966088 | tf_op jit(solution)/shard_map/ppermute | solution.py:381
  154.9 5.3 %collective-permute-start.21 = (f32[64,192]{1,0:T(8,128)S(1)}, f32[64,192]{1,0:T(8,128)S(1)}, u32[]{:S(2)}, u32[]{:S(2)}) collective-permute-start(f32[64,192]{1,0:T(8,128)S(1)} %project.3.refs_0_), channel_id=1, source_target_pairs={{0,24},{8,16},{16,8},{24,0},{1,25},{9,17},{17,9},{25,1},{2,26},{10... | collective-permute-start | bytes 147464 | tf_op jit(solution)/shard_map/ppermute | solution.py:367
  157.4 4.3 %collective-permute-start.20 = (f32[64,192]{1,0:T(8,128)S(1)}, f32[64,192]{1,0:T(8,128)S(1)}, u32[]{:S(2)}, u32[]{:S(2)}) collective-permute-start(f32[64,192]{1,0:T(8,128)S(1)} %project.3.refs_0_), channel_id=1, source_target_pairs={{0,16},{8,24},{16,0},{24,8},{1,17},{9,25},{17,1},{25,9},{2,18},{10... | collective-permute-start | bytes 147464 | tf_op jit(solution)/shard_map/ppermute | solution.py:367
  157.9 4.3 %collective-permute-start.19 = (f32[64,192]{1,0:T(8,128)S(1)}, f32[64,192]{1,0:T(8,128)S(1)}, u32[]{:S(2)}, u32[]{:S(2)}) collective-permute-start(f32[64,192]{1,0:T(8,128)S(1)} %project.3.refs_0_), channel_id=1, source_target_pairs={{0,8},{8,0},{16,24},{24,16},{1,9},{9,1},{17,25},{25,17},{2,10},{10... | collective-permute-start | bytes 147464 | tf_op jit(solution)/shard_map/ppermute | solution.py:367

commit v5 on v4

--- a/solution.py
+++ b/solution.py
@@ -14,6 +14,7 @@
 MIB = 1024 * 1024
 TILE = 2560
 FTILE = 5120
+CTILE = 1280
 WIDTHS = (4, 2)
 COST = dict(settle=10**6, hold=10**9, join=10**6, take=10**6, project=10**9, cross=10**9, weigh=10**6, apply=10**9, finish=10**9)
 FINISH = 24
@@ -147,8 +148,15 @@
 
 def take(x, at, width, *after):
     out = jax.ShapeDtypeStruct((*x.shape[:-1], width), F32)
-    return call(
-        take_kernel, width // TILE, [x, *after], [columns(x, at)] + [corner(y) for y in after], out, columns(out), "take"
+    tile = width if at % width == 0 else TILE
+    return call(
+        take_kernel,
+        width // tile,
+        [x, *after],
+        [columns(x, at, tile)] + [corner(y) for y in after],
+        out,
+        columns(out, 0, tile),
+        "take",
     )
 
 
@@ -202,7 +210,7 @@
     gram_ref[...] += wide3((high[half:], low[half:]), (high[:half], low[:half]))
     mine = half // len(pieces)
     pick = lambda x: jnp.concatenate([x[b * half + first * mine :][: count * mine] for b in (0, 1)], axis=0)
-    acc_ref[...] += wide3(split(tile_of(slab_ref)), (pick(high), pick(low)))
+    acc_ref[...] += wide3(split(tile_of(slab_ref, CTILE)), (pick(high), pick(low)))
 
     @pl.when(step == steps - 1)
     def _():
@@ -218,15 +226,15 @@
     n, rows = mine * len(pieces), 2 * mine * count
     out = MADE((n, n + nev // 2), F32)
     return call(
-        functools.partial(cross_kernel, width // TILE, first, count),
-        width // TILE,
+        functools.partial(cross_kernel, width // CTILE, first, count),
+        width // CTILE,
         [held(slab), *pieces],
-        [HELD] + [columns(p) for p in pieces],
+        [HELD] + [columns(p, 0, CTILE) for p in pieces],
         out,
         whole(out),
         "cross",
         [pltpu.VMEM((n, n), F32), pltpu.VMEM((nev, rows), F32)],
-        vmem=24,
+        vmem=16,
     )
 
 

time: 169 us -> 169 us (level)
  waiting for transfers between devices: 98.5 us -> 95.5 us
  local copies, waits for them, and re-layouts: 0.03 us -> 1.77 us
    ppermute x13, waiting for transfers between devices: 82.7 us -> 79.6 us  [along(): return lax.ppermute(x, 'col', pairs)]
    unnamed x14 -> x18, local copies, waits for them, and re-layouts: 0.03 us -> 1.77 us
  transfers between devices with their start and end apart: 22 -> 22, of which waited for: 17 -> 15; matrix products, arithmetic and copies ran while one was open for 0% -> 0% of each run, Pallas kernels for 24% -> 25%
where the time goes in v5:
time: 169 us; the launch traced here: 168 us
  waiting for transfers between devices  95.5 us (57%)
  Pallas kernels  52.1 us (31%)
  starting transfers between devices  18.7 us (11%)
  local copies, waits for them, and re-layouts  1.77 us (1%)
    ppermute x13, waiting for transfers between devices, along(): return lax.ppermute(x, 'col', pairs)  79.6 us
    pallas_call x14, Pallas kernels, call(): pl.pallas_call(kernel, out_shape=outs, grid=(steps,), in_specs=specs, out...  52.1 us
    ppermute x9, waiting for transfers between devices, others(): lax.ppermute(x, 'row', [(i, i ^ k) for i in range(4)])  15.9 us
    ppermute x9, starting transfers between devices, others(): lax.ppermute(x, 'row', [(i, i ^ k) for i in range(4)])  10.7 us
    ppermute x13, starting transfers between devices, along(): return lax.ppermute(x, 'col', pairs)  8.01 us
  transfers between devices with their start and end apart: 22, of which 15 were waited for; matrix products, arithmetic and copies ran while one was open for 0% of the time, Pallas kernels for 25%

profile of v5, /device:TPU:0, one launch (start us, length us, event | category | flops | bytes accessed | tf_op | source)
XLA Modules:
  0.0 168.3 jit_solution(749368065428194022)
XLA Ops:
  0.0 3.0 %collective-permute-start.1 = (f32[2,16,15360]{2,1,0:T(8,128)}, f32[2,16,15360]{2,1,0:T(8,128)S(1)}, u32[]{:S(2)}, u32[]{:S(2)}) collective-permute-start(f32[2,16,15360]{2,1,0:T(8,128)} %refs_0_.5), channel_id=1, source_target_pairs={{0,2},{1,3},{2,0},{3,1},{4,6},{5,7},{6,4},{7,5},{8,10},{9,11},{10,... | collective-permute-start | bytes 5898248 | tf_op jit(solution)/shard_map/ppermute | solution.py:389
  3.0 0.8 collective-permute-start.7
  3.8 0.1 collective-permute-start
  3.9 42.2 %collective-permute-done.1.refs_2_ = f32[2,16,15360]{2,1,0:T(8,128)S(1)} collective-permute-done((f32[2,16,15360]{2,1,0:T(8,128)}, f32[2,16,15360]{2,1,0:T(8,128)S(1)}, u32[]{:S(2)}, u32[]{:S(2)}) %collective-permute-start.1) | collective-permute-done | bytes 1966112 | tf_op jit(solution)/shard_map/ppermute | solution.py:389
  46.1 0.0 collective-permute-start.2
  46.1 0.8 collective-permute-start.3
  46.9 0.0 collective-permute-done.7.refs_6_
  46.9 1.3 collective-permute-start.8
  48.2 6.3 %hold.1.slab_ref = f32[192,15360]{1,0:T(8,128)S(1)} custom-call(f32[192,15360]{1,0:T(8,128)} %slab_ref.3), custom_call_target="tpu_custom_call" | custom-call | flops 1000000000 | bytes 1 | tf_op jit(solution)/shard_map/hold/pallas_call | solution.py:71
  54.5 0.0 collective-permute-done.refs_1_
  54.5 0.0 copy-start.2
  54.6 0.0 collective-permute-done.2.refs_3_
  54.6 0.0 copy-done
  54.6 0.0 copy-start.3
  54.6 5.7 %project.2.refs_0_ = f32[128,192]{1,0:T(8,128)S(1)} custom-call(f32[192,15360]{1,0:T(8,128)S(1)} %hold.1.slab_ref, f32[2,16,15360]{2,1,0:T(8,128)S(1)} %copy-done, f32[2,16,15360]{2,1,0:T(8,128)S(1)} %collective-permute-done.refs_1_, f32[2,16,15360]{2,1,0:T(8,128)S(1)} %collective-permute-done.1.refs_2_, f32[2,16,15360]{2,1,0:T(8,128)S(1)} %collective-permute-done.2.refs_3_), custom_call_target="tpu_custom_call" | custom-call | flops 1000000000 | bytes 1 | tf_op jit(solution)/shard_map/project/pallas_call | solution.py:71
  60.3 2.6 %collective-permute-start.6 = (f32[128,192]{1,0:T(8,128)S(1)}, f32[128,192]{1,0:T(8,128)S(1)}, u32[]{:S(2)}, u32[]{:S(2)}) collective-permute-start(f32[128,192]{1,0:T(8,128)S(1)} %project.2.refs_0_), channel_id=1, source_target_pairs={{0,24},{8,16},{16,8},{24,0},{1,25},{9,17},{17,9},{25,1},{2,26},{10... | collective-permute-start | bytes 294920 | tf_op jit(solution)/shard_map/ppermute | solution.py:375
  62.9 0.5 collective-permute-start.5
  63.4 0.4 collective-permute-start.4
  63.9 3.5 %collective-permute-done.6.refs_3_ = f32[128,192]{1,0:T(8,128)S(1)} collective-permute-done((f32[128,192]{1,0:T(8,128)S(1)}, f32[128,192]{1,0:T(8,128)S(1)}, u32[]{:S(2)}, u32[]{:S(2)}) %collective-permute-start.6) | collective-permute-done | bytes 98336 | tf_op jit(solution)/shard_map/ppermute | solution.py:375
  67.4 0.0 collective-permute-start.10
  67.4 2.6 %collective-permute-done.5.refs_2_ = f32[128,192]{1,0:T(8,128)S(1)} collective-permute-done((f32[128,192]{1,0:T(8,128)S(1)}, f32[128,192]{1,0:T(8,128)S(1)}, u32[]{:S(2)}, u32[]{:S(2)}) %collective-permute-start.5) | collective-permute-done | bytes 98336 | tf_op jit(solution)/shard_map/ppermute | solution.py:375
  70.0 0.2 collective-permute-done.4.refs_1_
  70.2 0.0 collective-permute-done.3.x_ref
  70.2 0.1 take.4.a_ref
  70.4 25.4 %collective-permute-done.8.b_ref = f32[2,16,15360]{2,1,0:T(8,128)S(1)} collective-permute-done((f32[2,16,15360]{2,1,0:T(8,128)S(1)}, f32[2,16,15360]{2,1,0:T(8,128)S(1)}, u32[]{:S(2)}, u32[]{:S(2)}) %collective-permute-start.8) | collective-permute-done | bytes 1966112 | tf_op jit(solution)/shard_map/ppermute | solution.py:389
  95.8 1.0 join.1
  96.8 0.0 copy-start.4
  96.8 0.1 collective-permute-start.9
  96.8 0.1 collective-permute-start.15
  96.9 0.0 collective-permute-done.10.refs_7_
  96.9 3.9 %collective-permute-done.9.refs_5_ = f32[2,16,15360]{2,1,0:T(8,128)S(1)} collective-permute-done((f32[2,16,15360]{2,1,0:T(8,128)S(1)}, f32[2,16,15360]{2,1,0:T(8,128)S(1)}, u32[]{:S(2)}, u32[]{:S(2)}) %collective-permute-start.9) | collective-permute-done | bytes 1966112 | tf_op jit(solution)/shard_map/ppermute | solution.py:389
  100.8 0.0 copy-done.1
  100.8 11.5 %cross.1.a_ref = f32[128,224]{1,0:T(8,128)S(1)} custom-call(f32[192,15360]{1,0:T(8,128)S(1)} %hold.1.slab_ref, f32[2,16,15360]{2,1,0:T(8,128)S(1)} %copy-done, f32[2,16,15360]{2,1,0:T(8,128)S(1)} %collective-permute-done.refs_1_, f32[2,16,15360]{2,1,0:T(8,128)S(1)} %collective-permute-done.1.refs_2_, f32[2,16,15360]{2,1,0:T(8,128)S(1)} %collective-permute-done.2.refs_3_, ...), custom_call_target="tpu_custom_call" | custom-call | flops 1000000000 | bytes 1 | tf_op jit(solution)/shard_map/cross/pallas_call | solution.py:71
  112.3 2.5 %collective-permute-start.13 = (f32[128,224]{1,0:T(8,128)S(1)}, f32[128,224]{1,0:T(8,128)S(1)}, u32[]{:S(2)}, u32[]{:S(2)}) collective-permute-start(f32[128,224]{1,0:T(8,128)S(1)} %cross.1.a_ref), channel_id=1, source_target_pairs={{0,24},{8,16},{16,8},{24,0},{1,25},{9,17},{17,9},{25,1},{2,26},{10... | collective-permute-start | bytes 344072 | tf_op jit(solution)/shard_map/ppermute | solution.py:375
  114.8 0.5 collective-permute-start.12
  115.3 0.5 collective-permute-start.11
  115.8 3.2 %collective-permute-done.13.d_ref = f32[128,224]{1,0:T(8,128)S(1)} collective-permute-done((f32[128,224]{1,0:T(8,128)S(1)}, f32[128,224]{1,0:T(8,128)S(1)}, u32[]{:S(2)}, u32[]{:S(2)}) %collective-permute-start.13) | collective-permute-done | bytes 114720 | tf_op jit(solution)/shard_map/ppermute | solution.py:375
  119.1 2.5 %collective-permute-done.12.c_ref = f32[128,224]{1,0:T(8,128)S(1)} collective-permute-done((f32[128,224]{1,0:T(8,128)S(1)}, f32[128,224]{1,0:T(8,128)S(1)}, u32[]{:S(2)}, u32[]{:S(2)}) %collective-permute-start.12) | collective-permute-done | bytes 114720 | tf_op jit(solution)/shard_map/ppermute | solution.py:375
  121.6 0.1 collective-permute-done.11.b_ref
  121.7 0.1 settle.3
  121.8 1.3 collective-permute-start.14
  123.1 5.4 %collective-permute-done.15.x_ref = f32[2,16,10240]{2,1,0:T(8,128)S(1)} collective-permute-done((f32[2,16,10240]{2,1,0:T(8,128)S(1)}, f32[2,16,10240]{2,1,0:T(8,128)S(1)}, u32[]{:S(2)}, u32[]{:S(2)}) %collective-permute-start.15) | collective-permute-done | bytes 1310752 | tf_op jit(solution)/shard_map/ppermute | solution.py:389
  128.5 1.0 collective-permute-done.14.given_ref.refs_0_
  129.4 0.1 take.5.refs_6_.refs_4_
  129.5 0.1 collective-permute-start.16
  129.6 0.0 copy-done.4
  129.6 0.9 take.6
  130.6 0.0 collective-permute-start.17
  130.6 0.9 copy-done.6
  131.5 0.8 copy-done.8
  132.3 1.5 weigh.1
  133.8 0.0 collective-permute-done.16.refs_7_.refs_5_
  133.8 14.8 %apply.1 = (f32[192,15360]{1,0:T(8,128)S(1)}, bf16[64,15360]{1,0:T(8,128)(2,1)S(1)}, bf16[64,15360]{1,0:T(8,128)(2,1)S(1)}, f32[64,192]{1,0:T(8,128)S(1)}) custom-call(bf16[256,192]{1,0:T(8,128)(2,1)S(1)} %get-tuple-element.19.high_ref, bf16[256,192]{1,0:T(8,128)(2,1)S(1)} %get-tuple-element.20.low_ref, f32[192,15360]{1,0:T(8,128)} %slab_ref.3, ...), custom_call_target="tpu_custom_call" | custom-call | flops 1000000000 | bytes 1 | tf_op jit(solution)/shard_map/apply/pallas_call | solution.py:71
  148.6 0.0 collective-permute-done.17.x_ref
  148.7 0.6 collective-permute-start.18
  149.2 1.7 %collective-permute-done.18.refs_2_.refs_7_ = f32[2,16,5120]{2,1,0:T(8,128)S(1)} collective-permute-done((f32[2,16,5120]{2,1,0:T(8,128)S(1)}, f32[2,16,5120]{2,1,0:T(8,128)S(1)}, u32[]{:S(2)}, u32[]{:S(2)}) %collective-permute-start.18) | collective-permute-done | bytes 655392 | tf_op jit(solution)/shard_map/ppermute | solution.py:389
  150.9 3.3 %project.3.refs_0_ = f32[64,192]{1,0:T(8,128)S(1)} custom-call(f32[192,15360]{1,0:T(8,128)} %slab_ref.3, f32[64,192]{1,0:T(8,128)S(1)} %get-tuple-element.26.refs_0_, f32[2,16,5120]{2,1,0:T(8,128)S(1)} %take.7.refs_1_.refs_6_, f32[2,16,5120]{2,1,0:T(8,128)S(1)} %collective-permute-done.18.refs_2_.refs_7_), custom_call_target="tpu_custom_call" | custom-call | flops 1000000000 | bytes 1 | tf_op jit(solution)/shard_map/project/pallas_call | solution.py:71
  154.2 2.5 %collective-permute-start.21 = (f32[64,192]{1,0:T(8,128)S(1)}, f32[64,192]{1,0:T(8,128)S(1)}, u32[]{:S(2)}, u32[]{:S(2)}) collective-permute-start(f32[64,192]{1,0:T(8,128)S(1)} %project.3.refs_0_), channel_id=1, source_target_pairs={{0,24},{8,16},{16,8},{24,0},{1,25},{9,17},{17,9},{25,1},{2,26},{10... | collective-permute-start | bytes 147464 | tf_op jit(solution)/shard_map/ppermute | solution.py:375
  156.7 0.5 collective-permute-start.20
  157.2 0.5 collective-permute-start.19
  157.8 1.8 %collective-permute-done.21.refs_3_ = f32[64,192]{1,0:T(8,128)S(1)} collective-permute-done((f32[64,192]{1,0:T(8,128)S(1)}, f32[64,192]{1,0:T(8,128)S(1)}, u32[]{:S(2)}, u32[]{:S(2)}) %collective-permute-start.21) | collective-permute-done | bytes 49184 | tf_op jit(solution)/shard_map/ppermute | solution.py:375
  159.6 1.4 collective-permute-done.20.refs_2_
  161.0 0.5 collective-permute-done.19.refs_1_
  161.5 6.8 %finish.1 = f32[192,15360]{1,0:T(8,128)} custom-call(f32[192,15360]{1,0:T(8,128)S(1)} %get-tuple-element.22.part_ref, bf16[64,15360]{1,0:T(8,128)(2,1)S(1)} %get-tuple-element.23.xh_ref, bf16[64,15360]{1,0:T(8,128)(2,1)S(1)} %get-tuple-element.24.xl_ref, f32[64,256]{1,0:T(8,128)S(1)} %get-tuple-element.25.rest_ref, f32[64,192]{1,0:T(8,128)S(1)} %project.3.refs_0_, ...), custom_call_target="tpu_custom_call" | custom-call | flops 1000000000 | bytes 1 | tf_op jit(solution)/shard_map/finish/pallas_call | solution.py:71
  (12 shorter events, 0.1 us)
Async XLA Ops:
  0.0 54.6 %copy-start = (f32[2,16,15360]{2,1,0:T(8,128)S(1)}, f32[2,16,15360]{2,1,0:T(8,128)}, u32[]{:S(2)}) copy-start(f32[2,16,15360]{2,1,0:T(8,128)} %refs_0_.5) | copy-start | bytes 5898244
  0.0 46.1 %collective-permute-start.1 = (f32[2,16,15360]{2,1,0:T(8,128)}, f32[2,16,15360]{2,1,0:T(8,128)S(1)}, u32[]{:S(2)}, u32[]{:S(2)}) collective-permute-start(f32[2,16,15360]{2,1,0:T(8,128)} %refs_0_.5), channel_id=1, source_target_pairs={{0,2},{1,3},{2,0},{3,1},{4,6},{5,7},{6,4},{7,5},{8,10},{9,11},{10,... | collective-permute-start | bytes 5898248 | tf_op jit(solution)/shard_map/ppermute | solution.py:389
  3.0 43.9 %collective-permute-start.7 = (f32[2,16,15360]{2,1,0:T(8,128)}, f32[2,16,15360]{2,1,0:T(8,128)S(1)}, u32[]{:S(2)}, u32[]{:S(2)}) collective-permute-start(f32[2,16,15360]{2,1,0:T(8,128)} %refs_0_.5), channel_id=1, source_target_pairs={{2,4},{3,5},{4,2},{5,3},{10,12},{11,13},{12,10},{13,11},{18,20},{1... | collective-permute-start | bytes 5898248 | tf_op jit(solution)/shard_map/ppermute | solution.py:389
  3.8 50.7 %collective-permute-start = (f32[2,16,15360]{2,1,0:T(8,128)}, f32[2,16,15360]{2,1,0:T(8,128)S(1)}, u32[]{:S(2)}, u32[]{:S(2)}) collective-permute-start(f32[2,16,15360]{2,1,0:T(8,128)} %refs_0_.5), channel_id=1, source_target_pairs={{0,1},{1,0},{2,3},{3,2},{4,5},{5,4},{6,7},{7,6},{8,9},{9,8},{10,11... | collective-permute-start | bytes 5898248 | tf_op jit(solution)/shard_map/ppermute | solution.py:389
  46.1 54.7 %copy-start.1 = (f32[2,16,15360]{2,1,0:T(8,128)}, f32[2,16,15360]{2,1,0:T(8,128)S(1)}, u32[]{:S(2)}) copy-start(f32[2,16,15360]{2,1,0:T(8,128)S(1)} %collective-permute-done.1.refs_2_) | copy-start | bytes 5898244
  46.1 8.4 %collective-permute-start.2 = (f32[2,16,15360]{2,1,0:T(8,128)S(1)}, f32[2,16,15360]{2,1,0:T(8,128)S(1)}, u32[]{:S(2)}, u32[]{:S(2)}) collective-permute-start(f32[2,16,15360]{2,1,0:T(8,128)S(1)} %collective-permute-done.1.refs_2_), channel_id=1, source_target_pairs={{0,1},{1,0},{2,3},{3,2},{4,5},{5,4},{6,7},{7,6},{8,9},{9,8},{10,11... | collective-permute-start | bytes 5898248 | tf_op jit(solution)/shard_map/ppermute | solution.py:389
  46.1 24.1 %collective-permute-start.3 = (f32[2,16,15360]{2,1,0:T(8,128)S(1)}, f32[2,16,15360]{2,1,0:T(8,128)S(1)}, u32[]{:S(2)}, u32[]{:S(2)}) collective-permute-start(f32[2,16,15360]{2,1,0:T(8,128)S(1)} %collective-permute-done.1.refs_2_), channel_id=1, source_target_pairs={{2,4},{3,5},{4,2},{5,3},{10,12},{11,13},{12,10},{13,11},{18,20},{1... | collective-permute-start | bytes 5898248 | tf_op jit(solution)/shard_map/ppermute | solution.py:389
  46.9 48.9 %collective-permute-start.8 = (f32[2,16,15360]{2,1,0:T(8,128)S(1)}, f32[2,16,15360]{2,1,0:T(8,128)S(1)}, u32[]{:S(2)}, u32[]{:S(2)}) collective-permute-start(f32[2,16,15360]{2,1,0:T(8,128)S(1)} %collective-permute-done.7.refs_6_), channel_id=1, source_target_pairs={{2,0},{3,1},{4,6},{5,7},{10,8},{11,9},{12,14},{13,15},{18,16},{19,... | collective-permute-start | bytes 5898248 | tf_op jit(solution)/shard_map/ppermute | solution.py:389
  54.5 46.3 %copy-start.2 = (f32[2,16,15360]{2,1,0:T(8,128)}, f32[2,16,15360]{2,1,0:T(8,128)S(1)}, u32[]{:S(2)}) copy-start(f32[2,16,15360]{2,1,0:T(8,128)S(1)} %collective-permute-done.refs_1_) | copy-start | bytes 5898244
  54.6 46.2 %copy-start.3 = (f32[2,16,15360]{2,1,0:T(8,128)}, f32[2,16,15360]{2,1,0:T(8,128)S(1)}, u32[]{:S(2)}) copy-start(f32[2,16,15360]{2,1,0:T(8,128)S(1)} %collective-permute-done.2.refs_3_) | copy-start | bytes 5898244
  60.3 7.0 %collective-permute-start.6 = (f32[128,192]{1,0:T(8,128)S(1)}, f32[128,192]{1,0:T(8,128)S(1)}, u32[]{:S(2)}, u32[]{:S(2)}) collective-permute-start(f32[128,192]{1,0:T(8,128)S(1)} %project.2.refs_0_), channel_id=1, source_target_pairs={{0,24},{8,16},{16,8},{24,0},{1,25},{9,17},{17,9},{25,1},{2,26},{10... | collective-permute-start | bytes 294920 | tf_op jit(solution)/shard_map/ppermute | solution.py:375
  62.9 7.1 %collective-permute-start.5 = (f32[128,192]{1,0:T(8,128)S(1)}, f32[128,192]{1,0:T(8,128)S(1)}, u32[]{:S(2)}, u32[]{:S(2)}) collective-permute-start(f32[128,192]{1,0:T(8,128)S(1)} %project.2.refs_0_), channel_id=1, source_target_pairs={{0,16},{8,24},{16,0},{24,8},{1,17},{9,25},{17,1},{25,9},{2,18},{10... | collective-permute-start | bytes 294920 | tf_op jit(solution)/shard_map/ppermute | solution.py:375
  63.4 6.8 %collective-permute-start.4 = (f32[128,192]{1,0:T(8,128)S(1)}, f32[128,192]{1,0:T(8,128)S(1)}, u32[]{:S(2)}, u32[]{:S(2)}) collective-permute-start(f32[128,192]{1,0:T(8,128)S(1)} %project.2.refs_0_), channel_id=1, source_target_pairs={{0,8},{8,0},{16,24},{24,16},{1,9},{9,1},{17,25},{25,17},{2,10},{10... | collective-permute-start | bytes 294920 | tf_op jit(solution)/shard_map/ppermute | solution.py:375
  67.4 29.6 %collective-permute-start.10 = (f32[2,16,15360]{2,1,0:T(8,128)S(1)}, f32[2,16,15360]{2,1,0:T(8,128)S(1)}, u32[]{:S(2)}, u32[]{:S(2)}) collective-permute-start(f32[2,16,15360]{2,1,0:T(8,128)S(1)} %collective-permute-done.7.refs_6_), channel_id=1, source_target_pairs={{0,1},{1,0},{2,3},{3,2},{4,5},{5,4},{6,7},{7,6},{8,9},{9,8},{10,11... | collective-permute-start | bytes 5898248 | tf_op jit(solution)/shard_map/ppermute | solution.py:389
  96.8 32.9 %copy-start.4 = (f32[2,16,15360]{2,1,0:T(8,128)}, f32[2,16,15360]{2,1,0:T(8,128)S(1)}, u32[]{:S(2)}) copy-start(f32[2,16,15360]{2,1,0:T(8,128)S(1)} %get-tuple-element.16.refs_4_.x_ref) | copy-start | bytes 5898244
  96.8 4.0 %collective-permute-start.9 = (f32[2,16,15360]{2,1,0:T(8,128)S(1)}, f32[2,16,15360]{2,1,0:T(8,128)S(1)}, u32[]{:S(2)}, u32[]{:S(2)}) collective-permute-start(f32[2,16,15360]{2,1,0:T(8,128)S(1)} %get-tuple-element.16.refs_4_.x_ref), channel_id=1, source_target_pairs={{0,1},{1,0},{2,3},{3,2},{4,5},{5,4},{6,7},{7,6},{8,9},{9,8},{10,11... | collective-permute-start | bytes 5898248 | tf_op jit(solution)/shard_map/ppermute | solution.py:389
  96.8 31.6 %collective-permute-start.15 = (f32[2,16,10240]{2,1,0:T(8,128)S(1)}, f32[2,16,10240]{2,1,0:T(8,128)S(1)}, u32[]{:S(2)}, u32[]{:S(2)}) collective-permute-start(f32[2,16,10240]{2,1,0:T(8,128)S(1)} %get-tuple-element.21), channel_id=1, source_target_pairs={{0,2},{1,3},{2,0},{3,1},{4,6},{5,7},{6,4},{7,5},{8,10},{9,11},{10,... | collective-permute-start | bytes 3932168 | tf_op jit(solution)/shard_map/ppermute | solution.py:389
  100.8 11.5 %copy-start.5 = (f32[2,16,15360]{2,1,0:T(8,128)}, f32[2,16,15360]{2,1,0:T(8,128)S(1)}, u32[]{:S(2)}) copy-start(f32[2,16,15360]{2,1,0:T(8,128)S(1)} %collective-permute-done.9.refs_5_) | copy-start | bytes 5898244
  112.3 6.8 %collective-permute-start.13 = (f32[128,224]{1,0:T(8,128)S(1)}, f32[128,224]{1,0:T(8,128)S(1)}, u32[]{:S(2)}, u32[]{:S(2)}) collective-permute-start(f32[128,224]{1,0:T(8,128)S(1)} %cross.1.a_ref), channel_id=1, source_target_pairs={{0,24},{8,16},{16,8},{24,0},{1,25},{9,17},{17,9},{25,1},{2,26},{10... | collective-permute-start | bytes 344072 | tf_op jit(solution)/shard_map/ppermute | solution.py:375
  114.8 6.8 %collective-permute-start.12 = (f32[128,224]{1,0:T(8,128)S(1)}, f32[128,224]{1,0:T(8,128)S(1)}, u32[]{:S(2)}, u32[]{:S(2)}) collective-permute-start(f32[128,224]{1,0:T(8,128)S(1)} %cross.1.a_ref), channel_id=1, source_target_pairs={{0,16},{8,24},{16,0},{24,8},{1,17},{9,25},{17,1},{25,9},{2,18},{10... | collective-permute-start | bytes 344072 | tf_op jit(solution)/shard_map/ppermute | solution.py:375
  115.3 6.4 %collective-permute-start.11 = (f32[128,224]{1,0:T(8,128)S(1)}, f32[128,224]{1,0:T(8,128)S(1)}, u32[]{:S(2)}, u32[]{:S(2)}) collective-permute-start(f32[128,224]{1,0:T(8,128)S(1)} %cross.1.a_ref), channel_id=1, source_target_pairs={{0,8},{8,0},{16,24},{24,16},{1,9},{9,1},{17,25},{25,17},{2,10},{10... | collective-permute-start | bytes 344072 | tf_op jit(solution)/shard_map/ppermute | solution.py:375
  121.8 8.8 %copy-start.7 = (f32[64,192]{1,0:T(8,128)}, f32[64,192]{1,0:T(8,128)S(1)}, u32[]{:S(2)}) copy-start(f32[64,192]{1,0:T(8,128)S(1)} %get-tuple-element.18.refs_1_) | copy-start | bytes 147460
  121.8 7.7 %collective-permute-start.14 = (f32[128,128]{1,0:T(8,128)S(1)}, f32[128,128]{1,0:T(8,128)S(1)}, u32[]{:S(2)}, u32[]{:S(2)}) collective-permute-start(f32[128,128]{1,0:T(8,128)S(1)} %get-tuple-element.17.gram_ref), channel_id=1, source_target_pairs={{2,0},{3,1},{4,6},{5,7},{10,8},{11,9},{12,14},{13,15},{18,16},{19,... | collective-permute-start | bytes 196616 | tf_op jit(solution)/shard_map/ppermute | solution.py:389
  129.5 4.3 %collective-permute-start.16 = (f32[2,16,10240]{2,1,0:T(8,128)S(1)}, f32[2,16,10240]{2,1,0:T(8,128)S(1)}, u32[]{:S(2)}, u32[]{:S(2)}) collective-permute-start(f32[2,16,10240]{2,1,0:T(8,128)S(1)} %take.5.refs_6_.refs_4_), channel_id=1, source_target_pairs={{0,1},{1,0},{2,3},{3,2},{4,5},{5,4},{6,7},{7,6},{8,9},{9,8},{10,11... | collective-permute-start | bytes 3932168 | tf_op jit(solution)/shard_map/ppermute | solution.py:389
  130.6 18.0 %collective-permute-start.17 = (f32[2,16,5120]{2,1,0:T(8,128)}, f32[2,16,5120]{2,1,0:T(8,128)S(1)}, u32[]{:S(2)}, u32[]{:S(2)}) collective-permute-start(f32[2,16,5120]{2,1,0:T(8,128)} %take.6), channel_id=1, source_target_pairs={{0,2},{1,3},{2,0},{3,1},{4,6},{5,7},{6,4},{7,5},{8,10},{9,11},{10,... | collective-permute-start | bytes 1966088 | tf_op jit(solution)/shard_map/ppermute | solution.py:389
  130.6 0.9 copy-start.6
  131.5 0.8 copy-start.8
  148.7 2.3 %collective-permute-start.18 = (f32[2,16,5120]{2,1,0:T(8,128)S(1)}, f32[2,16,5120]{2,1,0:T(8,128)S(1)}, u32[]{:S(2)}, u32[]{:S(2)}) collective-permute-start(f32[2,16,5120]{2,1,0:T(8,128)S(1)} %take.7.refs_1_.refs_6_), channel_id=1, source_target_pairs={{0,1},{1,0},{2,3},{3,2},{4,5},{5,4},{6,7},{7,6},{8,9},{9,8},{10,11... | collective-permute-start | bytes 1966088 | tf_op jit(solution)/shard_map/ppermute | solution.py:389
  154.2 5.3 %collective-permute-start.21 = (f32[64,192]{1,0:T(8,128)S(1)}, f32[64,192]{1,0:T(8,128)S(1)}, u32[]{:S(2)}, u32[]{:S(2)}) collective-permute-start(f32[64,192]{1,0:T(8,128)S(1)} %project.3.refs_0_), channel_id=1, source_target_pairs={{0,24},{8,16},{16,8},{24,0},{1,25},{9,17},{17,9},{25,1},{2,26},{10... | collective-permute-start | bytes 147464 | tf_op jit(solution)/shard_map/ppermute | solution.py:375
  156.7 4.3 %collective-permute-start.20 = (f32[64,192]{1,0:T(8,128)S(1)}, f32[64,192]{1,0:T(8,128)S(1)}, u32[]{:S(2)}, u32[]{:S(2)}) collective-permute-start(f32[64,192]{1,0:T(8,128)S(1)} %project.3.refs_0_), channel_id=1, source_target_pairs={{0,16},{8,24},{16,0},{24,8},{1,17},{9,25},{17,1},{25,9},{2,18},{10... | collective-permute-start | bytes 147464 | tf_op jit(solution)/shard_map/ppermute | solution.py:375
  157.2 4.3 %collective-permute-start.19 = (f32[64,192]{1,0:T(8,128)S(1)}, f32[64,192]{1,0:T(8,128)S(1)}, u32[]{:S(2)}, u32[]{:S(2)}) collective-permute-start(f32[64,192]{1,0:T(8,128)S(1)} %project.3.refs_0_), channel_id=1, source_target_pairs={{0,8},{8,0},{16,24},{24,16},{1,9},{9,1},{17,25},{25,17},{2,10},{10... | collective-permute-start | bytes 147464 | tf_op jit(solution)/shard_map/ppermute | solution.py:375
